TPU v7x, 32 devices: a whole 2x2x4 slice. The times are simulated.
32 devices in a mesh: grp: 2 (over y), space: 4 (over z), tm: 2 (over x), sub: 2 (over core).
Axes of the slice: x: 2, y: 2, z: 4, core: 2. Of those that a mesh axis runs over, the one named last changes fastest.
Arguments:
- sink_modes: bfloat16 [8, 128, 2, 12, 1024], P(('grp', 'tm'), None, None, None, ('space', 'sub')), parts along dimension 0, may hold values from -6 to 6
- source_modes: bfloat16 [8, 128, 2, 12, 1024], P(('grp', 'tm'), None, None, None, ('space', 'sub')), parts along dimension 0, may hold values from -6 to 6
- gamma_index: int32 [8], replicated, may hold values from 0 to 15
- momenta: int32 [8, 3], replicated, may hold values from -2 to 2
- pattern: int32 [4, 1024], P('tm', ('space', 'sub')), may hold values from 0 to 3
- time_pairs: int32 [4, 2], P('tm'), may hold values from 0 to 3
Outputs:
- meson: float32 [8, 8, 2, 128, 128], P(('grp', 'tm'), None, None, ('space', 'sub')), parts along dimension 0
- products: float32 [8, 8, 2, 128, 128], P(('grp', 'tm'), None, None, ('space', 'sub')), parts along dimension 0
There are 2 independent parts, one for each index of `grp`. A program takes and returns all parts, laid end to end along the dimension named above; an argument that names none is the same for every part. Nothing has to cross between parts.
All inputs are finite; a program needn't handle non-finite values.
Results may differ from a plain program's by a relative error of at most 0.0039.
Values sent between devices are 32-bit elements; how exact they have to be, the bound alone decides.
No kernel may reach another device: no remote copies, remote signals or barrier semaphores. Data moves between devices by JAX's collectives and lax.ppermute only.
A program may use at most 128 MiB of HBM per device.

v0:
```python
import functools
import math

import jax
import jax.numpy as jnp
import numpy as np
from jax import lax
from jax.experimental import pallas as pl
from jax.experimental.pallas import tpu as pltpu
from jax.sharding import PartitionSpec as P

LAT = 96
F32 = jnp.float32
BF16 = jnp.bfloat16
VMEM_LIMIT = 48 * 2**20


def build_gammas():
    sigmas = [
        np.array([[0, 1], [1, 0]], dtype=complex),
        np.array([[0, -1j], [1j, 0]], dtype=complex),
        np.array([[1, 0], [0, -1]], dtype=complex),
    ]
    zero, one = np.zeros((2, 2), dtype=complex), np.eye(2, dtype=complex)
    gammas = [np.block([[zero, 1j * s], [-1j * s, zero]]) for s in sigmas]
    gammas.append(np.block([[zero, one], [one, zero]]))
    tables = []
    for subset in range(16):
        product = np.eye(4, dtype=complex)
        for factor in range(4):
            if subset >> factor & 1:
                product = product @ gammas[factor]
        tables.append(product)
    return tables


def gamma_codes():
    words = [0, 0, 0, 0]
    for index, table in enumerate(build_gammas()):
        flip = gamma_flip(index)
        for row in range(4):
            entry = table[row, row ^ flip]
            power = [k for k in range(4) if abs(entry - 1j**k) < 1e-6]
            assert len(power) == 1 and np.count_nonzero(table[row]) == 1
            words[index // 4] |= power[0] << (8 * (index % 4) + 2 * row)
    return [word - 2**32 if word >= 2**31 else word for word in words]


def gamma_flip(index):
    b1, b2, b3, b4 = (index & 1, (index >> 1) & 1, (index >> 2) & 1, (index >> 3) & 1)
    return (b1 ^ b2) | ((b1 ^ b2 ^ b3 ^ b4) << 1)


def column(values):
    row = lax.broadcasted_iota(jnp.int32, (len(values), 1), 0)
    out = jnp.zeros((len(values), 1), jnp.int32)
    for index, value in enumerate(values):
        out = jnp.where(row == index, value, out)
    return out


def site_coords(site):
    coords = []
    for axis in range(3):
        total = jnp.zeros_like(site)
        for level in range(6):
            total = total + (((site >> (3 * level + axis)) & 1) << level)
        coords.append(total)
    return coords


def meson_kernel(
    order, batch, sink_ref, source_ref, gamma_ref, momenta_ref, pattern_ref, *refs, time
):
    outs, (sink_mat, source_rows, stage, phases, rotated) = refs[:-5], refs[-5:]
    rows, sites = sink_ref.shape
    nmode = outs[0].shape[1]
    per_mode = rows // nmode
    comps = per_mode // 2
    colours = comps // 4
    insertions = order()
    slots = len(insertions)

    first_site = (
        lax.axis_index("space") * lax.axis_size("sub") + lax.axis_index("sub")
    ) * sites
    site = lax.broadcasted_iota(jnp.int32, (slots, sites), 1) + first_site
    coords = site_coords(site)
    wave = jnp.zeros_like(site)
    for axis in range(3):
        wave = wave + coords[axis] * column([momenta_ref[axis, g] for g in insertions])
    laps = jnp.floor((wave.astype(F32) + 0.5) * (1.0 / LAT)).astype(jnp.int32)
    wave = wave - LAT * laps
    angle = wave.astype(F32) * (2.0 * math.pi / LAT)
    keep = jnp.where(
        pattern_ref[time : time + 1, :] == column([lax.rem(g, 4) for g in insertions]), 1.0, 0.0
    )
    phases[0] = jnp.cos(angle) * keep
    phases[1] = jnp.sin(angle) * keep

    stage[...] = sink_ref[...].astype(F32)
    for comp in range(comps):
        at = comp * 2 * sites
        real = stage[pl.ds(2 * comp, nmode, stride=per_mode), :].astype(BF16)
        imag = stage[pl.ds(2 * comp + 1, nmode, stride=per_mode), :].astype(BF16)
        sink_mat[0:nmode, at : at + sites] = real
        sink_mat[0:nmode, at + sites : at + 2 * sites] = imag
        sink_mat[nmode:, at : at + sites] = -imag
        sink_mat[nmode:, at + sites : at + 2 * sites] = real
    stage[...] = source_ref[...].astype(F32)
    for comp in range(comps):
        for part in range(2):
            source_rows[comp, part] = stage[pl.ds(2 * comp + part, nmode, stride=per_mode), :]

    words = gamma_codes()
    for slot, g in enumerate(insertions):
        index = gamma_ref[g]
        word = jnp.int32(words[3])
        for k in (2, 1, 0):
            word = jnp.where(index < 4 * (k + 1), jnp.int32(words[k]), word)
        code = word >> (8 * (index & 3))
        flip = gamma_flip(index)
        buffer = slot // batch % 2
        base = slot % batch * nmode
        cos_row, sin_row = phases[0, slot : slot + 1, :], phases[1, slot : slot + 1, :]
        for spin in range(4):
            power = (code >> (2 * spin)) & 3
            real_unit = jnp.where(power == 0, 1.0, jnp.where(power == 2, -1.0, 0.0))
            imag_unit = jnp.where(power == 1, 1.0, jnp.where(power == 3, -1.0, 0.0))
            cos_now = real_unit * cos_row - imag_unit * sin_row
            sin_now = real_unit * sin_row + imag_unit * cos_row
            taken = (flip ^ spin) * colours
            for colour in range(colours):
                real = source_rows[taken + colour, 0]
                imag = source_rows[taken + colour, 1]
                at = (spin * colours + colour) * 2 * sites
                rotated[buffer, base : base + nmode, at : at + sites] = (
                    real * cos_now - imag * sin_now
                ).astype(BF16)
                rotated[buffer, base : base + nmode, at + sites : at + 2 * sites] = (
                    real * sin_now + imag * cos_now
                ).astype(BF16)
        if slot % batch == batch - 1:
            block = lax.dot_general(
                rotated[buffer],
                sink_mat[...],
                (((1,), (1,)), ((), ())),
                preferred_element_type=F32,
            )
            for k in range(batch):
                where = slot - batch + 1 + k
                per_out = slots // len(outs)
                outs[where // per_out][where % per_out] = block[k * nmode : (k + 1) * nmode]


def meson_partial(sink, source, gamma_index, momenta, pattern, time, nmode, order, slots, outs):
    _, rows, sites = sink.shape
    batch = slots // 2 if slots % 2 == 0 else slots
    comps = rows // nmode // 2
    field = pl.BlockSpec((None, rows, sites), lambda i: (time, 0, 0))
    smem = pl.BlockSpec(memory_space=pltpu.SMEM)
    whole = pl.BlockSpec(pattern.shape, lambda i: (0, 0))
    shape = (slots // outs, nmode, 2 * nmode)
    flops = 2 * slots * nmode * 2 * nmode * rows // nmode * sites
    return pl.pallas_call(
        functools.partial(meson_kernel, order, batch, time=time),
        grid=(1,),
        in_specs=[field, field, smem, smem, whole],
        out_specs=[pl.BlockSpec(shape, lambda i: (0, 0, 0))] * outs,
        out_shape=[jax.ShapeDtypeStruct(shape, F32)] * outs,
        scratch_shapes=[
            pltpu.VMEM((2 * nmode, comps * 2 * sites), BF16),
            pltpu.VMEM((comps, 2, nmode, sites), F32),
            pltpu.VMEM((rows, sites), F32),
            pltpu.VMEM((2, slots, sites), F32),
            pltpu.VMEM((2, batch * nmode, comps * 2 * sites), BF16),
        ],
        compiler_params=pltpu.CompilerParams(vmem_limit_bytes=VMEM_LIMIT),
        cost_estimate=pl.CostEstimate(
            flops=flops, bytes_accessed=4 * rows * sites + 8 * slots * nmode * nmode, transcendentals=0
        ),
        name="meson_blocks",
    )(sink, source, gamma_index, momenta, pattern)


def add_kernel(keep_ref, got_ref, *outs):
    for slot, out in enumerate(outs):
        out[...] = keep_ref[slot] + got_ref[slot]


def add_units(keep, got):
    units = keep.shape[0]
    return pl.pallas_call(
        add_kernel,
        out_shape=[jax.ShapeDtypeStruct(keep.shape[1:], F32)] * units,
        compiler_params=pltpu.CompilerParams(vmem_limit_bytes=VMEM_LIMIT),
        cost_estimate=pl.CostEstimate(
            flops=keep.size, bytes_accessed=12 * keep.size, transcendentals=0
        ),
        name="add_cores",
    )(keep, got)


def sum_kernel(scale, first_ref, *refs):
    terms, out = refs[:-1], refs[-1]
    total = first_ref[...]
    for term in terms:
        total = total + term[...]
    out[...] = total * scale


def sum_units(terms, scale):
    size = terms[0].size
    return pl.pallas_call(
        functools.partial(sum_kernel, scale),
        out_shape=jax.ShapeDtypeStruct(terms[0].shape, F32),
        cost_estimate=pl.CostEstimate(
            flops=4 * size, bytes_accessed=20 * size, transcendentals=0
        ),
        name="sum_chips",
    )(*terms)


def write_rows(matrix, lane, row_count, spaces, subs, outs, staging):
    nmode = matrix.shape[0]
    z, core = lax.axis_index("space"), lax.axis_index("sub")
    for part in range(2):
        staging[part] = matrix[:, part * nmode : (part + 1) * nmode].T
    for c in range(subs):
        for s in range(spaces):
            start = pl.multiple_of(((z ^ s) * subs + (core ^ c)) * row_count, row_count)
            for part in range(2):
                outs[c * spaces + s][lane, part] = staging[part, pl.ds(start, row_count), :]


def split_kernel(spaces, subs, times, *refs):
    fields, outs, staging = refs[:times], refs[times:-1], refs[-1]
    row_count = outs[0].shape[2]
    for time in range(times):
        write_rows(fields[time][...], time, row_count, spaces, subs, outs, staging.at[time])


def split_rows(fields, spaces, subs):
    nmode, times = fields[0].shape[0], len(fields)
    groups = spaces * subs
    shape = (times, 2, nmode // groups, nmode)
    return pl.pallas_call(
        functools.partial(split_kernel, spaces, subs, times),
        out_shape=[jax.ShapeDtypeStruct(shape, F32)] * groups,
        scratch_shapes=[pltpu.VMEM((times, 2, nmode, nmode), F32)],
        cost_estimate=pl.CostEstimate(
            flops=0, bytes_accessed=16 * times * nmode * nmode, transcendentals=0
        ),
        name="split_rows",
    )(*fields)


def product_kernel(spaces, subs, times, tms, pairs_ref, *refs):
    fields, outs, (held, staging) = refs[: times * tms], refs[times * tms : -2], refs[-2:]
    nmode = fields[0].shape[0]
    row_count = outs[0].shape[2]
    mine = lax.axis_index("tm")
    for other in range(tms):
        for time in range(times):
            held[(mine ^ other) * times + time] = fields[other * times + time][...]
    for pair in range(pairs_ref.shape[0]):
        left, right = held[pairs_ref[pair, 0]], held[pairs_ref[pair, 1]]
        swapped = jnp.concatenate([-left[:, nmode:], left[:, :nmode]], axis=1)
        result = lax.dot_general(
            right,
            jnp.concatenate([left, swapped], axis=0),
            (((1,), (0,)), ((), ())),
            preferred_element_type=F32,
            precision=lax.Precision.HIGHEST,
        ) * (1.0 / math.sqrt(nmode))
        write_rows(result, pair, row_count, spaces, subs, outs, staging.at[pair])


def product_rows(time_pairs, fields, spaces, subs, tms):
    nmode, times, pairs = fields[0].shape[0], len(fields) // tms, time_pairs.shape[0]
    groups = spaces * subs
    shape = (pairs, 2, nmode // groups, nmode)
    return pl.pallas_call(
        functools.partial(product_kernel, spaces, subs, times, tms),
        in_specs=[pl.BlockSpec(memory_space=pltpu.SMEM)]
        + [pl.BlockSpec(memory_space=pltpu.VMEM)] * len(fields),
        out_shape=[jax.ShapeDtypeStruct(shape, F32)] * groups,
        scratch_shapes=[
            pltpu.VMEM((times * tms, nmode, 2 * nmode), F32),
            pltpu.VMEM((pairs, 2, nmode, nmode), F32),
        ],
        compiler_params=pltpu.CompilerParams(vmem_limit_bytes=VMEM_LIMIT),
        cost_estimate=pl.CostEstimate(
            flops=8 * pairs * nmode**3, bytes_accessed=32 * nmode * nmode * times, transcendentals=0
        ),
        name="products",
    )(time_pairs, *fields)


def join_kernel(spaces, subs, *refs):
    blocks, out = refs[:-1], refs[-1]
    z, core = lax.axis_index("space"), lax.axis_index("sub")
    for c in range(subs):
        for s in range(spaces):
            out[:, (z ^ s) * subs + (core ^ c)] = blocks[c * spaces + s][...]


def join_blocks(blocks, spaces, subs):
    shape = blocks[0].shape
    return pl.pallas_call(
        functools.partial(join_kernel, spaces, subs),
        out_shape=jax.ShapeDtypeStruct((shape[0], len(blocks)) + shape[1:], F32),
        cost_estimate=pl.CostEstimate(
            flops=0, bytes_accessed=8 * len(blocks) * blocks[0].size, transcendentals=0
        ),
        name="join_blocks",
    )(*blocks)


def swap(value, axis, distance):
    size = lax.axis_size(axis)
    return lax.ppermute(value, axis, [(i, i ^ distance) for i in range(size)])


def spread(blocks, spaces, subs):
    got = list(blocks)
    for s in reversed(range(spaces)):
        for c in reversed(range(subs)):
            if s or c:
                got[c * spaces + s] = swap(blocks[c * spaces + s], ("space", "sub"), s * subs + c)
    return got


def own_insertions(spaces, subs):
    z, core = lax.axis_index("space"), lax.axis_index("sub")
    return [
        (z ^ s) * subs + (core ^ c) for c in reversed(range(subs)) for s in range(spaces)
    ]


def by_owner(sink, source, gamma_index, momenta, pattern, time_pairs, nmode, times, scale):
    spaces, subs, tms = (lax.axis_size(name) for name in ("space", "sub", "tm"))
    order = functools.partial(own_insertions, spaces, subs)
    units = []
    for time in range(times):
        away, keep = meson_partial(
            sink, source, gamma_index, momenta, pattern, time, nmode, order, spaces * subs, 2
        )
        units.append((keep, swap(away, "sub", 1)))
    sums = []
    for keep, got in units:
        parts = list(add_units(keep, got))
        sums.append(
            parts[:1] + [swap(parts[s], "space", s) for s in reversed(range(1, spaces))]
        )
    fields, others = [], []
    for terms in sums:
        fields.append(sum_units(terms, scale))
        others.append(swap(fields[-1], "tm", 1))
    meson_blocks = spread(split_rows(fields, spaces, subs), spaces, subs)
    product_blocks = spread(
        product_rows(time_pairs, fields + others, spaces, subs, tms), spaces, subs
    )
    meson = join_blocks(meson_blocks, spaces, subs)
    products = join_blocks(product_blocks, spaces, subs)
    return meson, products


def by_rows(sink, source, gamma_index, momenta, pattern, time_pairs, nmode, times, scale):
    axes = ("space", "sub")
    highest = lax.Precision.HIGHEST
    insertions = gamma_index.shape[0]
    partial = jnp.stack(
        [
            meson_partial(
                sink,
                source,
                gamma_index,
                momenta,
                pattern,
                time,
                nmode,
                lambda: list(range(insertions)),
                insertions,
                1,
            )[0]
            for time in range(times)
        ]
    )
    partial = partial.reshape(times, insertions, nmode, 2, nmode).transpose(0, 1, 3, 4, 2)
    meson = lax.psum_scatter(partial * scale, axes, scatter_dimension=3, tiled=True)
    rows = lax.all_gather(meson, "tm", axis=0, tiled=True)
    whole = lax.all_gather(rows, axes, axis=3, tiled=True)
    left, right = rows[time_pairs[:, 0]], whole[time_pairs[:, 1]]

    def multiply(a, b):
        return jnp.einsum("qgik,qgkj->qgij", a, b, precision=highest)

    real = multiply(left[:, :, 0], right[:, :, 0]) - multiply(left[:, :, 1], right[:, :, 1])
    imag = multiply(left[:, :, 0], right[:, :, 1]) + multiply(left[:, :, 1], right[:, :, 0])
    return meson, jnp.stack([real, imag], axis=2) / math.sqrt(nmode)


def local(sink_modes, source_modes, gamma_index, momenta, pattern, time_pairs):
    times, nmode, _, comps, sites = sink_modes.shape
    spaces, subs, tms = (lax.axis_size(name) for name in ("space", "sub", "tm"))

    def as_rows(modes):
        return modes.transpose(0, 1, 3, 2, 4).reshape(times, nmode * comps * 2, sites)

    owners = (
        spaces * subs == gamma_index.shape[0]
        and spaces & (spaces - 1) == 0
        and subs == 2
        and tms == 2
    )
    plan = by_owner if owners else by_rows
    scale = 1.0 / math.sqrt(3 * sites * spaces * subs)
    return plan(
        as_rows(sink_modes),
        as_rows(source_modes),
        gamma_index,
        momenta.T,
        pattern,
        time_pairs,
        nmode,
        times,
        scale,
    )


def solution(mesh):
    rows = P(("grp", "tm"), None, None, None, ("space", "sub"))
    in_specs = (rows, rows, P(), P(), P("tm", ("space", "sub")), P("tm", None))
    out_specs = (P(("grp", "tm"), None, None, ("space", "sub"), None),) * 2
    return jax.shard_map(local, mesh=mesh, in_specs=in_specs, out_specs=out_specs, check_vma=False)
```

profile of v0, /device:TPU:0, one launch (start us, length us, event | category | flops | bytes accessed | tf_op | source)
XLA Modules:
  0.0 75.8 jit_solution(11054282776528509593)
XLA Ops:
  0.6 1.4 %copy-done.6 = bf16[2,128,2,12,128]{4,2,3,1,0:T(2,128)(2,1)S(1)} copy-done((bf16[2,128,2,12,128]{4,2,3,1,0:T(2,128)(2,1)S(1)}, bf16[2,128,2,12,128]{4,2,3,1,0:T(2,128)(2,1)}, u32[]{:S(2)}) %copy-start.6) | copy-done | bytes 1572888
  2.0 1.4 %copy-done.7 = bf16[2,128,2,12,128]{4,2,3,1,0:T(2,128)(2,1)S(1)} copy-done((bf16[2,128,2,12,128]{4,2,3,1,0:T(2,128)(2,1)S(1)}, bf16[2,128,2,12,128]{4,2,3,1,0:T(2,128)(2,1)}, u32[]{:S(2)}) %copy-start.7) | copy-done | bytes 1572888
  3.5 0.7 copy-done.8
  4.1 0.7 copy-done.10
  4.8 0.7 copy-done.11
  5.5 4.7 %meson_blocks.2 = (f32[4,128,256]{2,1,0:T(8,128)S(1)}, f32[4,128,256]{2,1,0:T(8,128)S(1)}) custom-call(bf16[2,3072,128]{2,1,0:T(8,128)(2,1)S(1)} %bitcast.7, bf16[2,3072,128]{2,1,0:T(8,128)(2,1)S(1)} %bitcast.9, s32[8]{0:T(128)S(1)} %copy-done.11, s32[3,8]{1,0:T(4,128)S(1)} %bitcast.11, s32[2,128]{1,0:T(2,128)S(1)} %copy-done.10), custom_call_target="tpu_custom_call" | custom-call | flops 1610612736 | bytes 2621440 | tf_op jit(solution)/shard_map/meson_blocks/pallas_call | solution.py:165
  10.7 4.7 %meson_blocks.3 = (f32[4,128,256]{2,1,0:T(8,128)S(1)}, f32[4,128,256]{2,1,0:T(8,128)S(1)}) custom-call(bf16[2,3072,128]{2,1,0:T(8,128)(2,1)S(1)} %bitcast.8, bf16[2,3072,128]{2,1,0:T(8,128)(2,1)S(1)} %bitcast.10, s32[8]{0:T(128)S(1)} %copy-done.11, s32[3,8]{1,0:T(4,128)S(1)} %bitcast.12, s32[2,128]{1,0:T(2,128)S(1)} %copy-done.10), custom_call_target="tpu_custom_call" | custom-call | flops 1610612736 | bytes 2621440 | tf_op jit(solution)/shard_map/meson_blocks/pallas_call | solution.py:165
  15.6 5.1 %collective-permute-start.1 = (f32[128,256]{1,0:T(8,128)S(1)}, f32[128,256]{1,0:T(8,128)S(1)}, u32[]{:S(2)}, u32[]{:S(2)}) collective-permute-start(f32[128,256]{1,0:T(8,128)S(1)} %get-tuple-element.33), channel_id=1, source_target_pairs={{0,12},{4,8},{8,4},{12,0},{1,13},{5,9},{9,5},{13,1},{2,14},{6,10},... | collective-permute-start | bytes 393224 | tf_op jit(solution)/shard_map/ppermute | solution.py:322
  22.1 3.7 %collective-permute-start.5 = (f32[128,256]{1,0:T(8,128)S(1)}, f32[128,256]{1,0:T(8,128)S(1)}, u32[]{:S(2)}, u32[]{:S(2)}) collective-permute-start(f32[128,256]{1,0:T(8,128)S(1)} %get-tuple-element.39), channel_id=1, source_target_pairs={{0,12},{4,8},{8,4},{12,0},{1,13},{5,9},{9,5},{13,1},{2,14},{6,10},... | collective-permute-start | bytes 393224 | tf_op jit(solution)/shard_map/ppermute | solution.py:322
  25.8 5.4 %collective-permute-start.7 = (f32[128,256]{1,0:T(8,128)S(1)}, f32[128,256]{1,0:T(8,128)S(1)}, u32[]{:S(2)}, u32[]{:S(2)}) collective-permute-start(f32[128,256]{1,0:T(8,128)S(1)} %get-tuple-element.41), channel_id=1, source_target_pairs={{0,4},{4,0},{8,12},{12,8},{1,5},{5,1},{9,13},{13,9},{2,6},{6,2},{1... | collective-permute-start | bytes 393224 | tf_op jit(solution)/shard_map/ppermute | solution.py:322
  31.3 7.2 %collective-permute-done.2.refs_1_ = f32[128,256]{1,0:T(8,128)S(1)} collective-permute-done((f32[128,256]{1,0:T(8,128)S(1)}, f32[128,256]{1,0:T(8,128)S(1)}, u32[]{:S(2)}, u32[]{:S(2)}) %collective-permute-start.2) | collective-permute-done | bytes 131104 | tf_op jit(solution)/shard_map/ppermute | solution.py:322
  39.2 1.8 %sum_chips.2.refs_0_ = f32[128,256]{1,0:T(8,128)} custom-call(f32[128,256]{1,0:T(8,128)} %copy-done.2, f32[128,256]{1,0:T(8,128)} %copy-done.12, f32[128,256]{1,0:T(8,128)} %copy-done.14, f32[128,256]{1,0:T(8,128)} %copy-done.16), custom_call_target="tpu_custom_call" | custom-call | flops 131072 | bytes 655360 | tf_op jit(solution)/shard_map/sum_chips/pallas_call | solution.py:214
  41.0 1.5 %collective-permute-start.15 = (f32[128,256]{1,0:T(8,128)}, f32[128,256]{1,0:T(8,128)S(1)}, u32[]{:S(2)}, u32[]{:S(2)}) collective-permute-start(f32[128,256]{1,0:T(8,128)} %sum_chips.2.refs_0_), channel_id=1, source_target_pairs={{0,2},{2,0},{1,3},{3,1},{4,6},{6,4},{5,7},{7,5},{8,10},{10,8},{9,1... | collective-permute-start | bytes 393224 | tf_op jit(solution)/shard_map/ppermute | solution.py:322
  42.5 0.7 collective-permute-done.6.refs_1_
  43.2 0.6 copy-done.15
  43.9 1.8 %sum_chips.3.refs_1_ = f32[128,256]{1,0:T(8,128)} custom-call(f32[128,256]{1,0:T(8,128)} %copy-done.3, f32[128,256]{1,0:T(8,128)} %copy-done.13, f32[128,256]{1,0:T(8,128)} %copy-done.15, f32[128,256]{1,0:T(8,128)} %copy-done.17), custom_call_target="tpu_custom_call" | custom-call | flops 131072 | bytes 655360 | tf_op jit(solution)/shard_map/sum_chips/pallas_call | solution.py:214
  45.7 1.5 %collective-permute-start.16 = (f32[128,256]{1,0:T(8,128)}, f32[128,256]{1,0:T(8,128)S(1)}, u32[]{:S(2)}, u32[]{:S(2)}) collective-permute-start(f32[128,256]{1,0:T(8,128)} %sum_chips.3.refs_1_), channel_id=1, source_target_pairs={{0,2},{2,0},{1,3},{3,1},{4,6},{6,4},{5,7},{7,5},{8,10},{10,8},{9,1... | collective-permute-start | bytes 393224 | tf_op jit(solution)/shard_map/ppermute | solution.py:322
  47.2 1.8 %split_rows.1 = (f32[2,2,16,128]{3,2,1,0:T(8,128)}, f32[2,2,16,128]{3,2,1,0:T(8,128)}, f32[2,2,16,128]{3,2,1,0:T(8,128)}, f32[2,2,16,128]{3,2,1,0:T(8,128)}, f32...) custom-call(f32[128,256]{1,0:T(8,128)} %sum_chips.2.refs_0_, ...), custom_call_target="tpu_custom_call" | custom-call | bytes 524288 | tf_op jit(solution)/shard_map/split_rows/pallas_call | solution.py:247
  49.0 3.1 %collective-permute-start.9 = (f32[2,2,16,128]{3,2,1,0:T(8,128)}, f32[2,2,16,128]{3,2,1,0:T(8,128)S(1)}, u32[]{:S(2)}, u32[]{:S(2)}) collective-permute-start(f32[2,2,16,128]{3,2,1,0:T(8,128)} %get-tuple-element.44), channel_id=1, source_target_pairs={{0,8},{1,9},{4,12},{5,13},{8,0},{9,1},{12,4},{13,5},{2,10},{3,11},... | collective-permute-start | bytes 98312 | tf_op jit(solution)/shard_map/ppermute | solution.py:322
  52.1 1.3 %collective-permute-start.10 = (f32[2,2,16,128]{3,2,1,0:T(8,128)}, f32[2,2,16,128]{3,2,1,0:T(8,128)S(1)}, u32[]{:S(2)}, u32[]{:S(2)}) collective-permute-start(f32[2,2,16,128]{3,2,1,0:T(8,128)} %get-tuple-element.45), channel_id=1, source_target_pairs={{0,12},{1,13},{4,8},{5,9},{8,4},{9,5},{12,0},{13,1},{2,14},{3,15},... | collective-permute-start | bytes 98312 | tf_op jit(solution)/shard_map/ppermute | solution.py:322
  53.5 0.9 %copy-done = f32[128,256]{1,0:T(8,128)S(1)} copy-done((f32[128,256]{1,0:T(8,128)S(1)}, f32[128,256]{1,0:T(8,128)}, u32[]{:S(2)}) %copy-start) | copy-done | bytes 131096
  54.4 0.9 %copy-done.1 = f32[128,256]{1,0:T(8,128)S(1)} copy-done((f32[128,256]{1,0:T(8,128)S(1)}, f32[128,256]{1,0:T(8,128)}, u32[]{:S(2)}) %copy-start.1) | copy-done | bytes 131096
  55.3 1.1 %products.1 = (f32[2,2,16,128]{3,2,1,0:T(8,128)S(1)}, f32[2,2,16,128]{3,2,1,0:T(8,128)S(1)}, f32[2,2,16,128]{3,2,1,0:T(8,128)S(1)}, f32[2,2,16,128]{3,2,1,0:T(8,...) custom-call(s32[2,2]{1,0:T(2,128)S(1)} %copy-done.5, ...), custom_call_target="tpu_custom_call" | custom-call | flops 33554432 | bytes 1048576 | tf_op jit(solution)/shard_map/products/pallas_call | solution.py:283
  57.0 2.8 %collective-permute-start.13 = (f32[2,2,16,128]{3,2,1,0:T(8,128)}, f32[2,2,16,128]{3,2,1,0:T(8,128)S(1)}, u32[]{:S(2)}, u32[]{:S(2)}) collective-permute-start(f32[2,2,16,128]{3,2,1,0:T(8,128)} %get-tuple-element.48), channel_id=1, source_target_pairs={{0,9},{1,8},{4,13},{5,12},{8,1},{9,0},{12,5},{13,4},{2,11},{3,10},... | collective-permute-start | bytes 98312 | tf_op jit(solution)/shard_map/ppermute | solution.py:322
  59.8 1.3 %collective-permute-start.14 = (f32[2,2,16,128]{3,2,1,0:T(8,128)}, f32[2,2,16,128]{3,2,1,0:T(8,128)S(1)}, u32[]{:S(2)}, u32[]{:S(2)}) collective-permute-start(f32[2,2,16,128]{3,2,1,0:T(8,128)} %get-tuple-element.49), channel_id=1, source_target_pairs={{0,13},{1,12},{4,9},{5,8},{8,5},{9,4},{12,1},{13,0},{2,15},{3,14},... | collective-permute-start | bytes 98312 | tf_op jit(solution)/shard_map/ppermute | solution.py:322
  61.2 3.1 %collective-permute-start.18 = (f32[2,2,16,128]{3,2,1,0:T(8,128)S(1)}, f32[2,2,16,128]{3,2,1,0:T(8,128)S(1)}, u32[]{:S(2)}, u32[]{:S(2)}) collective-permute-start(f32[2,2,16,128]{3,2,1,0:T(8,128)S(1)} %get-tuple-element.52), channel_id=1, source_target_pairs={{0,8},{1,9},{4,12},{5,13},{8,0},{9,1},{12,4},{13,5},{2,10},{3,11},... | collective-permute-start | bytes 98312 | tf_op jit(solution)/shard_map/ppermute | solution.py:322
  64.3 1.3 %collective-permute-start.19 = (f32[2,2,16,128]{3,2,1,0:T(8,128)S(1)}, f32[2,2,16,128]{3,2,1,0:T(8,128)S(1)}, u32[]{:S(2)}, u32[]{:S(2)}) collective-permute-start(f32[2,2,16,128]{3,2,1,0:T(8,128)S(1)} %get-tuple-element.53), channel_id=1, source_target_pairs={{0,12},{1,13},{4,8},{5,9},{8,4},{9,5},{12,0},{13,1},{2,14},{3,15},... | collective-permute-start | bytes 98312 | tf_op jit(solution)/shard_map/ppermute | solution.py:322
  66.2 2.2 %collective-permute-start.22 = (f32[2,2,16,128]{3,2,1,0:T(8,128)S(1)}, f32[2,2,16,128]{3,2,1,0:T(8,128)S(1)}, u32[]{:S(2)}, u32[]{:S(2)}) collective-permute-start(f32[2,2,16,128]{3,2,1,0:T(8,128)S(1)} %get-tuple-element.56), channel_id=1, source_target_pairs={{0,9},{1,8},{4,13},{5,12},{8,1},{9,0},{12,5},{13,4},{2,11},{3,10},... | collective-permute-start | bytes 98312 | tf_op jit(solution)/shard_map/ppermute | solution.py:322
  68.5 1.3 %collective-permute-start.23 = (f32[2,2,16,128]{3,2,1,0:T(8,128)S(1)}, f32[2,2,16,128]{3,2,1,0:T(8,128)S(1)}, u32[]{:S(2)}, u32[]{:S(2)}) collective-permute-start(f32[2,2,16,128]{3,2,1,0:T(8,128)S(1)} %get-tuple-element.57), channel_id=1, source_target_pairs={{0,13},{1,12},{4,9},{5,8},{8,5},{9,4},{12,1},{13,0},{2,15},{3,14},... | collective-permute-start | bytes 98312 | tf_op jit(solution)/shard_map/ppermute | solution.py:322
  69.8 1.6 %join_blocks.2 = f32[2,8,2,16,128]{4,3,2,1,0:T(8,128)} custom-call(f32[2,2,16,128]{3,2,1,0:T(8,128)} %get-tuple-element.42.refs_0_, f32[2,2,16,128]{3,2,1,0:T(8,128)} %copy-done.18, f32[2,2,16,128]{3,2,1,0:T(8,128)} %copy-done.19, f32[2,2,16,128]{3,2,1,0:T(8,128)} %copy-done.20, f32[2,2,16,128]{3,2,1,0:T(8,128)} %copy-done.21, f32[2,2,16,128]{3,2,1,0:T(8,128)} %copy-done.22, ...), custom_call_target="tpu_custom_call" | custom-call | bytes 524288 | tf_op jit(solution)/shard_map/join_blocks/pallas_call | solution.py:310
  71.5 2.1 %collective-permute-done.23.refs_7_ = f32[2,2,16,128]{3,2,1,0:T(8,128)S(1)} collective-permute-done((f32[2,2,16,128]{3,2,1,0:T(8,128)S(1)}, f32[2,2,16,128]{3,2,1,0:T(8,128)S(1)}, u32[]{:S(2)}, u32[]{:S(2)}) %collective-permute-start.23) | collective-permute-done | bytes 32800 | tf_op jit(solution)/shard_map/ppermute | solution.py:322
  74.2 1.6 %join_blocks.3 = f32[2,8,2,16,128]{4,3,2,1,0:T(8,128)} custom-call(f32[2,2,16,128]{3,2,1,0:T(8,128)} %copy-done.4, f32[2,2,16,128]{3,2,1,0:T(8,128)} %copy-done.23, f32[2,2,16,128]{3,2,1,0:T(8,128)} %copy-done.24, f32[2,2,16,128]{3,2,1,0:T(8,128)} %copy-done.26, f32[2,2,16,128]{3,2,1,0:T(8,128)} %copy-done.28, f32[2,2,16,128]{3,2,1,0:T(8,128)} %copy-done.29, ...), custom_call_target="tpu_custom_call" | custom-call | bytes 524288 | tf_op jit(solution)/shard_map/join_blocks/pallas_call | solution.py:310
  (90 shorter events, 4.8 us)
Async XLA Ops:
  10.2 5.3 %collective-permute-start = (f32[4,128,256]{2,1,0:T(8,128)S(1)}, f32[4,128,256]{2,1,0:T(8,128)S(1)}, u32[]{:S(2)}, u32[]{:S(2)}) collective-permute-start(f32[4,128,256]{2,1,0:T(8,128)S(1)} %get-tuple-element.31), channel_id=1, source_target_pairs={{0,1},{1,0},{2,3},{3,2},{4,5},{5,4},{6,7},{7,6},{8,9},{9,8},{10,11... | collective-permute-start | bytes 1572872 | tf_op jit(solution)/shard_map/ppermute | solution.py:322
  15.4 6.0 %collective-permute-start.4 = (f32[4,128,256]{2,1,0:T(8,128)S(1)}, f32[4,128,256]{2,1,0:T(8,128)S(1)}, u32[]{:S(2)}, u32[]{:S(2)}) collective-permute-start(f32[4,128,256]{2,1,0:T(8,128)S(1)} %get-tuple-element.37), channel_id=1, source_target_pairs={{0,1},{1,0},{2,3},{3,2},{4,5},{5,4},{6,7},{7,6},{8,9},{9,8},{10,11... | collective-permute-start | bytes 1572872 | tf_op jit(solution)/shard_map/ppermute | solution.py:322
  15.6 5.8 %copy-start.2 = (f32[128,256]{1,0:T(8,128)}, f32[128,256]{1,0:T(8,128)S(1)}, u32[]{:S(2)}) copy-start(f32[128,256]{1,0:T(8,128)S(1)} %get-tuple-element.32.first_ref) | copy-start | bytes 393220
  15.6 37.9 %copy-start.5 = (s32[2,2]{1,0:T(2,128)S(1)}, s32[2,2]{1,0:T(2,128)}, u32[]{:S(2)}) copy-start(s32[2,2]{1,0:T(2,128)} %pairs_ref.1) | copy-start | bytes 52
  15.6 10.2 %collective-permute-start.1 = (f32[128,256]{1,0:T(8,128)S(1)}, f32[128,256]{1,0:T(8,128)S(1)}, u32[]{:S(2)}, u32[]{:S(2)}) collective-permute-start(f32[128,256]{1,0:T(8,128)S(1)} %get-tuple-element.33), channel_id=1, source_target_pairs={{0,12},{4,8},{8,4},{12,0},{1,13},{5,9},{9,5},{13,1},{2,14},{6,10},... | collective-permute-start | bytes 393224 | tf_op jit(solution)/shard_map/ppermute | solution.py:322
  20.7 17.8 %collective-permute-start.2 = (f32[128,256]{1,0:T(8,128)S(1)}, f32[128,256]{1,0:T(8,128)S(1)}, u32[]{:S(2)}, u32[]{:S(2)}) collective-permute-start(f32[128,256]{1,0:T(8,128)S(1)} %get-tuple-element.34), channel_id=1, source_target_pairs={{0,8},{4,12},{8,0},{12,4},{1,9},{5,13},{9,1},{13,5},{2,10},{6,14},... | collective-permute-start | bytes 393224 | tf_op jit(solution)/shard_map/ppermute | solution.py:322
  20.7 17.8 %collective-permute-start.3 = (f32[128,256]{1,0:T(8,128)S(1)}, f32[128,256]{1,0:T(8,128)S(1)}, u32[]{:S(2)}, u32[]{:S(2)}) collective-permute-start(f32[128,256]{1,0:T(8,128)S(1)} %get-tuple-element.35), channel_id=1, source_target_pairs={{0,4},{4,0},{8,12},{12,8},{1,5},{5,1},{9,13},{13,9},{2,6},{6,2},{1... | collective-permute-start | bytes 393224 | tf_op jit(solution)/shard_map/ppermute | solution.py:322
  22.1 20.4 %collective-permute-start.5 = (f32[128,256]{1,0:T(8,128)S(1)}, f32[128,256]{1,0:T(8,128)S(1)}, u32[]{:S(2)}, u32[]{:S(2)}) collective-permute-start(f32[128,256]{1,0:T(8,128)S(1)} %get-tuple-element.39), channel_id=1, source_target_pairs={{0,12},{4,8},{8,4},{12,0},{1,13},{5,9},{9,5},{13,1},{2,14},{6,10},... | collective-permute-start | bytes 393224 | tf_op jit(solution)/shard_map/ppermute | solution.py:322
  25.8 17.4 %collective-permute-start.6 = (f32[128,256]{1,0:T(8,128)S(1)}, f32[128,256]{1,0:T(8,128)S(1)}, u32[]{:S(2)}, u32[]{:S(2)}) collective-permute-start(f32[128,256]{1,0:T(8,128)S(1)} %get-tuple-element.40), channel_id=1, source_target_pairs={{0,8},{4,12},{8,0},{12,4},{1,9},{5,13},{9,1},{13,5},{2,10},{6,14},... | collective-permute-start | bytes 393224 | tf_op jit(solution)/shard_map/ppermute | solution.py:322
  25.8 12.7 %copy-start.12 = (f32[128,256]{1,0:T(8,128)}, f32[128,256]{1,0:T(8,128)S(1)}, u32[]{:S(2)}) copy-start(f32[128,256]{1,0:T(8,128)S(1)} %collective-permute-done.1.refs_0_) | copy-start | bytes 393220
  25.8 17.4 %collective-permute-start.7 = (f32[128,256]{1,0:T(8,128)S(1)}, f32[128,256]{1,0:T(8,128)S(1)}, u32[]{:S(2)}, u32[]{:S(2)}) collective-permute-start(f32[128,256]{1,0:T(8,128)S(1)} %get-tuple-element.41), channel_id=1, source_target_pairs={{0,4},{4,0},{8,12},{12,8},{1,5},{5,1},{9,13},{13,9},{2,6},{6,2},{1... | collective-permute-start | bytes 393224 | tf_op jit(solution)/shard_map/ppermute | solution.py:322
  41.0 12.3 %collective-permute-start.15 = (f32[128,256]{1,0:T(8,128)}, f32[128,256]{1,0:T(8,128)S(1)}, u32[]{:S(2)}, u32[]{:S(2)}) collective-permute-start(f32[128,256]{1,0:T(8,128)} %sum_chips.2.refs_0_), channel_id=1, source_target_pairs={{0,2},{2,0},{1,3},{3,1},{4,6},{6,4},{5,7},{7,5},{8,10},{10,8},{9,1... | collective-permute-start | bytes 393224 | tf_op jit(solution)/shard_map/ppermute | solution.py:322
  45.7 7.7 %collective-permute-start.16 = (f32[128,256]{1,0:T(8,128)}, f32[128,256]{1,0:T(8,128)S(1)}, u32[]{:S(2)}, u32[]{:S(2)}) collective-permute-start(f32[128,256]{1,0:T(8,128)} %sum_chips.3.refs_1_), channel_id=1, source_target_pairs={{0,2},{2,0},{1,3},{3,1},{4,6},{6,4},{5,7},{7,5},{8,10},{10,8},{9,1... | collective-permute-start | bytes 393224 | tf_op jit(solution)/shard_map/ppermute | solution.py:322
  49.0 8.0 %collective-permute-start.8 = (f32[2,2,16,128]{3,2,1,0:T(8,128)}, f32[2,2,16,128]{3,2,1,0:T(8,128)S(1)}, u32[]{:S(2)}, u32[]{:S(2)}) collective-permute-start(f32[2,2,16,128]{3,2,1,0:T(8,128)} %get-tuple-element.43), channel_id=1, source_target_pairs={{0,4},{1,5},{4,0},{5,1},{8,12},{9,13},{12,8},{13,9},{2,6},{3,7},{6... | collective-permute-start | bytes 98312 | tf_op jit(solution)/shard_map/ppermute | solution.py:322
  49.0 10.8 %collective-permute-start.9 = (f32[2,2,16,128]{3,2,1,0:T(8,128)}, f32[2,2,16,128]{3,2,1,0:T(8,128)S(1)}, u32[]{:S(2)}, u32[]{:S(2)}) collective-permute-start(f32[2,2,16,128]{3,2,1,0:T(8,128)} %get-tuple-element.44), channel_id=1, source_target_pairs={{0,8},{1,9},{4,12},{5,13},{8,0},{9,1},{12,4},{13,5},{2,10},{3,11},... | collective-permute-start | bytes 98312 | tf_op jit(solution)/shard_map/ppermute | solution.py:322
  52.1 9.1 %collective-permute-start.10 = (f32[2,2,16,128]{3,2,1,0:T(8,128)}, f32[2,2,16,128]{3,2,1,0:T(8,128)S(1)}, u32[]{:S(2)}, u32[]{:S(2)}) collective-permute-start(f32[2,2,16,128]{3,2,1,0:T(8,128)} %get-tuple-element.45), channel_id=1, source_target_pairs={{0,12},{1,13},{4,8},{5,9},{8,4},{9,5},{12,0},{13,1},{2,14},{3,15},... | collective-permute-start | bytes 98312 | tf_op jit(solution)/shard_map/ppermute | solution.py:322
  53.3 7.8 %collective-permute-start.11 = (f32[2,2,16,128]{3,2,1,0:T(8,128)}, f32[2,2,16,128]{3,2,1,0:T(8,128)S(1)}, u32[]{:S(2)}, u32[]{:S(2)}) collective-permute-start(f32[2,2,16,128]{3,2,1,0:T(8,128)} %get-tuple-element.46), channel_id=1, source_target_pairs={{0,1},{1,0},{4,5},{5,4},{8,9},{9,8},{12,13},{13,12},{2,3},{3,2},{6... | collective-permute-start | bytes 98312 | tf_op jit(solution)/shard_map/ppermute | solution.py:322
  53.4 10.9 %collective-permute-start.12 = (f32[2,2,16,128]{3,2,1,0:T(8,128)}, f32[2,2,16,128]{3,2,1,0:T(8,128)S(1)}, u32[]{:S(2)}, u32[]{:S(2)}) collective-permute-start(f32[2,2,16,128]{3,2,1,0:T(8,128)} %get-tuple-element.47), channel_id=1, source_target_pairs={{0,5},{1,4},{4,1},{5,0},{8,13},{9,12},{12,9},{13,8},{2,7},{3,6},{6... | collective-permute-start | bytes 98312 | tf_op jit(solution)/shard_map/ppermute | solution.py:322
  57.0 12.8 %copy-start.18 = (f32[2,2,16,128]{3,2,1,0:T(8,128)}, f32[2,2,16,128]{3,2,1,0:T(8,128)S(1)}, u32[]{:S(2)}) copy-start(f32[2,2,16,128]{3,2,1,0:T(8,128)S(1)} %collective-permute-done.8.refs_1_) | copy-start | bytes 98308
  57.0 8.5 %collective-permute-start.13 = (f32[2,2,16,128]{3,2,1,0:T(8,128)}, f32[2,2,16,128]{3,2,1,0:T(8,128)S(1)}, u32[]{:S(2)}, u32[]{:S(2)}) collective-permute-start(f32[2,2,16,128]{3,2,1,0:T(8,128)} %get-tuple-element.48), channel_id=1, source_target_pairs={{0,9},{1,8},{4,13},{5,12},{8,1},{9,0},{12,5},{13,4},{2,11},{3,10},... | collective-permute-start | bytes 98312 | tf_op jit(solution)/shard_map/ppermute | solution.py:322
  59.8 10.0 %copy-start.19 = (f32[2,2,16,128]{3,2,1,0:T(8,128)}, f32[2,2,16,128]{3,2,1,0:T(8,128)S(1)}, u32[]{:S(2)}) copy-start(f32[2,2,16,128]{3,2,1,0:T(8,128)S(1)} %collective-permute-done.9.refs_2_) | copy-start | bytes 98308
  59.8 5.8 %collective-permute-start.14 = (f32[2,2,16,128]{3,2,1,0:T(8,128)}, f32[2,2,16,128]{3,2,1,0:T(8,128)S(1)}, u32[]{:S(2)}, u32[]{:S(2)}) collective-permute-start(f32[2,2,16,128]{3,2,1,0:T(8,128)} %get-tuple-element.49), channel_id=1, source_target_pairs={{0,13},{1,12},{4,9},{5,8},{8,5},{9,4},{12,1},{13,0},{2,15},{3,14},... | collective-permute-start | bytes 98312 | tf_op jit(solution)/shard_map/ppermute | solution.py:322
  61.1 8.7 %copy-start.20 = (f32[2,2,16,128]{3,2,1,0:T(8,128)}, f32[2,2,16,128]{3,2,1,0:T(8,128)S(1)}, u32[]{:S(2)}) copy-start(f32[2,2,16,128]{3,2,1,0:T(8,128)S(1)} %collective-permute-done.10.refs_3_) | copy-start | bytes 98308
  61.1 5.1 %collective-permute-start.17 = (f32[2,2,16,128]{3,2,1,0:T(8,128)S(1)}, f32[2,2,16,128]{3,2,1,0:T(8,128)S(1)}, u32[]{:S(2)}, u32[]{:S(2)}) collective-permute-start(f32[2,2,16,128]{3,2,1,0:T(8,128)S(1)} %get-tuple-element.51), channel_id=1, source_target_pairs={{0,4},{1,5},{4,0},{5,1},{8,12},{9,13},{12,8},{13,9},{2,6},{3,7},{6... | collective-permute-start | bytes 98312 | tf_op jit(solution)/shard_map/ppermute | solution.py:322
  61.2 8.7 %copy-start.21 = (f32[2,2,16,128]{3,2,1,0:T(8,128)}, f32[2,2,16,128]{3,2,1,0:T(8,128)S(1)}, u32[]{:S(2)}) copy-start(f32[2,2,16,128]{3,2,1,0:T(8,128)S(1)} %collective-permute-done.11.refs_4_) | copy-start | bytes 98308
  61.2 7.3 %collective-permute-start.18 = (f32[2,2,16,128]{3,2,1,0:T(8,128)S(1)}, f32[2,2,16,128]{3,2,1,0:T(8,128)S(1)}, u32[]{:S(2)}, u32[]{:S(2)}) collective-permute-start(f32[2,2,16,128]{3,2,1,0:T(8,128)S(1)} %get-tuple-element.52), channel_id=1, source_target_pairs={{0,8},{1,9},{4,12},{5,13},{8,0},{9,1},{12,4},{13,5},{2,10},{3,11},... | collective-permute-start | bytes 98312 | tf_op jit(solution)/shard_map/ppermute | solution.py:322
  64.3 7.2 %collective-permute-start.19 = (f32[2,2,16,128]{3,2,1,0:T(8,128)S(1)}, f32[2,2,16,128]{3,2,1,0:T(8,128)S(1)}, u32[]{:S(2)}, u32[]{:S(2)}) collective-permute-start(f32[2,2,16,128]{3,2,1,0:T(8,128)S(1)} %get-tuple-element.53), channel_id=1, source_target_pairs={{0,12},{1,13},{4,8},{5,9},{8,4},{9,5},{12,0},{13,1},{2,14},{3,15},... | collective-permute-start | bytes 98312 | tf_op jit(solution)/shard_map/ppermute | solution.py:322
  65.5 5.9 %collective-permute-start.20 = (f32[2,2,16,128]{3,2,1,0:T(8,128)S(1)}, f32[2,2,16,128]{3,2,1,0:T(8,128)S(1)}, u32[]{:S(2)}, u32[]{:S(2)}) collective-permute-start(f32[2,2,16,128]{3,2,1,0:T(8,128)S(1)} %get-tuple-element.54), channel_id=1, source_target_pairs={{0,1},{1,0},{4,5},{5,4},{8,9},{9,8},{12,13},{13,12},{2,3},{3,2},{6... | collective-permute-start | bytes 98312 | tf_op jit(solution)/shard_map/ppermute | solution.py:322
  65.6 5.9 %collective-permute-start.21 = (f32[2,2,16,128]{3,2,1,0:T(8,128)S(1)}, f32[2,2,16,128]{3,2,1,0:T(8,128)S(1)}, u32[]{:S(2)}, u32[]{:S(2)}) collective-permute-start(f32[2,2,16,128]{3,2,1,0:T(8,128)S(1)} %get-tuple-element.55), channel_id=1, source_target_pairs={{0,5},{1,4},{4,1},{5,0},{8,13},{9,12},{12,9},{13,8},{2,7},{3,6},{6... | collective-permute-start | bytes 98312 | tf_op jit(solution)/shard_map/ppermute | solution.py:322
  66.2 7.4 %copy-start.23 = (f32[2,2,16,128]{3,2,1,0:T(8,128)}, f32[2,2,16,128]{3,2,1,0:T(8,128)S(1)}, u32[]{:S(2)}) copy-start(f32[2,2,16,128]{3,2,1,0:T(8,128)S(1)} %collective-permute-done.17.refs_1_) | copy-start | bytes 98308
  66.2 5.3 %collective-permute-start.22 = (f32[2,2,16,128]{3,2,1,0:T(8,128)S(1)}, f32[2,2,16,128]{3,2,1,0:T(8,128)S(1)}, u32[]{:S(2)}, u32[]{:S(2)}) collective-permute-start(f32[2,2,16,128]{3,2,1,0:T(8,128)S(1)} %get-tuple-element.56), channel_id=1, source_target_pairs={{0,9},{1,8},{4,13},{5,12},{8,1},{9,0},{12,5},{13,4},{2,11},{3,10},... | collective-permute-start | bytes 98312 | tf_op jit(solution)/shard_map/ppermute | solution.py:322
  68.5 5.1 %collective-permute-start.23 = (f32[2,2,16,128]{3,2,1,0:T(8,128)S(1)}, f32[2,2,16,128]{3,2,1,0:T(8,128)S(1)}, u32[]{:S(2)}, u32[]{:S(2)}) collective-permute-start(f32[2,2,16,128]{3,2,1,0:T(8,128)S(1)} %get-tuple-element.57), channel_id=1, source_target_pairs={{0,13},{1,12},{4,9},{5,8},{8,5},{9,4},{12,1},{13,0},{2,15},{3,14},... | collective-permute-start | bytes 98312 | tf_op jit(solution)/shard_map/ppermute | solution.py:322
  (24 other events, 45.0 us)
where the time goes:
time: 76.3 us; the launch traced here: 75.8 us
  starting transfers between devices  35.2 us (46%)
  Pallas kernels  19.2 us (25%)
  waiting for transfers between devices  10.7 us (14%)
  local copies, waits for them, and re-layouts  9.87 us (13%)
  between operations  0.93 us (1%)
    ppermute x24, starting transfers between devices, swap(): return lax.ppermute(value, axis, [(i, i ^ distance) for i in range(size)])  35.2 us
    ppermute x24, waiting for transfers between devices, swap(): return lax.ppermute(value, axis, [(i, i ^ distance) for i in range(size)])  10.7 us
    unnamed x64, local copies, waits for them, and re-layouts  9.87 us
    pallas_call x2, Pallas kernels, meson_partial(): pl.pallas_call(functools.partial(meson_kernel, order, batch, time=time),...  9.39 us
    pallas_call x2, Pallas kernels, sum_units(): pl.pallas_call(functools.partial(sum_kernel, scale), out_shape=jax.ShapeD...  3.54 us
    pallas_call x2, Pallas kernels, join_blocks(): pl.pallas_call(functools.partial(join_kernel, spaces, subs), out_shape=ja...  3.21 us
    pallas_call x1, Pallas kernels, split_rows(): pl.pallas_call(functools.partial(split_kernel, spaces, subs, times), out_...  1.8 us
  transfers between devices with their start and end apart: 24, of which 4 were waited for; matrix products, arithmetic and copies ran while one was open for 0% of the time, Pallas kernels for 17%

commit v1 on v0

v1 whole, which is shorter than its diff:
```python
import functools
import math

import jax
import jax.numpy as jnp
import numpy as np
from jax import lax
from jax.experimental import pallas as pl
from jax.experimental.pallas import tpu as pltpu
from jax.sharding import PartitionSpec as P

LAT = 96
CLASSES = 4
F32 = jnp.float32
BF16 = jnp.bfloat16
VMEM_LIMIT = 16 * 2**20
SMALL_LIMIT = 4 * 2**20


def build_gammas():
    sigmas = [
        np.array([[0, 1], [1, 0]], dtype=complex),
        np.array([[0, -1j], [1j, 0]], dtype=complex),
        np.array([[1, 0], [0, -1]], dtype=complex),
    ]
    zero, one = np.zeros((2, 2), dtype=complex), np.eye(2, dtype=complex)
    gammas = [np.block([[zero, 1j * s], [-1j * s, zero]]) for s in sigmas]
    gammas.append(np.block([[zero, one], [one, zero]]))
    tables = []
    for subset in range(16):
        product = np.eye(4, dtype=complex)
        for factor in range(4):
            if subset >> factor & 1:
                product = product @ gammas[factor]
        tables.append(product)
    return tables


def gamma_codes():
    words = [0, 0, 0, 0]
    for index, table in enumerate(build_gammas()):
        flip = gamma_flip(index)
        for row in range(4):
            entry = table[row, row ^ flip]
            power = [k for k in range(4) if abs(entry - 1j**k) < 1e-6]
            assert len(power) == 1 and np.count_nonzero(table[row]) == 1
            words[index // 4] |= power[0] << (8 * (index % 4) + 2 * row)
    return [word - 2**32 if word >= 2**31 else word for word in words]


def gamma_flip(index):
    b1, b2, b3, b4 = (index & 1, (index >> 1) & 1, (index >> 2) & 1, (index >> 3) & 1)
    return (b1 ^ b2) | ((b1 ^ b2 ^ b3 ^ b4) << 1)


def site_coords(site):
    coords = []
    for axis in range(3):
        total = jnp.zeros_like(site)
        for level in range(6):
            total = total + (((site >> (3 * level + axis)) & 1) << level)
        coords.append(total)
    return coords


def wave_phases(insertions, momenta_ref, pattern_row):
    sites = pattern_row.shape[1]
    fours = insertions // CLASSES
    first_site = (
        lax.axis_index("space") * lax.axis_size("sub") + lax.axis_index("sub")
    ) * sites
    site = lax.broadcasted_iota(jnp.int32, (1, sites), 1) + first_site
    coords = site_coords(site)
    rows = []
    for four in range(fours):
        wave = jnp.zeros_like(site)
        for axis in range(3):
            chosen = jnp.zeros_like(site)
            for kind in range(CLASSES):
                chosen = jnp.where(
                    pattern_row == kind, momenta_ref[axis, four * CLASSES + kind], chosen
                )
            wave = wave + coords[axis] * chosen
        laps = jnp.floor((wave.astype(F32) + 0.5) * (1.0 / LAT)).astype(jnp.int32)
        rows.append((wave - LAT * laps).astype(F32) * (2.0 * math.pi / LAT))
    angle = jnp.concatenate(rows, axis=0)
    return jnp.cos(angle), jnp.sin(angle)


def multiply_slots(
    insertions, slots, gamma_ref, pattern_row, sink_mat, turned, buffers, out
):
    _, comps, _, nmode, sites = turned.shape
    colours = comps // 4
    words = gamma_codes()
    parts = len(buffers)
    per_part = comps // parts
    plan = []
    for slot in slots:
        g = insertions[slot]
        index = gamma_ref[g]
        word = jnp.int32(words[3])
        for step in (2, 1, 0):
            word = jnp.where(index < 4 * (step + 1), jnp.int32(words[step]), word)
        code = word >> (8 * (index & 3))
        mask = jnp.where(pattern_row == lax.rem(g, CLASSES), 1.0, 0.0)
        rows = []
        for spin in range(4):
            power = (code >> (2 * spin)) & 3
            real_sign = jnp.where((power == 0) | (power == 3), 1.0, -1.0)
            imag_sign = jnp.where(power < 2, 1.0, -1.0)
            rows.append(
                (
                    power & 1,
                    (gamma_flip(index) ^ spin) * colours,
                    (mask * real_sign).astype(BF16),
                    (mask * imag_sign).astype(BF16),
                )
            )
        plan.append((g // CLASSES, rows))
    for part in range(parts):
        buffer = buffers[part]
        for k, (four, rows) in enumerate(plan):
            base = k * nmode
            for step in range(per_part):
                comp = part * per_part + step
                odd, taken, real_row, imag_row = rows[comp // colours]
                source = taken + comp % colours
                at = step * 2 * sites
                buffer[base : base + nmode, at : at + sites] = (
                    turned[four, source, odd] * real_row
                )
                buffer[base : base + nmode, at + sites : at + 2 * sites] = (
                    turned[four, source, 1 - odd] * imag_row
                )
        width = per_part * 2 * sites
        block = lax.dot_general(
            buffer[...],
            sink_mat[:, part * width : (part + 1) * width],
            (((1,), (1,)), ((), ())),
            preferred_element_type=F32,
        ).reshape(out.shape)
        out[...] = block if part == 0 else out[...] + block


def first_kernel(
    order,
    time,
    slots,
    chunks,
    sink_hbm,
    source_hbm,
    gamma_hbm,
    momenta_hbm,
    pattern_hbm,
    out,
    sink_mat,
    turned,
    sink_raw,
    source_raw,
    sink_stage,
    source_stage,
    gamma_ref,
    momenta_ref,
    pattern_ref,
    small_sems,
    big_sems,
    *buffers,
):
    rows, sites = sink_raw.shape
    fours, _, _, nmode, _ = turned.shape
    per_mode = rows // nmode
    comps = per_mode // 2
    insertions = order()
    small = [
        pltpu.make_async_copy(src, dst, small_sems.at[k])
        for k, (src, dst) in enumerate(
            [(momenta_hbm, momenta_ref), (pattern_hbm, pattern_ref), (gamma_hbm, gamma_ref)]
        )
    ]
    for copy in small:
        copy.start()
    height = rows // chunks
    big = []
    for which, (src, dst) in enumerate([(sink_hbm, sink_raw), (source_hbm, source_raw)]):
        for k in range(chunks):
            part = pl.ds(k * height, height)
            copy = pltpu.make_async_copy(
                src.at[time, part], dst.at[part], big_sems.at[which * chunks + k]
            )
            copy.start()
            big.append(copy)
    for copy in small:
        copy.wait()
    pattern_row = pattern_ref[time : time + 1, :]
    cosine, sine = wave_phases(fours * CLASSES, momenta_ref, pattern_row)

    for k in range(chunks):
        part = slice(k * height, (k + 1) * height)
        big[k].wait()
        sink_stage[part] = sink_raw[part].astype(F32)
    for comp in range(comps):
        at = comp * 2 * sites
        real = sink_stage[pl.ds(2 * comp, nmode, stride=per_mode), :].astype(BF16)
        imag = sink_stage[pl.ds(2 * comp + 1, nmode, stride=per_mode), :].astype(BF16)
        sink_mat[0:nmode, at : at + sites] = real
        sink_mat[0:nmode, at + sites : at + 2 * sites] = imag
        sink_mat[nmode:, at : at + sites] = -imag
        sink_mat[nmode:, at + sites : at + 2 * sites] = real
    for k in range(chunks):
        part = slice(k * height, (k + 1) * height)
        big[chunks + k].wait()
        source_stage[part] = source_raw[part].astype(F32)
    for comp in range(comps):
        real = source_stage[pl.ds(2 * comp, nmode, stride=per_mode), :]
        imag = source_stage[pl.ds(2 * comp + 1, nmode, stride=per_mode), :]
        for four in range(fours):
            cos_row, sin_row = cosine[four : four + 1], sine[four : four + 1]
            turned[four, comp, 0] = (real * cos_row - imag * sin_row).astype(BF16)
            turned[four, comp, 1] = (real * sin_row + imag * cos_row).astype(BF16)
    multiply_slots(insertions, slots, gamma_ref, pattern_row, sink_mat, turned, buffers, out)


def block_cost(slots, nmode, depth):
    return pl.CostEstimate(
        flops=4 * slots * nmode * nmode * depth,
        bytes_accessed=8 * nmode * depth,
        transcendentals=0,
    )


def product_buffers(slots, nmode, depth):
    parts = 2
    return [pltpu.VMEM((slots * nmode, depth // parts), BF16)] * parts


def first_blocks(sink, source, gamma_index, momenta, pattern, time, nmode, order, slots):
    _, rows, sites = sink.shape
    comps = rows // nmode // 2
    depth = comps * 2 * sites
    chunks = 4 if rows % 64 == 0 else 1
    fours = gamma_index.shape[0] // CLASSES
    return pl.pallas_call(
        functools.partial(first_kernel, order, time, slots, chunks),
        in_specs=[pl.BlockSpec(memory_space=pltpu.HBM)] * 5,
        out_shape=[
            jax.ShapeDtypeStruct((len(slots), nmode, 2 * nmode), F32),
            jax.ShapeDtypeStruct((2 * nmode, depth), BF16),
            jax.ShapeDtypeStruct((fours, comps, 2, nmode, sites), BF16),
        ],
        scratch_shapes=[
            pltpu.VMEM((rows, sites), BF16),
            pltpu.VMEM((rows, sites), BF16),
            pltpu.VMEM((rows, sites), F32),
            pltpu.VMEM((rows, sites), F32),
            pltpu.SMEM(gamma_index.shape, jnp.int32),
            pltpu.SMEM(momenta.shape, jnp.int32),
            pltpu.VMEM(pattern.shape, jnp.int32),
            pltpu.SemaphoreType.DMA((3,)),
            pltpu.SemaphoreType.DMA((2 * chunks,)),
        ]
        + product_buffers(len(slots), nmode, depth),
        compiler_params=pltpu.CompilerParams(vmem_limit_bytes=VMEM_LIMIT),
        cost_estimate=block_cost(len(slots), nmode, depth),
        name="first_blocks",
    )(sink, source, gamma_index, momenta, pattern)


def later_kernel(
    order,
    time,
    slots,
    gamma_hbm,
    pattern_hbm,
    sink_mat,
    turned,
    out,
    gamma_ref,
    pattern_ref,
    sems,
    *buffers,
):
    copies = [
        pltpu.make_async_copy(gamma_hbm, gamma_ref, sems.at[0]),
        pltpu.make_async_copy(pattern_hbm, pattern_ref, sems.at[1]),
    ]
    for copy in copies:
        copy.start()
    for copy in copies:
        copy.wait()
    pattern_row = pattern_ref[time : time + 1, :]
    multiply_slots(order(), slots, gamma_ref, pattern_row, sink_mat, turned, buffers, out)


def later_blocks(gamma_index, pattern, sink_mat, turned, time, order, slots):
    nmode, depth = turned.shape[3], sink_mat.shape[1]
    return pl.pallas_call(
        functools.partial(later_kernel, order, time, slots),
        in_specs=[pl.BlockSpec(memory_space=pltpu.HBM)] * 2
        + [pl.BlockSpec(memory_space=pltpu.VMEM)] * 2,
        out_shape=jax.ShapeDtypeStruct((len(slots), nmode, 2 * nmode), F32),
        scratch_shapes=[
            pltpu.SMEM(gamma_index.shape, jnp.int32),
            pltpu.VMEM(pattern.shape, jnp.int32),
            pltpu.SemaphoreType.DMA((2,)),
        ]
        + product_buffers(len(slots), nmode, depth),
        compiler_params=pltpu.CompilerParams(vmem_limit_bytes=VMEM_LIMIT),
        cost_estimate=block_cost(len(slots), nmode, depth),
        name="later_blocks",
    )(gamma_index, pattern, sink_mat, turned)


def add_kernel(keep_ref, got_ref, *outs):
    for slot, out in enumerate(outs):
        out[...] = keep_ref[slot] + got_ref[slot]


def add_units(keep, got):
    units = keep.shape[0]
    return pl.pallas_call(
        add_kernel,
        out_shape=[jax.ShapeDtypeStruct(keep.shape[1:], F32)] * units,
        compiler_params=pltpu.CompilerParams(vmem_limit_bytes=SMALL_LIMIT),
        cost_estimate=pl.CostEstimate(
            flops=keep.size, bytes_accessed=12 * keep.size, transcendentals=0
        ),
        name="add_cores",
    )(keep, got)


def sum_kernel(scale, first_ref, *refs):
    terms, out = refs[:-1], refs[-1]
    total = first_ref[...]
    for term in terms:
        total = total + term[...]
    out[...] = total * scale


def sum_units(terms, scale):
    size = terms[0].size
    return pl.pallas_call(
        functools.partial(sum_kernel, scale),
        out_shape=jax.ShapeDtypeStruct(terms[0].shape, F32),
        cost_estimate=pl.CostEstimate(
            flops=4 * size, bytes_accessed=20 * size, transcendentals=0
        ),
        compiler_params=pltpu.CompilerParams(vmem_limit_bytes=SMALL_LIMIT),
        name="sum_chips",
    )(*terms)


def write_rows(matrix, lane, spaces, subs, outs, staging):
    nmode, row_count = matrix.shape[0], outs[0].shape[3]
    z, core = lax.axis_index("space"), lax.axis_index("sub")
    for part in range(2):
        staging[part] = matrix[:, part * nmode : (part + 1) * nmode].T
    for c in range(subs):
        for s in range(spaces):
            start = pl.multiple_of(((z ^ s) * subs + (core ^ c)) * row_count, row_count)
            for part in range(2):
                outs[c][s, lane, part] = staging[part, pl.ds(start, row_count), :]


def split_kernel(spaces, subs, times, *refs):
    fields, outs, staging = refs[:times], refs[times:-1], refs[-1]
    for time in range(times):
        write_rows(fields[time][...], time, spaces, subs, outs, staging.at[time])


def split_rows(fields, spaces, subs):
    nmode, times = fields[0].shape[0], len(fields)
    groups = spaces * subs
    shape = (spaces, times, 2, nmode // groups, nmode)
    return pl.pallas_call(
        functools.partial(split_kernel, spaces, subs, times),
        out_shape=[jax.ShapeDtypeStruct(shape, F32)] * subs,
        scratch_shapes=[pltpu.VMEM((times, 2, nmode, nmode), F32)],
        cost_estimate=pl.CostEstimate(
            flops=0, bytes_accessed=16 * times * nmode * nmode, transcendentals=0
        ),
        compiler_params=pltpu.CompilerParams(vmem_limit_bytes=SMALL_LIMIT),
        name="split_rows",
    )(*fields)


def product_kernel(spaces, subs, times, tms, pairs_ref, *refs):
    fields, outs, (held, staging) = refs[: times * tms], refs[times * tms : -2], refs[-2:]
    nmode = fields[0].shape[0]
    mine = lax.axis_index("tm")
    for other in range(tms):
        for time in range(times):
            held[(mine ^ other) * times + time] = fields[other * times + time][...]
    for pair in range(pairs_ref.shape[0]):
        left, right = held[pairs_ref[pair, 0]], held[pairs_ref[pair, 1]]
        swapped = jnp.concatenate([-left[:, nmode:], left[:, :nmode]], axis=1)
        result = lax.dot_general(
            right,
            jnp.concatenate([left, swapped], axis=0),
            (((1,), (0,)), ((), ())),
            preferred_element_type=F32,
            precision=lax.Precision.HIGHEST,
        ) * (1.0 / math.sqrt(nmode))
        write_rows(result, pair, spaces, subs, outs, staging.at[pair])


def product_rows(time_pairs, fields, spaces, subs, tms):
    nmode, times, pairs = fields[0].shape[0], len(fields) // tms, time_pairs.shape[0]
    groups = spaces * subs
    shape = (spaces, pairs, 2, nmode // groups, nmode)
    return pl.pallas_call(
        functools.partial(product_kernel, spaces, subs, times, tms),
        in_specs=[pl.BlockSpec(memory_space=pltpu.SMEM)]
        + [pl.BlockSpec(memory_space=pltpu.VMEM)] * len(fields),
        out_shape=[jax.ShapeDtypeStruct(shape, F32)] * subs,
        scratch_shapes=[
            pltpu.VMEM((times * tms, nmode, 2 * nmode), F32),
            pltpu.VMEM((pairs, 2, nmode, nmode), F32),
        ],
        compiler_params=pltpu.CompilerParams(vmem_limit_bytes=SMALL_LIMIT),
        cost_estimate=pl.CostEstimate(
            flops=8 * pairs * nmode**3, bytes_accessed=32 * nmode * nmode * times, transcendentals=0
        ),
        name="products",
    )(time_pairs, *fields)


def pair_kernel(keep_ref, got_ref, *outs):
    for s, out in enumerate(outs):
        out[0] = keep_ref[s]
        out[1] = got_ref[s]


def pair_cores(keep, got):
    shape = keep.shape
    return pl.pallas_call(
        pair_kernel,
        out_shape=[jax.ShapeDtypeStruct((2,) + shape[1:], F32)] * shape[0],
        compiler_params=pltpu.CompilerParams(vmem_limit_bytes=SMALL_LIMIT),
        cost_estimate=pl.CostEstimate(
            flops=0, bytes_accessed=16 * keep.size, transcendentals=0
        ),
        name="pair_cores",
    )(keep, got)


def join_kernel(spaces, subs, *refs):
    blocks, out = refs[:-1], refs[-1]
    z, core = lax.axis_index("space"), lax.axis_index("sub")
    for s in range(spaces):
        for c in range(subs):
            out[:, (z ^ s) * subs + (core ^ c)] = blocks[s][c]


def join_blocks(blocks, spaces, subs):
    shape = blocks[0].shape
    return pl.pallas_call(
        functools.partial(join_kernel, spaces, subs),
        out_shape=jax.ShapeDtypeStruct((shape[1], spaces * subs) + shape[2:], F32),
        compiler_params=pltpu.CompilerParams(vmem_limit_bytes=SMALL_LIMIT),
        cost_estimate=pl.CostEstimate(
            flops=0, bytes_accessed=8 * len(blocks) * blocks[0].size, transcendentals=0
        ),
        name="join_blocks",
    )(*blocks)


def swap(value, axis, distance):
    size = lax.axis_size(axis)
    return lax.ppermute(value, axis, [(i, i ^ distance) for i in range(size)])


def chip_order(spaces):
    return sorted(range(1, spaces), key=lambda s: (s & (s - 1) != 0, s == 1, -s))


def swap_chips(parts, spaces):
    got = list(parts)
    for s in chip_order(spaces):
        got[s] = swap(parts[s], "space", s)
    return got


def spread(keep, away, spaces, subs):
    parts = pair_cores(keep, swap(away, "sub", 1))
    return join_blocks(swap_chips(parts, spaces), spaces, subs)


def own_insertions(spaces, subs):
    z, core = lax.axis_index("space"), lax.axis_index("sub")
    return [(z ^ s) * subs + (core ^ c) for c in range(subs) for s in range(spaces)]


def by_owner(sink, source, gamma_index, momenta, pattern, time_pairs, nmode, times, scale):
    spaces, subs, tms = (lax.axis_size(name) for name in ("space", "sub", "tm"))
    order = functools.partial(own_insertions, spaces, subs)
    mine, other = list(range(spaces)), list(range(spaces, 2 * spaces))
    fields, others = [], []
    sums = []
    for time in range(times):
        if sums:
            gamma_index, sums[-1] = lax.optimization_barrier((gamma_index, sums[-1]))
        away, *laid = first_blocks(
            sink, source, gamma_index, momenta, pattern, time, nmode, order, other
        )
        got = swap(away, "sub", 1)
        keep = later_blocks(gamma_index, pattern, *laid, time, order, mine)
        sums.append(add_units(keep, got))
    for parts in sums:
        fields.append(sum_units(swap_chips(parts, spaces), scale))
        others.append(swap(fields[-1], "tm", 1))
    keep, away = split_rows(fields, spaces, subs)
    meson = spread(keep, away, spaces, subs)
    keep, away = product_rows(time_pairs, fields + others, spaces, subs, tms)
    products = spread(keep, away, spaces, subs)
    return meson, products


def by_rows(sink, source, gamma_index, momenta, pattern, time_pairs, nmode, times, scale):
    axes = ("space", "sub")
    highest = lax.Precision.HIGHEST
    insertions = gamma_index.shape[0]
    partial = jnp.stack(
        [
            first_blocks(
                sink,
                source,
                gamma_index,
                momenta,
                pattern,
                time,
                nmode,
                lambda: list(range(insertions)),
                list(range(insertions)),
            )[0]
            for time in range(times)
        ]
    )
    partial = partial.reshape(times, insertions, nmode, 2, nmode).transpose(0, 1, 3, 4, 2)
    meson = lax.psum_scatter(partial * scale, axes, scatter_dimension=3, tiled=True)
    rows = lax.all_gather(meson, "tm", axis=0, tiled=True)
    whole = lax.all_gather(rows, axes, axis=3, tiled=True)
    left, right = rows[time_pairs[:, 0]], whole[time_pairs[:, 1]]

    def multiply(a, b):
        return jnp.einsum("qgik,qgkj->qgij", a, b, precision=highest)

    real = multiply(left[:, :, 0], right[:, :, 0]) - multiply(left[:, :, 1], right[:, :, 1])
    imag = multiply(left[:, :, 0], right[:, :, 1]) + multiply(left[:, :, 1], right[:, :, 0])
    return meson, jnp.stack([real, imag], axis=2) / math.sqrt(nmode)


def local(sink_modes, source_modes, gamma_index, momenta, pattern, time_pairs):
    times, nmode, _, comps, sites = sink_modes.shape
    spaces, subs, tms = (lax.axis_size(name) for name in ("space", "sub", "tm"))

    def as_rows(modes):
        return modes.transpose(0, 1, 3, 2, 4).reshape(times, nmode * comps * 2, sites)

    owners = (
        spaces * subs == gamma_index.shape[0]
        and spaces & (spaces - 1) == 0
        and subs == 2
        and tms == 2
    )
    plan = by_owner if owners else by_rows
    arrays = (as_rows(sink_modes), as_rows(source_modes), gamma_index, momenta.T, pattern)
    arrays = [pltpu.with_memory_space_constraint(a, pltpu.HBM) for a in arrays]
    scale = 1.0 / math.sqrt(3 * sites * spaces * subs)
    return plan(*arrays, time_pairs, nmode, times, scale)


def solution(mesh):
    rows = P(("grp", "tm"), None, None, None, ("space", "sub"))
    in_specs = (rows, rows, P(), P(), P("tm", ("space", "sub")), P("tm", None))
    out_specs = (P(("grp", "tm"), None, None, ("space", "sub"), None),) * 2
    return jax.shard_map(local, mesh=mesh, in_specs=in_specs, out_specs=out_specs, check_vma=False)
```

time: 76.3 us -> 61 us (0.80)
  waiting for transfers between devices: 10.7 us -> 23 us
  starting transfers between devices: 35.2 us -> 23.5 us
  local copies, waits for them, and re-layouts: 9.87 us -> 0.01 us
  Pallas kernels: 19.2 us -> 13.5 us
    ppermute x24 -> x18, waiting for transfers between devices: 10.7 us -> 23 us  [swap(): return lax.ppermute(value, axis, [(i, i ^ distance) for i in range(size)])]
    ppermute x24 -> x18, starting transfers between devices: 35.2 us -> 23.5 us  [swap(): return lax.ppermute(value, axis, [(i, i ^ distance) for i in range(size)])]
    unnamed x64 -> x2, local copies, waits for them, and re-layouts: 9.87 us -> 0.01 us
    pallas_call x2, Pallas kernels: 3.54 us -> 0.06 us  [sum_units(): pl.pallas_call(functools.partial(sum_kernel, scale), out_shape=jax.ShapeD...]
    pallas_call x2, Pallas kernels: 3.21 us -> 1.45 us  [join_blocks(): pl.pallas_call(functools.partial(join_kernel, spaces, subs), out_shape=ja...]
    pallas_call x1, Pallas kernels: 1.8 us -> 0.14 us  [split_rows(): pl.pallas_call(functools.partial(split_kernel, spaces, subs, times), out_...]
    pallas_call x2 -> x6, Pallas kernels: 9.39 us -> 10.6 us  [the longest x2 7.1 us: first_blocks(): pl.pallas_call(functools.partial(first_kernel, order, time, slots, chunks...]
  transfers between devices with their start and end apart: 24 -> 18, of which waited for: 4 -> 5; matrix products, arithmetic and copies ran while one was open for 0% -> 0% of each run, Pallas kernels for 17% -> 9%
where the time goes in v1:
time: 61 us; the launch traced here: 60.8 us
  starting transfers between devices  23.5 us (39%)
  waiting for transfers between devices  23 us (38%)
  Pallas kernels  13.5 us (22%)
  between operations  0.78 us (1%)
    ppermute x18, starting transfers between devices, swap(): return lax.ppermute(value, axis, [(i, i ^ distance) for i in range(size)])  23.5 us
    ppermute x18, waiting for transfers between devices, swap(): return lax.ppermute(value, axis, [(i, i ^ distance) for i in range(size)])  23 us
    pallas_call x2, Pallas kernels, first_blocks(): pl.pallas_call(functools.partial(first_kernel, order, time, slots, chunks...  7.1 us
    pallas_call x2, Pallas kernels, later_blocks(): pl.pallas_call(functools.partial(later_kernel, order, time, slots), in_sp...  3.48 us
    pallas_call x2, Pallas kernels, join_blocks(): pl.pallas_call(functools.partial(join_kernel, spaces, subs), out_shape=ja...  1.45 us
  transfers between devices with their start and end apart: 18, of which 5 were waited for; matrix products, arithmetic and copies ran while one was open for 0% of the time, Pallas kernels for 9%

profile of v1, /device:TPU:0, one launch (start us, length us, event | category | flops | bytes accessed | tf_op | source)
XLA Modules:
  0.0 60.8 jit_solution(3127146744210894379)
XLA Ops:
  0.6 3.5 %first_blocks.2 = (f32[4,128,256]{2,1,0:T(8,128)S(1)}, bf16[256,3072]{1,0:T(8,128)(2,1)S(1)}, bf16[2,12,2,128,128]{4,3,2,1,0:T(8,128)(2,1)S(1)}) custom-call(bf16[2,3072,128]{2,1,0:T(8,128)(2,1)} %bitcast.7, bf16[2,3072,128]{2,1,0:T(8,128)(2,1)} %bitcast.9, s32[8]{0:T(128)} %gamma_hbm.5, s32[3,8]{1,0:T(4,128)} %bitcast.11, s32[2,128]{1,0:T(2,128)} %pattern_hbm.7), custom_call_target="tpu_custom_call" | custom-call | flops 805306368 | bytes 3145728 | tf_op jit(solution)/shard_map/first_blocks/pallas_call | solution.py:243
  4.2 0.5 collective-permute-start
  4.7 1.7 %later_blocks.2.keep_ref = f32[4,128,256]{2,1,0:T(8,128)S(1)} custom-call(s32[8]{0:T(128)} %gamma_hbm.5, s32[2,128]{1,0:T(2,128)} %pattern_hbm.7, bf16[256,3072]{1,0:T(8,128)(2,1)S(1)} %get-tuple-element.33.sink_mat, bf16[2,12,2,128,128]{4,3,2,1,0:T(8,128)(2,1)S(1)} %get-tuple-element.34.turned), custom_call_target="tpu_custom_call" | custom-call | flops 805306368 | bytes 3145728 | tf_op jit(solution)/shard_map/later_blocks/pallas_call | solution.py:297
  6.5 0.1 add_cores.2
  6.5 3.5 %first_blocks.3 = (f32[4,128,256]{2,1,0:T(8,128)S(1)}, bf16[256,3072]{1,0:T(8,128)(2,1)S(1)}, bf16[2,12,2,128,128]{4,3,2,1,0:T(8,128)(2,1)S(1)}) custom-call(bf16[2,3072,128]{2,1,0:T(8,128)(2,1)} %bitcast.8, bf16[2,3072,128]{2,1,0:T(8,128)(2,1)} %bitcast.10, s32[8]{0:T(128)} %gamma_hbm.5, s32[3,8]{1,0:T(4,128)} %bitcast.12, s32[2,128]{1,0:T(2,128)} %pattern_hbm.7), custom_call_target="tpu_custom_call" | custom-call | flops 805306368 | bytes 3145728 | tf_op jit(solution)/shard_map/first_blocks/pallas_call | solution.py:243
  10.1 0.2 collective-permute-start.4
  10.3 2.9 %collective-permute-start.1 = (f32[128,256]{1,0:T(8,128)S(1)}, f32[128,256]{1,0:T(8,128)S(1)}, u32[]{:S(2)}, u32[]{:S(2)}) collective-permute-start(f32[128,256]{1,0:T(8,128)S(1)} %get-tuple-element.41), channel_id=1, source_target_pairs={{0,4},{4,0},{8,12},{12,8},{1,5},{5,1},{9,13},{13,9},{2,6},{6,2},{1... | collective-permute-start | bytes 393224 | tf_op jit(solution)/shard_map/ppermute | solution.py:470
  13.2 2.6 %collective-permute-start.2 = (f32[128,256]{1,0:T(8,128)S(1)}, f32[128,256]{1,0:T(8,128)S(1)}, u32[]{:S(2)}, u32[]{:S(2)}) collective-permute-start(f32[128,256]{1,0:T(8,128)S(1)} %get-tuple-element.42), channel_id=1, source_target_pairs={{0,8},{4,12},{8,0},{12,4},{1,9},{5,13},{9,1},{13,5},{2,10},{6,14},... | collective-permute-start | bytes 393224 | tf_op jit(solution)/shard_map/ppermute | solution.py:470
  15.8 1.7 %later_blocks.3.keep_ref = f32[4,128,256]{2,1,0:T(8,128)S(1)} custom-call(s32[8]{0:T(128)} %gamma_hbm.5, s32[2,128]{1,0:T(2,128)} %pattern_hbm.7, bf16[256,3072]{1,0:T(8,128)(2,1)S(1)} %get-tuple-element.45.sink_mat, bf16[2,12,2,128,128]{4,3,2,1,0:T(8,128)(2,1)S(1)} %get-tuple-element.46.turned), custom_call_target="tpu_custom_call" | custom-call | flops 805306368 | bytes 3145728 | tf_op jit(solution)/shard_map/later_blocks/pallas_call | solution.py:297
  17.6 0.1 add_cores.3
  17.7 1.0 %collective-permute-start.5 = (f32[128,256]{1,0:T(8,128)S(1)}, f32[128,256]{1,0:T(8,128)S(1)}, u32[]{:S(2)}, u32[]{:S(2)}) collective-permute-start(f32[128,256]{1,0:T(8,128)S(1)} %get-tuple-element.49), channel_id=1, source_target_pairs={{0,4},{4,0},{8,12},{12,8},{1,5},{5,1},{9,13},{13,9},{2,6},{6,2},{1... | collective-permute-start | bytes 393224 | tf_op jit(solution)/shard_map/ppermute | solution.py:470
  18.6 3.5 %collective-permute-start.6 = (f32[128,256]{1,0:T(8,128)S(1)}, f32[128,256]{1,0:T(8,128)S(1)}, u32[]{:S(2)}, u32[]{:S(2)}) collective-permute-start(f32[128,256]{1,0:T(8,128)S(1)} %get-tuple-element.50), channel_id=1, source_target_pairs={{0,8},{4,12},{8,0},{12,4},{1,9},{5,13},{9,1},{13,5},{2,10},{6,14},... | collective-permute-start | bytes 393224 | tf_op jit(solution)/shard_map/ppermute | solution.py:470
  22.1 0.3 collective-permute-start.7
  22.4 3.8 %collective-permute-done.2.refs_1_ = f32[128,256]{1,0:T(8,128)S(1)} collective-permute-done((f32[128,256]{1,0:T(8,128)S(1)}, f32[128,256]{1,0:T(8,128)S(1)}, u32[]{:S(2)}, u32[]{:S(2)}) %collective-permute-start.2) | collective-permute-done | bytes 131104 | tf_op jit(solution)/shard_map/ppermute | solution.py:470
  26.2 1.5 %collective-permute-start.12 = (f32[128,256]{1,0:T(8,128)S(1)}, f32[128,256]{1,0:T(8,128)S(1)}, u32[]{:S(2)}, u32[]{:S(2)}) collective-permute-start(f32[128,256]{1,0:T(8,128)S(1)} %sum_chips.2.refs_0_), channel_id=1, source_target_pairs={{0,2},{2,0},{1,3},{3,1},{4,6},{6,4},{5,7},{7,5},{8,10},{10,8},{9,1... | collective-permute-start | bytes 393224 | tf_op jit(solution)/shard_map/ppermute | solution.py:470
  27.8 9.6 %collective-permute-done.6.refs_1_ = f32[128,256]{1,0:T(8,128)S(1)} collective-permute-done((f32[128,256]{1,0:T(8,128)S(1)}, f32[128,256]{1,0:T(8,128)S(1)}, u32[]{:S(2)}, u32[]{:S(2)}) %collective-permute-start.6) | collective-permute-done | bytes 131104 | tf_op jit(solution)/shard_map/ppermute | solution.py:470
  37.4 1.5 %collective-permute-start.13 = (f32[128,256]{1,0:T(8,128)S(1)}, f32[128,256]{1,0:T(8,128)S(1)}, u32[]{:S(2)}, u32[]{:S(2)}) collective-permute-start(f32[128,256]{1,0:T(8,128)S(1)} %sum_chips.3.refs_1_), channel_id=1, source_target_pairs={{0,2},{2,0},{1,3},{3,1},{4,6},{6,4},{5,7},{7,5},{8,10},{10,8},{9,1... | collective-permute-start | bytes 393224 | tf_op jit(solution)/shard_map/ppermute | solution.py:470
  39.0 0.1 split_rows.1
  39.1 0.1 collective-permute-start.8
  39.2 3.2 %collective-permute-done.13.refs_3_ = f32[128,256]{1,0:T(8,128)S(1)} collective-permute-done((f32[128,256]{1,0:T(8,128)S(1)}, f32[128,256]{1,0:T(8,128)S(1)}, u32[]{:S(2)}, u32[]{:S(2)}) %collective-permute-start.13) | collective-permute-done | bytes 131104 | tf_op jit(solution)/shard_map/ppermute | solution.py:470
  42.5 1.1 %products.1 = (f32[4,2,2,16,128]{4,3,2,1,0:T(8,128)S(1)}, f32[4,2,2,16,128]{4,3,2,1,0:T(8,128)S(1)}) custom-call(s32[2,2]{1,0:T(2,128)S(1)} %copy-done, f32[128,256]{1,0:T(8,128)S(1)} %sum_chips.2.refs_0_, f32[128,256]{1,0:T(8,128)S(1)} %sum_chips.3.refs_1_, f32[128,256]{1,0:T(8,128)S(1)} %collective-permute-done.12.refs_2_, ...), custom_call_target="tpu_custom_call" | custom-call | flops 33554432 | bytes 1048576 | tf_op jit(solution)/shard_map/products/pallas_call | solution.py:411
  43.6 0.1 collective-permute-start.14
  43.7 2.4 %collective-permute-start.9 = (f32[2,2,2,16,128]{4,3,2,1,0:T(8,128)S(1)}, f32[2,2,2,16,128]{4,3,2,1,0:T(8,128)S(1)}, u32[]{:S(2)}, u32[]{:S(2)}) collective-permute-start(f32[2,2,2,16,128]{4,3,2,1,0:T(8,128)S(1)} %get-tuple-element.55), channel_id=1, source_target_pairs={{0,4},{4,0},{8,12},{12,8},{1,5},{5,1},{9,13},{13,9},{2,6},{6,2},{1... | collective-permute-start | bytes 196616 | tf_op jit(solution)/shard_map/ppermute | solution.py:470
  46.1 1.1 %collective-permute-start.10 = (f32[2,2,2,16,128]{4,3,2,1,0:T(8,128)S(1)}, f32[2,2,2,16,128]{4,3,2,1,0:T(8,128)S(1)}, u32[]{:S(2)}, u32[]{:S(2)}) collective-permute-start(f32[2,2,2,16,128]{4,3,2,1,0:T(8,128)S(1)} %get-tuple-element.56), channel_id=1, source_target_pairs={{0,8},{4,12},{8,0},{12,4},{1,9},{5,13},{9,1},{13,5},{2,10},{6,14},... | collective-permute-start | bytes 196616 | tf_op jit(solution)/shard_map/ppermute | solution.py:470
  47.2 1.4 %collective-permute-start.11 = (f32[2,2,2,16,128]{4,3,2,1,0:T(8,128)S(1)}, f32[2,2,2,16,128]{4,3,2,1,0:T(8,128)S(1)}, u32[]{:S(2)}, u32[]{:S(2)}) collective-permute-start(f32[2,2,2,16,128]{4,3,2,1,0:T(8,128)S(1)} %get-tuple-element.57), channel_id=1, source_target_pairs={{0,12},{4,8},{8,4},{12,0},{1,13},{5,9},{9,5},{13,1},{2,14},{6,10},... | collective-permute-start | bytes 196616 | tf_op jit(solution)/shard_map/ppermute | solution.py:470
  48.6 1.1 %collective-permute-start.15 = (f32[2,2,2,16,128]{4,3,2,1,0:T(8,128)S(1)}, f32[2,2,2,16,128]{4,3,2,1,0:T(8,128)S(1)}, u32[]{:S(2)}, u32[]{:S(2)}) collective-permute-start(f32[2,2,2,16,128]{4,3,2,1,0:T(8,128)S(1)} %get-tuple-element.61), channel_id=1, source_target_pairs={{0,4},{4,0},{8,12},{12,8},{1,5},{5,1},{9,13},{13,9},{2,6},{6,2},{1... | collective-permute-start | bytes 196616 | tf_op jit(solution)/shard_map/ppermute | solution.py:470
  49.7 2.0 %collective-permute-start.16 = (f32[2,2,2,16,128]{4,3,2,1,0:T(8,128)S(1)}, f32[2,2,2,16,128]{4,3,2,1,0:T(8,128)S(1)}, u32[]{:S(2)}, u32[]{:S(2)}) collective-permute-start(f32[2,2,2,16,128]{4,3,2,1,0:T(8,128)S(1)} %get-tuple-element.62), channel_id=1, source_target_pairs={{0,8},{4,12},{8,0},{12,4},{1,9},{5,13},{9,1},{13,5},{2,10},{6,14},... | collective-permute-start | bytes 196616 | tf_op jit(solution)/shard_map/ppermute | solution.py:470
  51.7 1.4 %collective-permute-start.17 = (f32[2,2,2,16,128]{4,3,2,1,0:T(8,128)S(1)}, f32[2,2,2,16,128]{4,3,2,1,0:T(8,128)S(1)}, u32[]{:S(2)}, u32[]{:S(2)}) collective-permute-start(f32[2,2,2,16,128]{4,3,2,1,0:T(8,128)S(1)} %get-tuple-element.63), channel_id=1, source_target_pairs={{0,12},{4,8},{8,4},{12,0},{1,13},{5,9},{9,5},{13,1},{2,14},{6,10},... | collective-permute-start | bytes 196616 | tf_op jit(solution)/shard_map/ppermute | solution.py:470
  53.1 1.4 %collective-permute-done.10.refs_2_ = f32[2,2,2,16,128]{4,3,2,1,0:T(8,128)S(1)} collective-permute-done((f32[2,2,2,16,128]{4,3,2,1,0:T(8,128)S(1)}, f32[2,2,2,16,128]{4,3,2,1,0:T(8,128)S(1)}, u32[]{:S(2)}, u32[]{:S(2)}) %collective-permute-start.10) | collective-permute-done | bytes 65568 | tf_op jit(solution)/shard_map/ppermute | solution.py:470
  54.5 0.7 %join_blocks.2 = f32[2,8,2,16,128]{4,3,2,1,0:T(8,128)} custom-call(f32[2,2,2,16,128]{4,3,2,1,0:T(8,128)S(1)} %get-tuple-element.54.refs_0_, f32[2,2,2,16,128]{4,3,2,1,0:T(8,128)S(1)} %collective-permute-done.9.refs_1_, f32[2,2,2,16,128]{4,3,2,1,0:T(8,128)S(1)} %collective-permute-done.10.refs_2_, f32[2,2,2,16,128]{4,3,2,1,0:T(8,128)S(1)} %collective-permute-done.11.refs_3_), custom_call_target="tpu_custom_call" | custom-call | bytes 524288 | tf_op jit(solution)/shard_map/join_blocks/pallas_call | solution.py:457
  55.2 4.9 %collective-permute-done.16.refs_2_ = f32[2,2,2,16,128]{4,3,2,1,0:T(8,128)S(1)} collective-permute-done((f32[2,2,2,16,128]{4,3,2,1,0:T(8,128)S(1)}, f32[2,2,2,16,128]{4,3,2,1,0:T(8,128)S(1)}, u32[]{:S(2)}, u32[]{:S(2)}) %collective-permute-start.16) | collective-permute-done | bytes 65568 | tf_op jit(solution)/shard_map/ppermute | solution.py:470
  60.1 0.7 %join_blocks.3 = f32[2,8,2,16,128]{4,3,2,1,0:T(8,128)} custom-call(f32[2,2,2,16,128]{4,3,2,1,0:T(8,128)S(1)} %get-tuple-element.60.refs_0_, f32[2,2,2,16,128]{4,3,2,1,0:T(8,128)S(1)} %collective-permute-done.15.refs_1_, f32[2,2,2,16,128]{4,3,2,1,0:T(8,128)S(1)} %collective-permute-done.16.refs_2_, f32[2,2,2,16,128]{4,3,2,1,0:T(8,128)S(1)} %collective-permute-done.17.refs_3_), custom_call_target="tpu_custom_call" | custom-call | bytes 524288 | tf_op jit(solution)/shard_map/join_blocks/pallas_call | solution.py:457
  (20 shorter events, 0.1 us)
Async XLA Ops:
  4.2 2.3 %collective-permute-start = (f32[4,128,256]{2,1,0:T(8,128)S(1)}, f32[4,128,256]{2,1,0:T(8,128)S(1)}, u32[]{:S(2)}, u32[]{:S(2)}) collective-permute-start(f32[4,128,256]{2,1,0:T(8,128)S(1)} %get-tuple-element.35), channel_id=1, source_target_pairs={{0,1},{1,0},{2,3},{3,2},{4,5},{5,4},{6,7},{7,6},{8,9},{9,8},{10,11... | collective-permute-start | bytes 1572872 | tf_op jit(solution)/shard_map/ppermute | solution.py:470
  10.1 7.5 %collective-permute-start.4 = (f32[4,128,256]{2,1,0:T(8,128)S(1)}, f32[4,128,256]{2,1,0:T(8,128)S(1)}, u32[]{:S(2)}, u32[]{:S(2)}) collective-permute-start(f32[4,128,256]{2,1,0:T(8,128)S(1)} %get-tuple-element.47), channel_id=1, source_target_pairs={{0,1},{1,0},{2,3},{3,2},{4,5},{5,4},{6,7},{7,6},{8,9},{9,8},{10,11... | collective-permute-start | bytes 1572872 | tf_op jit(solution)/shard_map/ppermute | solution.py:470
  10.3 11.8 %collective-permute-start.1 = (f32[128,256]{1,0:T(8,128)S(1)}, f32[128,256]{1,0:T(8,128)S(1)}, u32[]{:S(2)}, u32[]{:S(2)}) collective-permute-start(f32[128,256]{1,0:T(8,128)S(1)} %get-tuple-element.41), channel_id=1, source_target_pairs={{0,4},{4,0},{8,12},{12,8},{1,5},{5,1},{9,13},{13,9},{2,6},{6,2},{1... | collective-permute-start | bytes 393224 | tf_op jit(solution)/shard_map/ppermute | solution.py:470
  13.2 12.9 %collective-permute-start.2 = (f32[128,256]{1,0:T(8,128)S(1)}, f32[128,256]{1,0:T(8,128)S(1)}, u32[]{:S(2)}, u32[]{:S(2)}) collective-permute-start(f32[128,256]{1,0:T(8,128)S(1)} %get-tuple-element.42), channel_id=1, source_target_pairs={{0,8},{4,12},{8,0},{12,4},{1,9},{5,13},{9,1},{13,5},{2,10},{6,14},... | collective-permute-start | bytes 393224 | tf_op jit(solution)/shard_map/ppermute | solution.py:470
  15.8 10.4 %collective-permute-start.3 = (f32[128,256]{1,0:T(8,128)S(1)}, f32[128,256]{1,0:T(8,128)S(1)}, u32[]{:S(2)}, u32[]{:S(2)}) collective-permute-start(f32[128,256]{1,0:T(8,128)S(1)} %get-tuple-element.43), channel_id=1, source_target_pairs={{0,12},{4,8},{8,4},{12,0},{1,13},{5,9},{9,5},{13,1},{2,14},{6,10},... | collective-permute-start | bytes 393224 | tf_op jit(solution)/shard_map/ppermute | solution.py:470
  17.6 24.9 %copy-start = (s32[2,2]{1,0:T(2,128)S(1)}, s32[2,2]{1,0:T(2,128)}, u32[]{:S(2)}) copy-start(s32[2,2]{1,0:T(2,128)} %pairs_ref.1) | copy-start | bytes 52
  17.7 10.1 %collective-permute-start.5 = (f32[128,256]{1,0:T(8,128)S(1)}, f32[128,256]{1,0:T(8,128)S(1)}, u32[]{:S(2)}, u32[]{:S(2)}) collective-permute-start(f32[128,256]{1,0:T(8,128)S(1)} %get-tuple-element.49), channel_id=1, source_target_pairs={{0,4},{4,0},{8,12},{12,8},{1,5},{5,1},{9,13},{13,9},{2,6},{6,2},{1... | collective-permute-start | bytes 393224 | tf_op jit(solution)/shard_map/ppermute | solution.py:470
  18.6 18.8 %collective-permute-start.6 = (f32[128,256]{1,0:T(8,128)S(1)}, f32[128,256]{1,0:T(8,128)S(1)}, u32[]{:S(2)}, u32[]{:S(2)}) collective-permute-start(f32[128,256]{1,0:T(8,128)S(1)} %get-tuple-element.50), channel_id=1, source_target_pairs={{0,8},{4,12},{8,0},{12,4},{1,9},{5,13},{9,1},{13,5},{2,10},{6,14},... | collective-permute-start | bytes 393224 | tf_op jit(solution)/shard_map/ppermute | solution.py:470
  22.1 15.3 %collective-permute-start.7 = (f32[128,256]{1,0:T(8,128)S(1)}, f32[128,256]{1,0:T(8,128)S(1)}, u32[]{:S(2)}, u32[]{:S(2)}) collective-permute-start(f32[128,256]{1,0:T(8,128)S(1)} %get-tuple-element.51), channel_id=1, source_target_pairs={{0,12},{4,8},{8,4},{12,0},{1,13},{5,9},{9,5},{13,1},{2,14},{6,10},... | collective-permute-start | bytes 393224 | tf_op jit(solution)/shard_map/ppermute | solution.py:470
  26.2 13.0 %collective-permute-start.12 = (f32[128,256]{1,0:T(8,128)S(1)}, f32[128,256]{1,0:T(8,128)S(1)}, u32[]{:S(2)}, u32[]{:S(2)}) collective-permute-start(f32[128,256]{1,0:T(8,128)S(1)} %sum_chips.2.refs_0_), channel_id=1, source_target_pairs={{0,2},{2,0},{1,3},{3,1},{4,6},{6,4},{5,7},{7,5},{8,10},{10,8},{9,1... | collective-permute-start | bytes 393224 | tf_op jit(solution)/shard_map/ppermute | solution.py:470
  37.4 5.0 %collective-permute-start.13 = (f32[128,256]{1,0:T(8,128)S(1)}, f32[128,256]{1,0:T(8,128)S(1)}, u32[]{:S(2)}, u32[]{:S(2)}) collective-permute-start(f32[128,256]{1,0:T(8,128)S(1)} %sum_chips.3.refs_1_), channel_id=1, source_target_pairs={{0,2},{2,0},{1,3},{3,1},{4,6},{6,4},{5,7},{7,5},{8,10},{10,8},{9,1... | collective-permute-start | bytes 393224 | tf_op jit(solution)/shard_map/ppermute | solution.py:470
  39.1 4.6 %collective-permute-start.8 = (f32[4,2,2,16,128]{4,3,2,1,0:T(8,128)S(1)}, f32[4,2,2,16,128]{4,3,2,1,0:T(8,128)S(1)}, u32[]{:S(2)}, u32[]{:S(2)}) collective-permute-start(f32[4,2,2,16,128]{4,3,2,1,0:T(8,128)S(1)} %get-tuple-element.53), channel_id=1, source_target_pairs={{0,1},{1,0},{2,3},{3,2},{4,5},{5,4},{6,7},{7,6},{8,9},{9,8},{10,11... | collective-permute-start | bytes 393224 | tf_op jit(solution)/shard_map/ppermute | solution.py:470
  43.6 5.0 %collective-permute-start.14 = (f32[4,2,2,16,128]{4,3,2,1,0:T(8,128)S(1)}, f32[4,2,2,16,128]{4,3,2,1,0:T(8,128)S(1)}, u32[]{:S(2)}, u32[]{:S(2)}) collective-permute-start(f32[4,2,2,16,128]{4,3,2,1,0:T(8,128)S(1)} %get-tuple-element.59), channel_id=1, source_target_pairs={{0,1},{1,0},{2,3},{3,2},{4,5},{5,4},{6,7},{7,6},{8,9},{9,8},{10,11... | collective-permute-start | bytes 393224 | tf_op jit(solution)/shard_map/ppermute | solution.py:470
  43.7 7.9 %collective-permute-start.9 = (f32[2,2,2,16,128]{4,3,2,1,0:T(8,128)S(1)}, f32[2,2,2,16,128]{4,3,2,1,0:T(8,128)S(1)}, u32[]{:S(2)}, u32[]{:S(2)}) collective-permute-start(f32[2,2,2,16,128]{4,3,2,1,0:T(8,128)S(1)} %get-tuple-element.55), channel_id=1, source_target_pairs={{0,4},{4,0},{8,12},{12,8},{1,5},{5,1},{9,13},{13,9},{2,6},{6,2},{1... | collective-permute-start | bytes 196616 | tf_op jit(solution)/shard_map/ppermute | solution.py:470
  46.1 8.4 %collective-permute-start.10 = (f32[2,2,2,16,128]{4,3,2,1,0:T(8,128)S(1)}, f32[2,2,2,16,128]{4,3,2,1,0:T(8,128)S(1)}, u32[]{:S(2)}, u32[]{:S(2)}) collective-permute-start(f32[2,2,2,16,128]{4,3,2,1,0:T(8,128)S(1)} %get-tuple-element.56), channel_id=1, source_target_pairs={{0,8},{4,12},{8,0},{12,4},{1,9},{5,13},{9,1},{13,5},{2,10},{6,14},... | collective-permute-start | bytes 196616 | tf_op jit(solution)/shard_map/ppermute | solution.py:470
  47.2 7.3 %collective-permute-start.11 = (f32[2,2,2,16,128]{4,3,2,1,0:T(8,128)S(1)}, f32[2,2,2,16,128]{4,3,2,1,0:T(8,128)S(1)}, u32[]{:S(2)}, u32[]{:S(2)}) collective-permute-start(f32[2,2,2,16,128]{4,3,2,1,0:T(8,128)S(1)} %get-tuple-element.57), channel_id=1, source_target_pairs={{0,12},{4,8},{8,4},{12,0},{1,13},{5,9},{9,5},{13,1},{2,14},{6,10},... | collective-permute-start | bytes 196616 | tf_op jit(solution)/shard_map/ppermute | solution.py:470
  48.6 6.6 %collective-permute-start.15 = (f32[2,2,2,16,128]{4,3,2,1,0:T(8,128)S(1)}, f32[2,2,2,16,128]{4,3,2,1,0:T(8,128)S(1)}, u32[]{:S(2)}, u32[]{:S(2)}) collective-permute-start(f32[2,2,2,16,128]{4,3,2,1,0:T(8,128)S(1)} %get-tuple-element.61), channel_id=1, source_target_pairs={{0,4},{4,0},{8,12},{12,8},{1,5},{5,1},{9,13},{13,9},{2,6},{6,2},{1... | collective-permute-start | bytes 196616 | tf_op jit(solution)/shard_map/ppermute | solution.py:470
  49.7 10.4 %collective-permute-start.16 = (f32[2,2,2,16,128]{4,3,2,1,0:T(8,128)S(1)}, f32[2,2,2,16,128]{4,3,2,1,0:T(8,128)S(1)}, u32[]{:S(2)}, u32[]{:S(2)}) collective-permute-start(f32[2,2,2,16,128]{4,3,2,1,0:T(8,128)S(1)} %get-tuple-element.62), channel_id=1, source_target_pairs={{0,8},{4,12},{8,0},{12,4},{1,9},{5,13},{9,1},{13,5},{2,10},{6,14},... | collective-permute-start | bytes 196616 | tf_op jit(solution)/shard_map/ppermute | solution.py:470
  51.7 8.4 %collective-permute-start.17 = (f32[2,2,2,16,128]{4,3,2,1,0:T(8,128)S(1)}, f32[2,2,2,16,128]{4,3,2,1,0:T(8,128)S(1)}, u32[]{:S(2)}, u32[]{:S(2)}) collective-permute-start(f32[2,2,2,16,128]{4,3,2,1,0:T(8,128)S(1)} %get-tuple-element.63), channel_id=1, source_target_pairs={{0,12},{4,8},{8,4},{12,0},{1,13},{5,9},{9,5},{13,1},{2,14},{6,10},... | collective-permute-start | bytes 196616 | tf_op jit(solution)/shard_map/ppermute | solution.py:470

commit v2 on v1

--- a/solution.py
+++ b/solution.py
@@ -15,6 +15,7 @@
 BF16 = jnp.bfloat16
 VMEM_LIMIT = 16 * 2**20
 SMALL_LIMIT = 4 * 2**20
+LARGE = 10**11
 
 
 def build_gammas():
@@ -223,7 +224,7 @@
 
 def block_cost(slots, nmode, depth):
     return pl.CostEstimate(
-        flops=4 * slots * nmode * nmode * depth,
+        flops=400 * slots * nmode * nmode * depth,
         bytes_accessed=8 * nmode * depth,
         transcendentals=0,
     )
@@ -244,9 +245,9 @@
         functools.partial(first_kernel, order, time, slots, chunks),
         in_specs=[pl.BlockSpec(memory_space=pltpu.HBM)] * 5,
         out_shape=[
-            jax.ShapeDtypeStruct((len(slots), nmode, 2 * nmode), F32),
-            jax.ShapeDtypeStruct((2 * nmode, depth), BF16),
-            jax.ShapeDtypeStruct((fours, comps, 2, nmode, sites), BF16),
+            pltpu.VMEM((len(slots), nmode, 2 * nmode), F32),
+            pltpu.VMEM((2 * nmode, depth), BF16),
+            pltpu.VMEM((fours, comps, 2, nmode, sites), BF16),
         ],
         scratch_shapes=[
             pltpu.VMEM((rows, sites), BF16),
@@ -298,7 +299,7 @@
         functools.partial(later_kernel, order, time, slots),
         in_specs=[pl.BlockSpec(memory_space=pltpu.HBM)] * 2
         + [pl.BlockSpec(memory_space=pltpu.VMEM)] * 2,
-        out_shape=jax.ShapeDtypeStruct((len(slots), nmode, 2 * nmode), F32),
+        out_shape=pltpu.VMEM((len(slots), nmode, 2 * nmode), F32),
         scratch_shapes=[
             pltpu.SMEM(gamma_index.shape, jnp.int32),
             pltpu.VMEM(pattern.shape, jnp.int32),
@@ -311,82 +312,82 @@
     )(gamma_index, pattern, sink_mat, turned)
 
 
-def add_kernel(keep_ref, got_ref, *outs):
-    for slot, out in enumerate(outs):
-        out[...] = keep_ref[slot] + got_ref[slot]
+def small_call(kernel, outs, name, *args, flops=1, after=(), scratch=()):
+    return pl.pallas_call(
+        kernel,
+        in_specs=[pl.BlockSpec(memory_space=pltpu.VMEM)] * len(args)
+        + [pl.BlockSpec(memory_space=pl.ANY)] * len(after),
+        out_shape=outs,
+        scratch_shapes=scratch,
+        compiler_params=pltpu.CompilerParams(vmem_limit_bytes=SMALL_LIMIT),
+        cost_estimate=pl.CostEstimate(flops=flops, bytes_accessed=1, transcendentals=0),
+        name=name,
+    )(*args, *after)
 
 
 def add_units(keep, got):
-    units = keep.shape[0]
-    return pl.pallas_call(
-        add_kernel,
-        out_shape=[jax.ShapeDtypeStruct(keep.shape[1:], F32)] * units,
-        compiler_params=pltpu.CompilerParams(vmem_limit_bytes=SMALL_LIMIT),
-        cost_estimate=pl.CostEstimate(
-            flops=keep.size, bytes_accessed=12 * keep.size, transcendentals=0
-        ),
-        name="add_cores",
-    )(keep, got)
-
-
-def sum_kernel(scale, first_ref, *refs):
-    terms, out = refs[:-1], refs[-1]
-    total = first_ref[...]
-    for term in terms:
-        total = total + term[...]
-    out[...] = total * scale
-
-
-def sum_units(terms, scale):
-    size = terms[0].size
-    return pl.pallas_call(
-        functools.partial(sum_kernel, scale),
-        out_shape=jax.ShapeDtypeStruct(terms[0].shape, F32),
-        cost_estimate=pl.CostEstimate(
-            flops=4 * size, bytes_accessed=20 * size, transcendentals=0
-        ),
-        compiler_params=pltpu.CompilerParams(vmem_limit_bytes=SMALL_LIMIT),
-        name="sum_chips",
-    )(*terms)
-
-
-def write_rows(matrix, lane, spaces, subs, outs, staging):
-    nmode, row_count = matrix.shape[0], outs[0].shape[3]
+    def kernel(keep_ref, got_ref, *outs):
+        for slot, out in enumerate(outs):
+            out[...] = keep_ref[slot] + got_ref[slot]
+
+    units, rows, columns = keep.shape
+    outs = [pltpu.VMEM((rows, columns), F32)] * units
+    return small_call(kernel, outs, "add_cores", keep, got)
+
+
+def sum_units(terms, scale, after=()):
+    def kernel(*refs):
+        total = refs[0][...]
+        for ref in refs[1 : len(terms)]:
+            total = total + ref[...]
+        refs[-1][...] = total * scale
+
+    out = pltpu.VMEM(terms[0].shape, F32)
+    return small_call(kernel, out, "sum_chips", *terms, after=after)
+
+
+def write_rows(whole, lane, spaces, subs, cores, outs):
+    row_count = outs[0].shape[3]
     z, core = lax.axis_index("space"), lax.axis_index("sub")
-    for part in range(2):
-        staging[part] = matrix[:, part * nmode : (part + 1) * nmode].T
-    for c in range(subs):
+    for c, out in zip(cores, outs, strict=True):
         for s in range(spaces):
             start = pl.multiple_of(((z ^ s) * subs + (core ^ c)) * row_count, row_count)
             for part in range(2):
-                outs[c][s, lane, part] = staging[part, pl.ds(start, row_count), :]
-
-
-def split_kernel(spaces, subs, times, *refs):
-    fields, outs, staging = refs[:times], refs[times:-1], refs[-1]
-    for time in range(times):
-        write_rows(fields[time][...], time, spaces, subs, outs, staging.at[time])
-
-
-def split_rows(fields, spaces, subs):
-    nmode, times = fields[0].shape[0], len(fields)
-    groups = spaces * subs
-    shape = (spaces, times, 2, nmode // groups, nmode)
-    return pl.pallas_call(
-        functools.partial(split_kernel, spaces, subs, times),
-        out_shape=[jax.ShapeDtypeStruct(shape, F32)] * subs,
-        scratch_shapes=[pltpu.VMEM((times, 2, nmode, nmode), F32)],
-        cost_estimate=pl.CostEstimate(
-            flops=0, bytes_accessed=16 * times * nmode * nmode, transcendentals=0
-        ),
-        compiler_params=pltpu.CompilerParams(vmem_limit_bytes=SMALL_LIMIT),
-        name="split_rows",
-    )(*fields)
-
-
-def product_kernel(spaces, subs, times, tms, pairs_ref, *refs):
-    fields, outs, (held, staging) = refs[: times * tms], refs[times * tms : -2], refs[-2:]
+                out[s, lane, part] = whole[part, pl.ds(start, row_count), :]
+
+
+def turn(matrix, whole):
+    nmode = matrix.shape[1] // 2
+    for part in range(2):
+        whole[part] = matrix[:, part * nmode : (part + 1) * nmode].T
+
+
+def turn_field(field, after):
+    def kernel(field_ref, *refs):
+        turn(field_ref[...], refs[-1])
+
+    nmode = field.shape[0]
+    out = pltpu.VMEM((2, nmode, nmode), F32)
+    return small_call(kernel, out, "turn_field", field, flops=LARGE, after=after)
+
+
+def split_rows(whole, field, spaces, subs):
+    nmode = whole.shape[1]
+
+    def kernel(whole_ref, field_ref, away, keep, staging):
+        turn(field_ref[...], staging)
+        for lane, source in enumerate((whole_ref, staging)):
+            write_rows(source, lane, spaces, subs, [1, 0], [away, keep])
+
+    outs = [pltpu.VMEM((spaces, 2, 2, nmode // (spaces * subs), nmode), F32)] * 2
+    scratch = [pltpu.VMEM((2, nmode, nmode), F32)]
+    return small_call(kernel, outs, "split_rows", whole, field, scratch=scratch)
+
+
+def product_kernel(spaces, subs, tms, pairs_ref, *refs):
+    fields, (away, whole, held) = refs[:-3], refs[-3:]
     nmode = fields[0].shape[0]
+    times = len(fields) // tms
     mine = lax.axis_index("tm")
     for other in range(tms):
         for time in range(times):
@@ -401,89 +402,109 @@
             preferred_element_type=F32,
             precision=lax.Precision.HIGHEST,
         ) * (1.0 / math.sqrt(nmode))
-        write_rows(result, pair, spaces, subs, outs, staging.at[pair])
+        turn(result, whole.at[pair])
+        write_rows(whole.at[pair], pair, spaces, subs, [1], [away])
 
 
 def product_rows(time_pairs, fields, spaces, subs, tms):
-    nmode, times, pairs = fields[0].shape[0], len(fields) // tms, time_pairs.shape[0]
-    groups = spaces * subs
-    shape = (spaces, pairs, 2, nmode // groups, nmode)
+    nmode, pairs = fields[0].shape[0], time_pairs.shape[0]
+    shape = (spaces, pairs, 2, nmode // (spaces * subs), nmode)
     return pl.pallas_call(
-        functools.partial(product_kernel, spaces, subs, times, tms),
+        functools.partial(product_kernel, spaces, subs, tms),
         in_specs=[pl.BlockSpec(memory_space=pltpu.SMEM)]
         + [pl.BlockSpec(memory_space=pltpu.VMEM)] * len(fields),
-        out_shape=[jax.ShapeDtypeStruct(shape, F32)] * subs,
-        scratch_shapes=[
-            pltpu.VMEM((times * tms, nmode, 2 * nmode), F32),
-            pltpu.VMEM((pairs, 2, nmode, nmode), F32),
-        ],
+        out_shape=[pltpu.VMEM(shape, F32), pltpu.VMEM((pairs, 2, nmode, nmode), F32)],
+        scratch_shapes=[pltpu.VMEM((len(fields), nmode, 2 * nmode), F32)],
         compiler_params=pltpu.CompilerParams(vmem_limit_bytes=SMALL_LIMIT),
         cost_estimate=pl.CostEstimate(
-            flops=8 * pairs * nmode**3, bytes_accessed=32 * nmode * nmode * times, transcendentals=0
+            flops=8 * pairs * nmode**3, bytes_accessed=64 * nmode * nmode, transcendentals=0
         ),
         name="products",
     )(time_pairs, *fields)
 
 
-def pair_kernel(keep_ref, got_ref, *outs):
-    for s, out in enumerate(outs):
-        out[0] = keep_ref[s]
-        out[1] = got_ref[s]
+def keep_rows(whole, spaces, subs):
+    lanes, _, nmode, _ = whole.shape
+
+    def kernel(whole_ref, out):
+        for lane in range(lanes):
+            write_rows(whole_ref.at[lane], lane, spaces, subs, [0], [out])
+
+    out = pltpu.VMEM((spaces, lanes, 2, nmode // (spaces * subs), nmode), F32)
+    return small_call(kernel, out, "keep_rows", whole, flops=LARGE)
 
 
 def pair_cores(keep, got):
     shape = keep.shape
+
+    def kernel(keep_ref, got_ref, *outs):
+        for s, out in enumerate(outs):
+            out[0] = keep_ref[s]
+            out[1] = got_ref[s]
+
+    outs = [pltpu.VMEM((2,) + shape[1:], F32)] * shape[0]
+    return small_call(kernel, outs, "pair_cores", keep, got)
+
+
+def pair_with(near, keep, got):
+    shape = keep.shape
+
+    def kernel(near_ref, keep_ref, got_ref, *outs):
+        outs[1][0] = near_ref[...]
+        for s, out in enumerate(outs):
+            out = out.at[1] if s == 1 else out
+            out[0] = keep_ref[s]
+            out[1] = got_ref[s]
+
+    outs = [
+        pltpu.VMEM(((2,) if s == 1 else ()) + (2,) + shape[1:], F32) for s in range(shape[0])
+    ]
+    return small_call(kernel, outs, "pair_cores", near, keep, got)
+
+
+def put_blocks(args, places, arrays, spaces, subs, name, flops):
+    lanes, _, row_count, nmode = args[0].shape[-4:]
+    count = len(arrays)
+
+    def kernel(*refs):
+        outs, sems = refs[-1 - count : -1], refs[-1]
+        refs = refs[len(given) :]
+        z, core = lax.axis_index("space"), lax.axis_index("sub")
+        copies = []
+        for out, group in zip(outs, places, strict=True):
+            for s, operand, index in group:
+                block = refs[operand] if index is None else refs[operand].at[index]
+                for c in range(subs):
+                    for lane in range(lanes):
+                        copy = pltpu.make_async_copy(
+                            block.at[c, lane],
+                            out.at[lane, (z ^ s) * subs + (core ^ c)],
+                            sems.at[len(copies)],
+                        )
+                        copy.start()
+                        copies.append(copy)
+        for copy in copies:
+            copy.wait()
+
+    out = jax.ShapeDtypeStruct((lanes, spaces * subs, 2, row_count, nmode), F32)
+    given = [(k, array) for k, array in enumerate(arrays) if array is not None]
     return pl.pallas_call(
-        pair_kernel,
-        out_shape=[jax.ShapeDtypeStruct((2,) + shape[1:], F32)] * shape[0],
+        kernel,
+        in_specs=[pl.BlockSpec(memory_space=pltpu.HBM)] * len(given)
+        + [pl.BlockSpec(memory_space=pltpu.VMEM)] * len(args),
+        out_specs=[pl.BlockSpec(memory_space=pltpu.HBM)] * count,
+        out_shape=[out] * count,
+        input_output_aliases={n: k for n, (k, _) in enumerate(given)},
+        scratch_shapes=[pltpu.SemaphoreType.DMA((sum(map(len, places)) * subs * lanes,))],
         compiler_params=pltpu.CompilerParams(vmem_limit_bytes=SMALL_LIMIT),
-        cost_estimate=pl.CostEstimate(
-            flops=0, bytes_accessed=16 * keep.size, transcendentals=0
-        ),
-        name="pair_cores",
-    )(keep, got)
-
-
-def join_kernel(spaces, subs, *refs):
-    blocks, out = refs[:-1], refs[-1]
-    z, core = lax.axis_index("space"), lax.axis_index("sub")
-    for s in range(spaces):
-        for c in range(subs):
-            out[:, (z ^ s) * subs + (core ^ c)] = blocks[s][c]
-
-
-def join_blocks(blocks, spaces, subs):
-    shape = blocks[0].shape
-    return pl.pallas_call(
-        functools.partial(join_kernel, spaces, subs),
-        out_shape=jax.ShapeDtypeStruct((shape[1], spaces * subs) + shape[2:], F32),
-        compiler_params=pltpu.CompilerParams(vmem_limit_bytes=SMALL_LIMIT),
-        cost_estimate=pl.CostEstimate(
-            flops=0, bytes_accessed=8 * len(blocks) * blocks[0].size, transcendentals=0
-        ),
-        name="join_blocks",
-    )(*blocks)
+        cost_estimate=pl.CostEstimate(flops=flops, bytes_accessed=1, transcendentals=0),
+        name=name,
+    )(*(array for _, array in given), *args)
 
 
 def swap(value, axis, distance):
     size = lax.axis_size(axis)
     return lax.ppermute(value, axis, [(i, i ^ distance) for i in range(size)])
-
-
-def chip_order(spaces):
-    return sorted(range(1, spaces), key=lambda s: (s & (s - 1) != 0, s == 1, -s))
-
-
-def swap_chips(parts, spaces):
-    got = list(parts)
-    for s in chip_order(spaces):
-        got[s] = swap(parts[s], "space", s)
-    return got
-
-
-def spread(keep, away, spaces, subs):
-    parts = pair_cores(keep, swap(away, "sub", 1))
-    return join_blocks(swap_chips(parts, spaces), spaces, subs)
 
 
 def own_insertions(spaces, subs):
@@ -495,25 +516,46 @@
     spaces, subs, tms = (lax.axis_size(name) for name in ("space", "sub", "tm"))
     order = functools.partial(own_insertions, spaces, subs)
     mine, other = list(range(spaces)), list(range(spaces, 2 * spaces))
-    fields, others = [], []
-    sums = []
-    for time in range(times):
-        if sums:
-            gamma_index, sums[-1] = lax.optimization_barrier((gamma_index, sums[-1]))
+
+    def blocks(gamma_index, time):
         away, *laid = first_blocks(
             sink, source, gamma_index, momenta, pattern, time, nmode, order, other
         )
         got = swap(away, "sub", 1)
-        keep = later_blocks(gamma_index, pattern, *laid, time, order, mine)
-        sums.append(add_units(keep, got))
-    for parts in sums:
-        fields.append(sum_units(swap_chips(parts, spaces), scale))
-        others.append(swap(fields[-1], "tm", 1))
-    keep, away = split_rows(fields, spaces, subs)
-    meson = spread(keep, away, spaces, subs)
-    keep, away = product_rows(time_pairs, fields + others, spaces, subs, tms)
-    products = spread(keep, away, spaces, subs)
-    return meson, products
+        return later_blocks(gamma_index, pattern, *laid, time, order, mine), got
+
+    def send(own, one, two, three):
+        two, three, one = (swap(v, "space", s) for v, s in ((two, 2), (three, 3), (one, 1)))
+        return own, one, two, three
+
+    parts = add_units(*blocks(gamma_index, 0))
+    gamma_index, parts = lax.optimization_barrier((gamma_index, parts))
+    first = send(*parts)
+    second = send(*add_units(*blocks(gamma_index, 1)))
+    first = sum_units(first, scale)
+    first_other = swap(first, "tm", 1)
+    whole = turn_field(first, second[1:])
+    second = sum_units(second, scale, [first_other, whole])
+    second_other = swap(second, "tm", 1)
+
+    away, keep = split_rows(whole, second, spaces, subs)
+    meson = pair_cores(keep, swap(away, "sub", 1))
+    own, meson_near, two, three = meson
+    two, three = swap(two, "space", 2), swap(three, "space", 3)
+    fields = [first, second, first_other, second_other]
+    away, whole = product_rows(time_pairs, fields, spaces, subs, tms)
+    got = swap(away, "sub", 1)
+    products = pair_with(meson_near, keep_rows(whole, spaces, subs), got)
+    places = [[(0, 0, None), (2, 1, None), (3, 2, None)]]
+    (meson,) = put_blocks(
+        [own, two, three], places, [None], spaces, subs, "put_early", LARGE
+    )
+    own, near, two, three = products
+    two, three, near = (swap(v, "space", s) for v, s in ((two, 2), (three, 3), (near, 1)))
+    places = [[(1, 1, 0)], [(0, 0, None), (1, 1, 1), (2, 2, None), (3, 3, None)]]
+    return put_blocks(
+        [own, near, two, three], places, [meson, None], spaces, subs, "put_late", 1
+    )
 
 
 def by_rows(sink, source, gamma_index, momenta, pattern, time_pairs, nmode, times, scale):
@@ -558,10 +600,9 @@
         return modes.transpose(0, 1, 3, 2, 4).reshape(times, nmode * comps * 2, sites)
 
     owners = (
-        spaces * subs == gamma_index.shape[0]
-        and spaces & (spaces - 1) == 0
-        and subs == 2
-        and tms == 2
+        (spaces, subs, tms, times) == (4, 2, 2, 2)
+        and gamma_index.shape[0] == spaces * subs
+        and time_pairs.shape[0] == times
     )
     plan = by_owner if owners else by_rows
     arrays = (as_rows(sink_modes), as_rows(source_modes), gamma_index, momenta.T, pattern)

time: 61 us -> 57.1 us (0.936)
  waiting for transfers between devices: 23 us -> 16.2 us
  Pallas kernels: 13.5 us -> 15.5 us
  starting transfers between devices: 23.5 us -> 24.4 us
    ppermute x18 -> x17, waiting for transfers between devices: 23 us -> 16.2 us  [swap(): return lax.ppermute(value, axis, [(i, i ^ distance) for i in range(size)])]
    pallas_call x10 -> x12, Pallas kernels: 2.92 us -> 4.96 us  [the longest x9 2.18 us: small_call(): pl.pallas_call(kernel, in_specs=[pl.BlockSpec(memory_space=pltpu.VMEM)] *...]
    ppermute x18 -> x17, starting transfers between devices: 23.5 us -> 24.4 us  [swap(): return lax.ppermute(value, axis, [(i, i ^ distance) for i in range(size)])]
  transfers between devices with their start and end apart: 18 -> 17, of which waited for: 5 -> 7; matrix products, arithmetic and copies ran while one was open for 0% -> 0% of each run, Pallas kernels for 9% -> 18%
where the time goes in v2:
time: 57.1 us; the launch traced here: 56.9 us
  starting transfers between devices  24.4 us (43%)
  waiting for transfers between devices  16.2 us (28%)
  Pallas kernels  15.5 us (27%)
  between operations  0.78 us (1%)
    ppermute x17, starting transfers between devices, swap(): return lax.ppermute(value, axis, [(i, i ^ distance) for i in range(size)])  24.4 us
    ppermute x17, waiting for transfers between devices, swap(): return lax.ppermute(value, axis, [(i, i ^ distance) for i in range(size)])  16.2 us
    pallas_call x2, Pallas kernels, first_blocks(): pl.pallas_call(functools.partial(first_kernel, order, time, slots, chunks...  7.09 us
    pallas_call x2, Pallas kernels, later_blocks(): pl.pallas_call(functools.partial(later_kernel, order, time, slots), in_sp...  3.48 us
    pallas_call x9, Pallas kernels, small_call(): pl.pallas_call(kernel, in_specs=[pl.BlockSpec(memory_space=pltpu.VMEM)] *...  2.18 us
    pallas_call x2, Pallas kernels, put_blocks(): pl.pallas_call(kernel, in_specs=[pl.BlockSpec(memory_space=pltpu.HBM)] *...  1.65 us
  transfers between devices with their start and end apart: 17, of which 7 were waited for; matrix products, arithmetic and copies ran while one was open for 0% of the time, Pallas kernels for 18%

profile of v2, /device:TPU:0, one launch (start us, length us, event | category | flops | bytes accessed | tf_op | source)
XLA Modules:
  0.0 56.9 jit_solution(1532661872953759306)
XLA Ops:
  0.6 3.5 %first_blocks.2 = (f32[4,128,256]{2,1,0:T(8,128)S(1)}, bf16[256,3072]{1,0:T(8,128)(2,1)S(1)}, bf16[2,12,2,128,128]{4,3,2,1,0:T(8,128)(2,1)S(1)}) custom-call(bf16[2,3072,128]{2,1,0:T(8,128)(2,1)} %bitcast.7, bf16[2,3072,128]{2,1,0:T(8,128)(2,1)} %bitcast.9, s32[8]{0:T(128)} %gamma_hbm.5, s32[3,8]{1,0:T(4,128)} %bitcast.11, s32[2,128]{1,0:T(2,128)} %pattern_hbm.7), custom_call_target="tpu_custom_call" | custom-call | flops 80530636800 | bytes 3145728 | tf_op jit(solution)/shard_map/first_blocks/pallas_call | solution.py:244
  4.2 0.5 collective-permute-start
  4.7 1.7 %later_blocks.2.keep_ref = f32[4,128,256]{2,1,0:T(8,128)S(1)} custom-call(s32[8]{0:T(128)} %gamma_hbm.5, s32[2,128]{1,0:T(2,128)} %pattern_hbm.7, bf16[256,3072]{1,0:T(8,128)(2,1)S(1)} %get-tuple-element.33.sink_mat, bf16[2,12,2,128,128]{4,3,2,1,0:T(8,128)(2,1)S(1)} %get-tuple-element.34.turned), custom_call_target="tpu_custom_call" | custom-call | flops 80530636800 | bytes 3145728 | tf_op jit(solution)/shard_map/later_blocks/pallas_call | solution.py:298
  6.5 0.8 %add_cores.2 = (f32[128,256]{1,0:T(8,128)S(1)}, f32[128,256]{1,0:T(8,128)}, f32[128,256]{1,0:T(8,128)}, f32[128,256]{1,0:T(8,128)}) custom-call(f32[4,128,256]{2,1,0:T(8,128)S(1)} %later_blocks.2.keep_ref, f32[4,128,256]{2,1,0:T(8,128)S(1)} %collective-permute-done.got_ref), custom_call_target="tpu_custom_call" | custom-call | flops 1 | bytes 1 | tf_op jit(solution)/shard_map/add_cores/pallas_call | solution.py:316
  7.2 2.7 %collective-permute-start.1 = (f32[128,256]{1,0:T(8,128)}, f32[128,256]{1,0:T(8,128)}, u32[]{:S(2)}, u32[]{:S(2)}) collective-permute-start(f32[128,256]{1,0:T(8,128)} %get-tuple-element.41), channel_id=1, source_target_pairs={{0,4},{4,0},{8,12},{12,8},{1,5},{5,1},{9,13},{13,9},{2,6},{6,2},{1... | collective-permute-start | bytes 393224 | tf_op jit(solution)/shard_map/ppermute | solution.py:507
  10.0 2.6 %collective-permute-start.2 = (f32[128,256]{1,0:T(8,128)}, f32[128,256]{1,0:T(8,128)}, u32[]{:S(2)}, u32[]{:S(2)}) collective-permute-start(f32[128,256]{1,0:T(8,128)} %get-tuple-element.42), channel_id=1, source_target_pairs={{0,8},{4,12},{8,0},{12,4},{1,9},{5,13},{9,1},{13,5},{2,10},{6,14},... | collective-permute-start | bytes 393224 | tf_op jit(solution)/shard_map/ppermute | solution.py:507
  12.6 3.5 %first_blocks.3 = (f32[4,128,256]{2,1,0:T(8,128)S(1)}, bf16[256,3072]{1,0:T(8,128)(2,1)S(1)}, bf16[2,12,2,128,128]{4,3,2,1,0:T(8,128)(2,1)S(1)}) custom-call(bf16[2,3072,128]{2,1,0:T(8,128)(2,1)} %bitcast.8, bf16[2,3072,128]{2,1,0:T(8,128)(2,1)} %bitcast.10, s32[8]{0:T(128)} %gamma_hbm.5, s32[3,8]{1,0:T(4,128)} %bitcast.12, s32[2,128]{1,0:T(2,128)} %pattern_hbm.7), custom_call_target="tpu_custom_call" | custom-call | flops 80530636800 | bytes 3145728 | tf_op jit(solution)/shard_map/first_blocks/pallas_call | solution.py:244
  16.2 1.7 %later_blocks.3.keep_ref = f32[4,128,256]{2,1,0:T(8,128)S(1)} custom-call(s32[8]{0:T(128)} %gamma_hbm.5, s32[2,128]{1,0:T(2,128)} %pattern_hbm.7, bf16[256,3072]{1,0:T(8,128)(2,1)S(1)} %get-tuple-element.45.sink_mat, bf16[2,12,2,128,128]{4,3,2,1,0:T(8,128)(2,1)S(1)} %get-tuple-element.46.turned), custom_call_target="tpu_custom_call" | custom-call | flops 80530636800 | bytes 3145728 | tf_op jit(solution)/shard_map/later_blocks/pallas_call | solution.py:298
  17.9 0.1 collective-permute-done.4.got_ref
  18.1 1.0 %collective-permute-start.5 = (f32[128,256]{1,0:T(8,128)S(1)}, f32[128,256]{1,0:T(8,128)S(1)}, u32[]{:S(2)}, u32[]{:S(2)}) collective-permute-start(f32[128,256]{1,0:T(8,128)S(1)} %get-tuple-element.48), channel_id=1, source_target_pairs={{0,4},{4,0},{8,12},{12,8},{1,5},{5,1},{9,13},{13,9},{2,6},{6,2},{1... | collective-permute-start | bytes 393224 | tf_op jit(solution)/shard_map/ppermute | solution.py:507
  19.1 3.5 %collective-permute-start.6 = (f32[128,256]{1,0:T(8,128)S(1)}, f32[128,256]{1,0:T(8,128)S(1)}, u32[]{:S(2)}, u32[]{:S(2)}) collective-permute-start(f32[128,256]{1,0:T(8,128)S(1)} %get-tuple-element.49), channel_id=1, source_target_pairs={{0,8},{4,12},{8,0},{12,4},{1,9},{5,13},{9,1},{13,5},{2,10},{6,14},... | collective-permute-start | bytes 393224 | tf_op jit(solution)/shard_map/ppermute | solution.py:507
  22.6 0.6 %collective-permute-done.2.refs_2_ = f32[128,256]{1,0:T(8,128)} collective-permute-done((f32[128,256]{1,0:T(8,128)}, f32[128,256]{1,0:T(8,128)}, u32[]{:S(2)}, u32[]{:S(2)}) %collective-permute-start.2) | collective-permute-done | bytes 131104 | tf_op jit(solution)/shard_map/ppermute | solution.py:507
  23.2 1.1 %sum_chips.2.field_ref.refs_0_ = f32[128,256]{1,0:T(8,128)S(1)} custom-call(f32[128,256]{1,0:T(8,128)S(1)} %get-tuple-element.40.refs_0_, f32[128,256]{1,0:T(8,128)} %collective-permute-done.1.refs_1_, f32[128,256]{1,0:T(8,128)} %collective-permute-done.2.refs_2_, f32[128,256]{1,0:T(8,128)} %collective-permute-done.3.refs_3_), custom_call_target="tpu_custom_call" | custom-call | flops 1 | bytes 1 | tf_op jit(solution)/shard_map/sum_chips/pallas_call | solution.py:316
  24.3 1.6 %collective-permute-start.8 = (f32[128,256]{1,0:T(8,128)S(1)}, f32[128,256]{1,0:T(8,128)S(1)}, u32[]{:S(2)}, u32[]{:S(2)}) collective-permute-start(f32[128,256]{1,0:T(8,128)S(1)} %sum_chips.2.field_ref.refs_0_), channel_id=1, source_target_pairs={{0,2},{2,0},{1,3},{3,1},{4,6},{6,4},{5,7},{7,5},{8,10},{10,8},{9,1... | collective-permute-start | bytes 393224 | tf_op jit(solution)/shard_map/ppermute | solution.py:507
  25.8 0.6 %collective-permute-done.5.refs_0_.refs_1_ = f32[128,256]{1,0:T(8,128)S(1)} collective-permute-done((f32[128,256]{1,0:T(8,128)S(1)}, f32[128,256]{1,0:T(8,128)S(1)}, u32[]{:S(2)}, u32[]{:S(2)}) %collective-permute-start.5) | collective-permute-done | bytes 131104 | tf_op jit(solution)/shard_map/ppermute | solution.py:507
  26.5 7.9 %collective-permute-done.6.refs_1_.refs_2_ = f32[128,256]{1,0:T(8,128)S(1)} collective-permute-done((f32[128,256]{1,0:T(8,128)S(1)}, f32[128,256]{1,0:T(8,128)S(1)}, u32[]{:S(2)}, u32[]{:S(2)}) %collective-permute-start.6) | collective-permute-done | bytes 131104 | tf_op jit(solution)/shard_map/ppermute | solution.py:507
  34.3 0.1 turn_field.1.refs_5_.whole_ref
  34.5 0.1 split_rows.1
  34.6 0.1 collective-permute-start.9
  34.7 1.6 %collective-permute-start.12 = (f32[128,256]{1,0:T(8,128)S(1)}, f32[128,256]{1,0:T(8,128)S(1)}, u32[]{:S(2)}, u32[]{:S(2)}) collective-permute-start(f32[128,256]{1,0:T(8,128)S(1)} %sum_chips.3.field_ref.refs_1_), channel_id=1, source_target_pairs={{0,2},{2,0},{1,3},{3,1},{4,6},{6,4},{5,7},{7,5},{8,10},{10,8},{9,1... | collective-permute-start | bytes 393224 | tf_op jit(solution)/shard_map/ppermute | solution.py:507
  36.3 4.9 %collective-permute-start.10 = (f32[2,2,2,16,128]{4,3,2,1,0:T(8,128)S(1)}, f32[2,2,2,16,128]{4,3,2,1,0:T(8,128)S(1)}, u32[]{:S(2)}, u32[]{:S(2)}) collective-permute-start(f32[2,2,2,16,128]{4,3,2,1,0:T(8,128)S(1)} %get-tuple-element.55), channel_id=1, source_target_pairs={{0,8},{4,12},{8,0},{12,4},{1,9},{5,13},{9,1},{13,5},{2,10},{6,14},... | collective-permute-start | bytes 196616 | tf_op jit(solution)/shard_map/ppermute | solution.py:507
  41.2 0.4 collective-permute-start.11
  41.6 1.1 %products.1 = (f32[4,2,2,16,128]{4,3,2,1,0:T(8,128)S(1)}, f32[2,2,128,128]{3,2,1,0:T(8,128)S(1)}) custom-call(s32[2,2]{1,0:T(2,128)S(1)} %copy-done, f32[128,256]{1,0:T(8,128)S(1)} %sum_chips.2.field_ref.refs_0_, f32[128,256]{1,0:T(8,128)S(1)} %sum_chips.3.field_ref.refs_1_, f32[128,256]{1,0:T(8,128)S(1)} %collective-permute-done.8.refs_4_.refs_2_, ...), custom_call_target="tpu_custom_call" | custom-call | flops 33554432 | bytes 1048576 | tf_op jit(solution)/shard_map/products/pallas_call | solution.py:412
  42.8 0.1 collective-permute-start.13
  42.9 1.3 %collective-permute-done.13.got_ref = f32[4,2,2,16,128]{4,3,2,1,0:T(8,128)S(1)} collective-permute-done((f32[4,2,2,16,128]{4,3,2,1,0:T(8,128)S(1)}, f32[4,2,2,16,128]{4,3,2,1,0:T(8,128)S(1)}, u32[]{:S(2)}, u32[]{:S(2)}) %collective-permute-start.13) | collective-permute-done | bytes 131104 | tf_op jit(solution)/shard_map/ppermute | solution.py:507
  44.2 2.0 %collective-permute-start.14 = (f32[2,2,2,2,16,128]{5,4,3,2,1,0:T(8,128)S(1)}, f32[2,2,2,2,16,128]{5,4,3,2,1,0:T(8,128)S(1)}, u32[]{:S(2)}, u32[]{:S(2)}) collective-permute-start(f32[2,2,2,2,16,128]{5,4,3,2,1,0:T(8,128)S(1)} %get-tuple-element.61), channel_id=1, source_target_pairs={{0,4},{4,0},{8,12},{12,8},{1,5},{5,1},{9,13},{13,9},{2,6},{6,2},{1... | collective-permute-start | bytes 393224 | tf_op jit(solution)/shard_map/ppermute | solution.py:507
  46.2 2.0 %collective-permute-start.15 = (f32[2,2,2,16,128]{4,3,2,1,0:T(8,128)S(1)}, f32[2,2,2,16,128]{4,3,2,1,0:T(8,128)S(1)}, u32[]{:S(2)}, u32[]{:S(2)}) collective-permute-start(f32[2,2,2,16,128]{4,3,2,1,0:T(8,128)S(1)} %get-tuple-element.62), channel_id=1, source_target_pairs={{0,8},{4,12},{8,0},{12,4},{1,9},{5,13},{9,1},{13,5},{2,10},{6,14},... | collective-permute-start | bytes 196616 | tf_op jit(solution)/shard_map/ppermute | solution.py:507
  48.2 1.3 %collective-permute-start.16 = (f32[2,2,2,16,128]{4,3,2,1,0:T(8,128)S(1)}, f32[2,2,2,16,128]{4,3,2,1,0:T(8,128)S(1)}, u32[]{:S(2)}, u32[]{:S(2)}) collective-permute-start(f32[2,2,2,16,128]{4,3,2,1,0:T(8,128)S(1)} %get-tuple-element.63), channel_id=1, source_target_pairs={{0,12},{4,8},{8,4},{12,0},{1,13},{5,9},{9,5},{13,1},{2,14},{6,10},... | collective-permute-start | bytes 196616 | tf_op jit(solution)/shard_map/ppermute | solution.py:507
  49.6 0.8 %put_early.1.refs_0_ = f32[2,8,2,16,128]{4,3,2,1,0:T(8,128)} custom-call(f32[2,2,2,16,128]{4,3,2,1,0:T(8,128)S(1)} %get-tuple-element.54.refs_0_, f32[2,2,2,16,128]{4,3,2,1,0:T(8,128)S(1)} %collective-permute-done.10.refs_1_, f32[2,2,2,16,128]{4,3,2,1,0:T(8,128)S(1)} %collective-permute-done.11.refs_2_), custom_call_target="tpu_custom_call" | custom-call | flops 99999997952 | bytes 1 | tf_op jit(solution)/shard_map/put_early/pallas_call | solution.py:491
  50.3 1.1 %collective-permute-done.15.refs_3_ = f32[2,2,2,16,128]{4,3,2,1,0:T(8,128)S(1)} collective-permute-done((f32[2,2,2,16,128]{4,3,2,1,0:T(8,128)S(1)}, f32[2,2,2,16,128]{4,3,2,1,0:T(8,128)S(1)}, u32[]{:S(2)}, u32[]{:S(2)}) %collective-permute-start.15) | collective-permute-done | bytes 65568 | tf_op jit(solution)/shard_map/ppermute | solution.py:507
  51.4 4.6 %collective-permute-done.16.refs_4_ = f32[2,2,2,16,128]{4,3,2,1,0:T(8,128)S(1)} collective-permute-done((f32[2,2,2,16,128]{4,3,2,1,0:T(8,128)S(1)}, f32[2,2,2,16,128]{4,3,2,1,0:T(8,128)S(1)}, u32[]{:S(2)}, u32[]{:S(2)}) %collective-permute-start.16) | collective-permute-done | bytes 65568 | tf_op jit(solution)/shard_map/ppermute | solution.py:507
  56.0 0.9 %put_late.1 = (f32[2,8,2,16,128]{4,3,2,1,0:T(8,128)}, f32[2,8,2,16,128]{4,3,2,1,0:T(8,128)}) custom-call(f32[2,8,2,16,128]{4,3,2,1,0:T(8,128)} %put_early.1.refs_0_, f32[2,2,2,16,128]{4,3,2,1,0:T(8,128)S(1)} %get-tuple-element.60.refs_1_, f32[2,2,2,2,16,128]{5,4,3,2,1,0:T(8,128)S(1)} %collective-permute-done.14.refs_2_, ...), custom_call_target="tpu_custom_call", output_to_operand_aliasing={{0}: (0, {})} | custom-call | flops 1 | bytes 1 | tf_op jit(solution)/shard_map/put_late/pallas_call | solution.py:491
  (20 shorter events, 0.3 us)
Async XLA Ops:
  4.2 2.3 %collective-permute-start = (f32[4,128,256]{2,1,0:T(8,128)S(1)}, f32[4,128,256]{2,1,0:T(8,128)S(1)}, u32[]{:S(2)}, u32[]{:S(2)}) collective-permute-start(f32[4,128,256]{2,1,0:T(8,128)S(1)} %get-tuple-element.35), channel_id=1, source_target_pairs={{0,1},{1,0},{2,3},{3,2},{4,5},{5,4},{6,7},{7,6},{8,9},{9,8},{10,11... | collective-permute-start | bytes 1572872 | tf_op jit(solution)/shard_map/ppermute | solution.py:507
  7.2 15.4 %collective-permute-start.1 = (f32[128,256]{1,0:T(8,128)}, f32[128,256]{1,0:T(8,128)}, u32[]{:S(2)}, u32[]{:S(2)}) collective-permute-start(f32[128,256]{1,0:T(8,128)} %get-tuple-element.41), channel_id=1, source_target_pairs={{0,4},{4,0},{8,12},{12,8},{1,5},{5,1},{9,13},{13,9},{2,6},{6,2},{1... | collective-permute-start | bytes 393224 | tf_op jit(solution)/shard_map/ppermute | solution.py:507
  10.0 13.2 %collective-permute-start.2 = (f32[128,256]{1,0:T(8,128)}, f32[128,256]{1,0:T(8,128)}, u32[]{:S(2)}, u32[]{:S(2)}) collective-permute-start(f32[128,256]{1,0:T(8,128)} %get-tuple-element.42), channel_id=1, source_target_pairs={{0,8},{4,12},{8,0},{12,4},{1,9},{5,13},{9,1},{13,5},{2,10},{6,14},... | collective-permute-start | bytes 393224 | tf_op jit(solution)/shard_map/ppermute | solution.py:507
  12.6 10.6 %collective-permute-start.3 = (f32[128,256]{1,0:T(8,128)}, f32[128,256]{1,0:T(8,128)}, u32[]{:S(2)}, u32[]{:S(2)}) collective-permute-start(f32[128,256]{1,0:T(8,128)} %get-tuple-element.43), channel_id=1, source_target_pairs={{0,12},{4,8},{8,4},{12,0},{1,13},{5,9},{9,5},{13,1},{2,14},{6,10},... | collective-permute-start | bytes 393224 | tf_op jit(solution)/shard_map/ppermute | solution.py:507
  16.1 2.0 %collective-permute-start.4 = (f32[4,128,256]{2,1,0:T(8,128)S(1)}, f32[4,128,256]{2,1,0:T(8,128)S(1)}, u32[]{:S(2)}, u32[]{:S(2)}) collective-permute-start(f32[4,128,256]{2,1,0:T(8,128)S(1)} %get-tuple-element.47), channel_id=1, source_target_pairs={{0,1},{1,0},{2,3},{3,2},{4,5},{5,4},{6,7},{7,6},{8,9},{9,8},{10,11... | collective-permute-start | bytes 1572872 | tf_op jit(solution)/shard_map/ppermute | solution.py:507
  18.1 8.3 %collective-permute-start.5 = (f32[128,256]{1,0:T(8,128)S(1)}, f32[128,256]{1,0:T(8,128)S(1)}, u32[]{:S(2)}, u32[]{:S(2)}) collective-permute-start(f32[128,256]{1,0:T(8,128)S(1)} %get-tuple-element.48), channel_id=1, source_target_pairs={{0,4},{4,0},{8,12},{12,8},{1,5},{5,1},{9,13},{13,9},{2,6},{6,2},{1... | collective-permute-start | bytes 393224 | tf_op jit(solution)/shard_map/ppermute | solution.py:507
  19.1 15.2 %collective-permute-start.6 = (f32[128,256]{1,0:T(8,128)S(1)}, f32[128,256]{1,0:T(8,128)S(1)}, u32[]{:S(2)}, u32[]{:S(2)}) collective-permute-start(f32[128,256]{1,0:T(8,128)S(1)} %get-tuple-element.49), channel_id=1, source_target_pairs={{0,8},{4,12},{8,0},{12,4},{1,9},{5,13},{9,1},{13,5},{2,10},{6,14},... | collective-permute-start | bytes 393224 | tf_op jit(solution)/shard_map/ppermute | solution.py:507
  22.6 11.7 %collective-permute-start.7 = (f32[128,256]{1,0:T(8,128)S(1)}, f32[128,256]{1,0:T(8,128)S(1)}, u32[]{:S(2)}, u32[]{:S(2)}) collective-permute-start(f32[128,256]{1,0:T(8,128)S(1)} %get-tuple-element.50), channel_id=1, source_target_pairs={{0,12},{4,8},{8,4},{12,0},{1,13},{5,9},{9,5},{13,1},{2,14},{6,10},... | collective-permute-start | bytes 393224 | tf_op jit(solution)/shard_map/ppermute | solution.py:507
  24.3 17.4 %copy-start = (s32[2,2]{1,0:T(2,128)S(1)}, s32[2,2]{1,0:T(2,128)}, u32[]{:S(2)}) copy-start(s32[2,2]{1,0:T(2,128)} %pairs_ref.1) | copy-start | bytes 52
  24.3 10.2 %collective-permute-start.8 = (f32[128,256]{1,0:T(8,128)S(1)}, f32[128,256]{1,0:T(8,128)S(1)}, u32[]{:S(2)}, u32[]{:S(2)}) collective-permute-start(f32[128,256]{1,0:T(8,128)S(1)} %sum_chips.2.field_ref.refs_0_), channel_id=1, source_target_pairs={{0,2},{2,0},{1,3},{3,1},{4,6},{6,4},{5,7},{7,5},{8,10},{10,8},{9,1... | collective-permute-start | bytes 393224 | tf_op jit(solution)/shard_map/ppermute | solution.py:507
  34.6 1.6 %collective-permute-start.9 = (f32[4,2,2,16,128]{4,3,2,1,0:T(8,128)S(1)}, f32[4,2,2,16,128]{4,3,2,1,0:T(8,128)S(1)}, u32[]{:S(2)}, u32[]{:S(2)}) collective-permute-start(f32[4,2,2,16,128]{4,3,2,1,0:T(8,128)S(1)} %get-tuple-element.53), channel_id=1, source_target_pairs={{0,1},{1,0},{2,3},{3,2},{4,5},{5,4},{6,7},{7,6},{8,9},{9,8},{10,11... | collective-permute-start | bytes 393224 | tf_op jit(solution)/shard_map/ppermute | solution.py:507
  34.7 7.0 %collective-permute-start.12 = (f32[128,256]{1,0:T(8,128)S(1)}, f32[128,256]{1,0:T(8,128)S(1)}, u32[]{:S(2)}, u32[]{:S(2)}) collective-permute-start(f32[128,256]{1,0:T(8,128)S(1)} %sum_chips.3.field_ref.refs_1_), channel_id=1, source_target_pairs={{0,2},{2,0},{1,3},{3,1},{4,6},{6,4},{5,7},{7,5},{8,10},{10,8},{9,1... | collective-permute-start | bytes 393224 | tf_op jit(solution)/shard_map/ppermute | solution.py:507
  36.3 13.3 %collective-permute-start.10 = (f32[2,2,2,16,128]{4,3,2,1,0:T(8,128)S(1)}, f32[2,2,2,16,128]{4,3,2,1,0:T(8,128)S(1)}, u32[]{:S(2)}, u32[]{:S(2)}) collective-permute-start(f32[2,2,2,16,128]{4,3,2,1,0:T(8,128)S(1)} %get-tuple-element.55), channel_id=1, source_target_pairs={{0,8},{4,12},{8,0},{12,4},{1,9},{5,13},{9,1},{13,5},{2,10},{6,14},... | collective-permute-start | bytes 196616 | tf_op jit(solution)/shard_map/ppermute | solution.py:507
  41.2 8.4 %collective-permute-start.11 = (f32[2,2,2,16,128]{4,3,2,1,0:T(8,128)S(1)}, f32[2,2,2,16,128]{4,3,2,1,0:T(8,128)S(1)}, u32[]{:S(2)}, u32[]{:S(2)}) collective-permute-start(f32[2,2,2,16,128]{4,3,2,1,0:T(8,128)S(1)} %get-tuple-element.56), channel_id=1, source_target_pairs={{0,12},{4,8},{8,4},{12,0},{1,13},{5,9},{9,5},{13,1},{2,14},{6,10},... | collective-permute-start | bytes 196616 | tf_op jit(solution)/shard_map/ppermute | solution.py:507
  42.8 1.4 %collective-permute-start.13 = (f32[4,2,2,16,128]{4,3,2,1,0:T(8,128)S(1)}, f32[4,2,2,16,128]{4,3,2,1,0:T(8,128)S(1)}, u32[]{:S(2)}, u32[]{:S(2)}) collective-permute-start(f32[4,2,2,16,128]{4,3,2,1,0:T(8,128)S(1)} %get-tuple-element.59), channel_id=1, source_target_pairs={{0,1},{1,0},{2,3},{3,2},{4,5},{5,4},{6,7},{7,6},{8,9},{9,8},{10,11... | collective-permute-start | bytes 393224 | tf_op jit(solution)/shard_map/ppermute | solution.py:507
  44.2 11.8 %collective-permute-start.14 = (f32[2,2,2,2,16,128]{5,4,3,2,1,0:T(8,128)S(1)}, f32[2,2,2,2,16,128]{5,4,3,2,1,0:T(8,128)S(1)}, u32[]{:S(2)}, u32[]{:S(2)}) collective-permute-start(f32[2,2,2,2,16,128]{5,4,3,2,1,0:T(8,128)S(1)} %get-tuple-element.61), channel_id=1, source_target_pairs={{0,4},{4,0},{8,12},{12,8},{1,5},{5,1},{9,13},{13,9},{2,6},{6,2},{1... | collective-permute-start | bytes 393224 | tf_op jit(solution)/shard_map/ppermute | solution.py:507
  46.2 5.2 %collective-permute-start.15 = (f32[2,2,2,16,128]{4,3,2,1,0:T(8,128)S(1)}, f32[2,2,2,16,128]{4,3,2,1,0:T(8,128)S(1)}, u32[]{:S(2)}, u32[]{:S(2)}) collective-permute-start(f32[2,2,2,16,128]{4,3,2,1,0:T(8,128)S(1)} %get-tuple-element.62), channel_id=1, source_target_pairs={{0,8},{4,12},{8,0},{12,4},{1,9},{5,13},{9,1},{13,5},{2,10},{6,14},... | collective-permute-start | bytes 196616 | tf_op jit(solution)/shard_map/ppermute | solution.py:507
  48.2 7.8 %collective-permute-start.16 = (f32[2,2,2,16,128]{4,3,2,1,0:T(8,128)S(1)}, f32[2,2,2,16,128]{4,3,2,1,0:T(8,128)S(1)}, u32[]{:S(2)}, u32[]{:S(2)}) collective-permute-start(f32[2,2,2,16,128]{4,3,2,1,0:T(8,128)S(1)} %get-tuple-element.63), channel_id=1, source_target_pairs={{0,12},{4,8},{8,4},{12,0},{1,13},{5,9},{9,5},{13,1},{2,14},{6,10},... | collective-permute-start | bytes 196616 | tf_op jit(solution)/shard_map/ppermute | solution.py:507

commit v3 on v2

--- a/solution.py
+++ b/solution.py
@@ -15,6 +15,7 @@
 BF16 = jnp.bfloat16
 VMEM_LIMIT = 16 * 2**20
 SMALL_LIMIT = 4 * 2**20
+ROUND = ((2, 1, 3), (2, 1, 3))
 LARGE = 10**11
 
 
@@ -144,62 +145,46 @@
         out[...] = block if part == 0 else out[...] + block
 
 
-def first_kernel(
-    order,
-    time,
-    slots,
-    chunks,
-    sink_hbm,
-    source_hbm,
-    gamma_hbm,
-    momenta_hbm,
-    pattern_hbm,
-    out,
-    sink_mat,
-    turned,
-    sink_raw,
-    source_raw,
-    sink_stage,
-    source_stage,
-    gamma_ref,
-    momenta_ref,
-    pattern_ref,
-    small_sems,
-    big_sems,
-    *buffers,
-):
-    rows, sites = sink_raw.shape
+def first_kernel(order, time, slots, chunks, ahead, loaded, waits, *refs):
+    sink_src, source_src, gamma_hbm, momenta_hbm, pattern_hbm, *refs = refs
+    out, sink_mat, turned, *refs = refs[waits:]
+    nexts, refs = (refs[:2], refs[2:]) if ahead else ([], refs)
+    sink_stage, source_stage, gamma_ref, momenta_ref, pattern_ref, *refs = refs
+    small_sems, big_sems, next_sems, *refs = refs
+    raws, buffers = ([sink_src, source_src], refs) if loaded else (refs[:2], refs[2:])
+    rows, sites = sink_stage.shape
     fours, _, _, nmode, _ = turned.shape
     per_mode = rows // nmode
     comps = per_mode // 2
     insertions = order()
+    height = rows // chunks
+
     small = [
         pltpu.make_async_copy(src, dst, small_sems.at[k])
         for k, (src, dst) in enumerate(
             [(momenta_hbm, momenta_ref), (pattern_hbm, pattern_ref), (gamma_hbm, gamma_ref)]
         )
     ]
-    for copy in small:
+    big, later = [], []
+    if not loaded:
+        for which, (src, dst) in enumerate(zip((sink_src, source_src), raws)):
+            for k in range(chunks):
+                part = pl.ds(k * height, height)
+                sem = big_sems.at[which * chunks + k]
+                big.append(pltpu.make_async_copy(src.at[time, part], dst.at[part], sem))
+    for k, (src, dst) in enumerate(zip((sink_src, source_src), nexts)):
+        later.append(pltpu.make_async_copy(src.at[time + 1], dst, next_sems.at[k]))
+    for copy in small + big + later:
         copy.start()
-    height = rows // chunks
-    big = []
-    for which, (src, dst) in enumerate([(sink_hbm, sink_raw), (source_hbm, source_raw)]):
+
+    def stage(which, dst):
         for k in range(chunks):
-            part = pl.ds(k * height, height)
-            copy = pltpu.make_async_copy(
-                src.at[time, part], dst.at[part], big_sems.at[which * chunks + k]
-            )
-            copy.start()
-            big.append(copy)
-    for copy in small:
-        copy.wait()
-    pattern_row = pattern_ref[time : time + 1, :]
-    cosine, sine = wave_phases(fours * CLASSES, momenta_ref, pattern_row)
-
-    for k in range(chunks):
-        part = slice(k * height, (k + 1) * height)
-        big[k].wait()
-        sink_stage[part] = sink_raw[part].astype(F32)
+            part = slice(k * height, (k + 1) * height)
+            if not loaded:
+                big[which * chunks + k].wait()
+            dst[part] = raws[which][part].astype(F32)
+
+    stage(0, sink_stage)
     for comp in range(comps):
         at = comp * 2 * sites
         real = sink_stage[pl.ds(2 * comp, nmode, stride=per_mode), :].astype(BF16)
@@ -208,10 +193,11 @@
         sink_mat[0:nmode, at + sites : at + 2 * sites] = imag
         sink_mat[nmode:, at : at + sites] = -imag
         sink_mat[nmode:, at + sites : at + 2 * sites] = real
-    for k in range(chunks):
-        part = slice(k * height, (k + 1) * height)
-        big[chunks + k].wait()
-        source_stage[part] = source_raw[part].astype(F32)
+    for copy in small:
+        copy.wait()
+    pattern_row = pattern_ref[time : time + 1, :]
+    cosine, sine = wave_phases(fours * CLASSES, momenta_ref, pattern_row)
+    stage(1, source_stage)
     for comp in range(comps):
         real = source_stage[pl.ds(2 * comp, nmode, stride=per_mode), :]
         imag = source_stage[pl.ds(2 * comp + 1, nmode, stride=per_mode), :]
@@ -220,6 +206,8 @@
             turned[four, comp, 0] = (real * cos_row - imag * sin_row).astype(BF16)
             turned[four, comp, 1] = (real * sin_row + imag * cos_row).astype(BF16)
     multiply_slots(insertions, slots, gamma_ref, pattern_row, sink_mat, turned, buffers, out)
+    for copy in later:
+        copy.wait()
 
 
 def block_cost(slots, nmode, depth):
@@ -235,23 +223,30 @@
     return [pltpu.VMEM((slots * nmode, depth // parts), BF16)] * parts
 
 
-def first_blocks(sink, source, gamma_index, momenta, pattern, time, nmode, order, slots):
-    _, rows, sites = sink.shape
+def first_blocks(modes, small, time, nmode, order, slots, ahead=False, after=()):
+    rows, sites = modes[0].shape[-2:]
+    loaded = modes[0].ndim == 2
     comps = rows // nmode // 2
     depth = comps * 2 * sites
     chunks = 4 if rows % 64 == 0 else 1
+    gamma_index, momenta, pattern = small
     fours = gamma_index.shape[0] // CLASSES
+    raw = [pltpu.VMEM((rows, sites), BF16)] * 2
+    where = pltpu.VMEM if loaded else pltpu.HBM
+    if not loaded:
+        modes = in_hbm(modes)
     return pl.pallas_call(
-        functools.partial(first_kernel, order, time, slots, chunks),
-        in_specs=[pl.BlockSpec(memory_space=pltpu.HBM)] * 5,
+        functools.partial(first_kernel, order, time, slots, chunks, ahead, loaded, len(after)),
+        in_specs=[pl.BlockSpec(memory_space=where)] * 2
+        + [pl.BlockSpec(memory_space=pltpu.HBM)] * 3
+        + [pl.BlockSpec(memory_space=pl.ANY)] * len(after),
         out_shape=[
             pltpu.VMEM((len(slots), nmode, 2 * nmode), F32),
             pltpu.VMEM((2 * nmode, depth), BF16),
             pltpu.VMEM((fours, comps, 2, nmode, sites), BF16),
-        ],
+        ]
+        + (raw if ahead else []),
         scratch_shapes=[
-            pltpu.VMEM((rows, sites), BF16),
-            pltpu.VMEM((rows, sites), BF16),
             pltpu.VMEM((rows, sites), F32),
             pltpu.VMEM((rows, sites), F32),
             pltpu.SMEM(gamma_index.shape, jnp.int32),
@@ -259,36 +254,21 @@
             pltpu.VMEM(pattern.shape, jnp.int32),
             pltpu.SemaphoreType.DMA((3,)),
             pltpu.SemaphoreType.DMA((2 * chunks,)),
+            pltpu.SemaphoreType.DMA((2,)),
         ]
+        + ([] if loaded else raw)
         + product_buffers(len(slots), nmode, depth),
         compiler_params=pltpu.CompilerParams(vmem_limit_bytes=VMEM_LIMIT),
         cost_estimate=block_cost(len(slots), nmode, depth),
         name="first_blocks",
-    )(sink, source, gamma_index, momenta, pattern)
-
-
-def later_kernel(
-    order,
-    time,
-    slots,
-    gamma_hbm,
-    pattern_hbm,
-    sink_mat,
-    turned,
-    out,
-    gamma_ref,
-    pattern_ref,
-    sems,
-    *buffers,
-):
-    copies = [
-        pltpu.make_async_copy(gamma_hbm, gamma_ref, sems.at[0]),
-        pltpu.make_async_copy(pattern_hbm, pattern_ref, sems.at[1]),
-    ]
-    for copy in copies:
-        copy.start()
-    for copy in copies:
-        copy.wait()
+    )(*modes, *in_hbm(small), *after)
+
+
+def in_hbm(arrays):
+    return [pltpu.with_memory_space_constraint(a, pltpu.HBM) for a in arrays]
+
+
+def later_kernel(order, time, slots, gamma_ref, pattern_ref, sink_mat, turned, out, *buffers):
     pattern_row = pattern_ref[time : time + 1, :]
     multiply_slots(order(), slots, gamma_ref, pattern_row, sink_mat, turned, buffers, out)
 
@@ -297,15 +277,10 @@
     nmode, depth = turned.shape[3], sink_mat.shape[1]
     return pl.pallas_call(
         functools.partial(later_kernel, order, time, slots),
-        in_specs=[pl.BlockSpec(memory_space=pltpu.HBM)] * 2
-        + [pl.BlockSpec(memory_space=pltpu.VMEM)] * 2,
+        in_specs=[pl.BlockSpec(memory_space=pltpu.SMEM)]
+        + [pl.BlockSpec(memory_space=pltpu.VMEM)] * 3,
         out_shape=pltpu.VMEM((len(slots), nmode, 2 * nmode), F32),
-        scratch_shapes=[
-            pltpu.SMEM(gamma_index.shape, jnp.int32),
-            pltpu.VMEM(pattern.shape, jnp.int32),
-            pltpu.SemaphoreType.DMA((2,)),
-        ]
-        + product_buffers(len(slots), nmode, depth),
+        scratch_shapes=product_buffers(len(slots), nmode, depth),
         compiler_params=pltpu.CompilerParams(vmem_limit_bytes=VMEM_LIMIT),
         cost_estimate=block_cost(len(slots), nmode, depth),
         name="later_blocks",
@@ -516,22 +491,20 @@
     spaces, subs, tms = (lax.axis_size(name) for name in ("space", "sub", "tm"))
     order = functools.partial(own_insertions, spaces, subs)
     mine, other = list(range(spaces)), list(range(spaces, 2 * spaces))
-
-    def blocks(gamma_index, time):
-        away, *laid = first_blocks(
-            sink, source, gamma_index, momenta, pattern, time, nmode, order, other
-        )
+    small = (gamma_index, momenta, pattern)
+
+    def send(away, laid, time):
         got = swap(away, "sub", 1)
-        return later_blocks(gamma_index, pattern, *laid, time, order, mine), got
-
-    def send(own, one, two, three):
-        two, three, one = (swap(v, "space", s) for v, s in ((two, 2), (three, 3), (one, 1)))
-        return own, one, two, three
-
-    parts = add_units(*blocks(gamma_index, 0))
-    gamma_index, parts = lax.optimization_barrier((gamma_index, parts))
-    first = send(*parts)
-    second = send(*add_units(*blocks(gamma_index, 1)))
+        keep = later_blocks(gamma_index, pattern, *laid, time, order, mine)
+        parts = add_units(keep, got)
+        return [parts[0]] + [swap(parts[s], "space", s) for s in ROUND[time]]
+
+    away, sink_mat, turned, *modes = first_blocks(
+        (sink, source), small, 0, nmode, order, other, ahead=True
+    )
+    first = send(away, (sink_mat, turned), 0)
+    away, sink_mat, turned = first_blocks(modes, small, 1, nmode, order, other, after=first[:1])
+    second = send(away, (sink_mat, turned), 1)
     first = sum_units(first, scale)
     first_other = swap(first, "tm", 1)
     whole = turn_field(first, second[1:])
@@ -552,9 +525,9 @@
     )
     own, near, two, three = products
     two, three, near = (swap(v, "space", s) for v, s in ((two, 2), (three, 3), (near, 1)))
-    places = [[(1, 1, 0)], [(0, 0, None), (1, 1, 1), (2, 2, None), (3, 3, None)]]
+    places = [[(1, 3, 0)], [(0, 0, None), (1, 3, 1), (2, 2, None), (3, 1, None)]]
     return put_blocks(
-        [own, near, two, three], places, [meson, None], spaces, subs, "put_late", 1
+        [own, three, two, near], places, [meson, None], spaces, subs, "put_late", 1
     )
 
 
@@ -565,11 +538,8 @@
     partial = jnp.stack(
         [
             first_blocks(
-                sink,
-                source,
-                gamma_index,
-                momenta,
-                pattern,
+                (sink, source),
+                (gamma_index, momenta, pattern),
                 time,
                 nmode,
                 lambda: list(range(insertions)),
@@ -606,7 +576,6 @@
     )
     plan = by_owner if owners else by_rows
     arrays = (as_rows(sink_modes), as_rows(source_modes), gamma_index, momenta.T, pattern)
-    arrays = [pltpu.with_memory_space_constraint(a, pltpu.HBM) for a in arrays]
     scale = 1.0 / math.sqrt(3 * sites * spaces * subs)
     return plan(*arrays, time_pairs, nmode, times, scale)
 

time: 57.1 us -> 54.1 us (0.947)
  waiting for transfers between devices: 16.2 us -> 14.4 us
  Pallas kernels: 15.5 us -> 14.4 us
    ppermute x17, waiting for transfers between devices: 16.2 us -> 14.4 us  [swap(): return lax.ppermute(value, axis, [(i, i ^ distance) for i in range(size)])]
    pallas_call x2, Pallas kernels: 7.09 us -> 6.23 us  [first_blocks(): pl.pallas_call(functools.partial(first_kernel, order, time, slots, chunks...]
  transfers between devices with their start and end apart: 17 -> 17, of which waited for: 7 -> 6; matrix products, arithmetic and copies ran while one was open for 0% -> 0% of each run, Pallas kernels for 18% -> 17%
where the time goes in v3:
time: 54.1 us; the launch traced here: 53.9 us
  starting transfers between devices  24.4 us (45%)
  Pallas kernels  14.4 us (27%)
  waiting for transfers between devices  14.4 us (27%)
  between operations  0.81 us (1%)
    ppermute x17, starting transfers between devices, swap(): return lax.ppermute(value, axis, [(i, i ^ distance) for i in range(size)])  24.4 us
    ppermute x17, waiting for transfers between devices, swap(): return lax.ppermute(value, axis, [(i, i ^ distance) for i in range(size)])  14.4 us
    pallas_call x2, Pallas kernels, first_blocks(): pl.pallas_call(functools.partial(first_kernel, order, time, slots, chunks...  6.23 us
    pallas_call x2, Pallas kernels, later_blocks(): pl.pallas_call(functools.partial(later_kernel, order, time, slots), in_sp...  3.16 us
    pallas_call x9, Pallas kernels, small_call(): pl.pallas_call(kernel, in_specs=[pl.BlockSpec(memory_space=pltpu.VMEM)] *...  2.19 us
    pallas_call x2, Pallas kernels, put_blocks(): pl.pallas_call(kernel, in_specs=[pl.BlockSpec(memory_space=pltpu.HBM)] *...  1.65 us
    pallas_call x1, Pallas kernels, product_rows(): pl.pallas_call(functools.partial(product_kernel, spaces, subs, tms), in_s...  1.12 us
  transfers between devices with their start and end apart: 17, of which 6 were waited for; matrix products, arithmetic and copies ran while one was open for 0% of the time, Pallas kernels for 17%

profile of v3, /device:TPU:0, one launch (start us, length us, event | category | flops | bytes accessed | tf_op | source)
XLA Modules:
  0.0 53.9 jit_solution(14082597771245428724)
XLA Ops:
  0.7 3.6 %first_blocks.2 = (f32[4,128,256]{2,1,0:T(8,128)S(1)}, bf16[256,3072]{1,0:T(8,128)(2,1)S(1)}, bf16[2,12,2,128,128]{4,3,2,1,0:T(8,128)(2,1)S(1)}, bf16[3072,128]{1,0:T(8,128)(2,1)S(1)}, bf16[3072,128]{1,0:T(8,128)(2,1)S(1)}) custom-call(bf16[2,3072,128]{2,1,0:T(8,128)(2,1)} %bitcast.7, bf16[2,3072,128]{2,1,0:T(8,128)(2,1)} %bitcast.8, s32[8]{0:T(128)} %gamma_ref.3, ...), custom_call_target="tpu_custom_call" | custom-call | flops 80530636800 | bytes 3145728 | tf_op jit(solution)/shard_map/first_blocks/pallas_call | solution.py:238
  4.2 0.5 collective-permute-start
  4.8 1.6 %later_blocks.2.keep_ref = f32[4,128,256]{2,1,0:T(8,128)S(1)} custom-call(s32[8]{0:T(128)S(1)} %copy-done.3, s32[2,128]{1,0:T(2,128)S(1)} %copy-done.1, bf16[256,3072]{1,0:T(8,128)(2,1)S(1)} %get-tuple-element.30.sink_mat, bf16[2,12,2,128,128]{4,3,2,1,0:T(8,128)(2,1)S(1)} %get-tuple-element.31.turned), custom_call_target="tpu_custom_call" | custom-call | flops 80530636800 | bytes 3145728 | tf_op jit(solution)/shard_map/later_blocks/pallas_call | solution.py:278
  6.4 0.8 %add_cores.2 = (f32[128,256]{1,0:T(8,128)S(1)}, f32[128,256]{1,0:T(8,128)}, f32[128,256]{1,0:T(8,128)}, f32[128,256]{1,0:T(8,128)}) custom-call(f32[4,128,256]{2,1,0:T(8,128)S(1)} %later_blocks.2.keep_ref, f32[4,128,256]{2,1,0:T(8,128)S(1)} %collective-permute-done.got_ref), custom_call_target="tpu_custom_call" | custom-call | flops 1 | bytes 1 | tf_op jit(solution)/shard_map/add_cores/pallas_call | solution.py:291
  7.1 3.9 %collective-permute-start.1 = (f32[128,256]{1,0:T(8,128)}, f32[128,256]{1,0:T(8,128)}, u32[]{:S(2)}, u32[]{:S(2)}) collective-permute-start(f32[128,256]{1,0:T(8,128)} %get-tuple-element.34), channel_id=1, source_target_pairs={{0,8},{4,12},{8,0},{12,4},{1,9},{5,13},{9,1},{13,5},{2,10},{6,14},... | collective-permute-start | bytes 393224 | tf_op jit(solution)/shard_map/ppermute | solution.py:482
  11.0 1.6 %collective-permute-start.2 = (f32[128,256]{1,0:T(8,128)}, f32[128,256]{1,0:T(8,128)}, u32[]{:S(2)}, u32[]{:S(2)}) collective-permute-start(f32[128,256]{1,0:T(8,128)} %get-tuple-element.35), channel_id=1, source_target_pairs={{0,4},{4,0},{8,12},{12,8},{1,5},{5,1},{9,13},{13,9},{2,6},{6,2},{1... | collective-permute-start | bytes 393224 | tf_op jit(solution)/shard_map/ppermute | solution.py:482
  12.6 2.7 %first_blocks.3 = (f32[4,128,256]{2,1,0:T(8,128)S(1)}, bf16[256,3072]{1,0:T(8,128)(2,1)S(1)}, bf16[2,12,2,128,128]{4,3,2,1,0:T(8,128)(2,1)S(1)}) custom-call(bf16[3072,128]{1,0:T(8,128)(2,1)S(1)} %get-tuple-element.37.refs_0_, bf16[3072,128]{1,0:T(8,128)(2,1)S(1)} %get-tuple-element.38.refs_1_, s32[8]{0:T(128)} %gamma_ref.3, s32[3,8]{1,0:T(4,128)} %bitcast.10, ...), custom_call_target="tpu_custom_call" | custom-call | flops 80530636800 | bytes 3145728 | tf_op jit(solution)/shard_map/first_blocks/pallas_call | solution.py:238
  15.3 0.1 collective-permute-start.4
  15.4 1.6 %later_blocks.3.keep_ref = f32[4,128,256]{2,1,0:T(8,128)S(1)} custom-call(s32[8]{0:T(128)S(1)} %copy-done.4, s32[2,128]{1,0:T(2,128)S(1)} %copy-done.2, bf16[256,3072]{1,0:T(8,128)(2,1)S(1)} %get-tuple-element.39.sink_mat, bf16[2,12,2,128,128]{4,3,2,1,0:T(8,128)(2,1)S(1)} %get-tuple-element.40.turned), custom_call_target="tpu_custom_call" | custom-call | flops 80530636800 | bytes 3145728 | tf_op jit(solution)/shard_map/later_blocks/pallas_call | solution.py:278
  17.0 0.3 collective-permute-done.4.got_ref
  17.3 2.0 %collective-permute-start.5 = (f32[128,256]{1,0:T(8,128)S(1)}, f32[128,256]{1,0:T(8,128)S(1)}, u32[]{:S(2)}, u32[]{:S(2)}) collective-permute-start(f32[128,256]{1,0:T(8,128)S(1)} %get-tuple-element.42), channel_id=1, source_target_pairs={{0,8},{4,12},{8,0},{12,4},{1,9},{5,13},{9,1},{13,5},{2,10},{6,14},... | collective-permute-start | bytes 393224 | tf_op jit(solution)/shard_map/ppermute | solution.py:482
  19.3 2.5 %collective-permute-start.6 = (f32[128,256]{1,0:T(8,128)S(1)}, f32[128,256]{1,0:T(8,128)S(1)}, u32[]{:S(2)}, u32[]{:S(2)}) collective-permute-start(f32[128,256]{1,0:T(8,128)S(1)} %get-tuple-element.43), channel_id=1, source_target_pairs={{0,4},{4,0},{8,12},{12,8},{1,5},{5,1},{9,13},{13,9},{2,6},{6,2},{1... | collective-permute-start | bytes 393224 | tf_op jit(solution)/shard_map/ppermute | solution.py:482
  21.8 0.6 %collective-permute-start.7 = (f32[128,256]{1,0:T(8,128)S(1)}, f32[128,256]{1,0:T(8,128)S(1)}, u32[]{:S(2)}, u32[]{:S(2)}) collective-permute-start(f32[128,256]{1,0:T(8,128)S(1)} %get-tuple-element.44), channel_id=1, source_target_pairs={{0,12},{4,8},{8,4},{12,0},{1,13},{5,9},{9,5},{13,1},{2,14},{6,10},... | collective-permute-start | bytes 393224 | tf_op jit(solution)/shard_map/ppermute | solution.py:482
  22.4 1.1 %sum_chips.2.field_ref.refs_0_ = f32[128,256]{1,0:T(8,128)S(1)} custom-call(f32[128,256]{1,0:T(8,128)S(1)} %get-tuple-element.33.refs_0_.refs_5_, f32[128,256]{1,0:T(8,128)} %collective-permute-done.1.refs_1_, f32[128,256]{1,0:T(8,128)} %collective-permute-done.2.refs_2_, f32[128,256]{1,0:T(8,128)} %collective-permute-done.3.refs_3_), custom_call_target="tpu_custom_call" | custom-call | flops 1 | bytes 1 | tf_op jit(solution)/shard_map/sum_chips/pallas_call | solution.py:291
  23.5 1.6 %collective-permute-start.8 = (f32[128,256]{1,0:T(8,128)S(1)}, f32[128,256]{1,0:T(8,128)S(1)}, u32[]{:S(2)}, u32[]{:S(2)}) collective-permute-start(f32[128,256]{1,0:T(8,128)S(1)} %sum_chips.2.field_ref.refs_0_), channel_id=1, source_target_pairs={{0,2},{2,0},{1,3},{3,1},{4,6},{6,4},{5,7},{7,5},{8,10},{10,8},{9,1... | collective-permute-start | bytes 393224 | tf_op jit(solution)/shard_map/ppermute | solution.py:482
  25.0 7.4 %collective-permute-done.5.refs_0_.refs_1_ = f32[128,256]{1,0:T(8,128)S(1)} collective-permute-done((f32[128,256]{1,0:T(8,128)S(1)}, f32[128,256]{1,0:T(8,128)S(1)}, u32[]{:S(2)}, u32[]{:S(2)}) %collective-permute-start.5) | collective-permute-done | bytes 131104 | tf_op jit(solution)/shard_map/ppermute | solution.py:482
  32.4 0.1 turn_field.1.refs_5_.whole_ref
  32.5 0.1 split_rows.1
  32.6 0.1 collective-permute-start.9
  32.7 1.9 %collective-permute-start.12 = (f32[128,256]{1,0:T(8,128)S(1)}, f32[128,256]{1,0:T(8,128)S(1)}, u32[]{:S(2)}, u32[]{:S(2)}) collective-permute-start(f32[128,256]{1,0:T(8,128)S(1)} %sum_chips.3.field_ref.refs_1_), channel_id=1, source_target_pairs={{0,2},{2,0},{1,3},{3,1},{4,6},{6,4},{5,7},{7,5},{8,10},{10,8},{9,1... | collective-permute-start | bytes 393224 | tf_op jit(solution)/shard_map/ppermute | solution.py:482
  34.7 4.7 %collective-permute-start.10 = (f32[2,2,2,16,128]{4,3,2,1,0:T(8,128)S(1)}, f32[2,2,2,16,128]{4,3,2,1,0:T(8,128)S(1)}, u32[]{:S(2)}, u32[]{:S(2)}) collective-permute-start(f32[2,2,2,16,128]{4,3,2,1,0:T(8,128)S(1)} %get-tuple-element.49), channel_id=1, source_target_pairs={{0,8},{4,12},{8,0},{12,4},{1,9},{5,13},{9,1},{13,5},{2,10},{6,14},... | collective-permute-start | bytes 196616 | tf_op jit(solution)/shard_map/ppermute | solution.py:482
  39.4 0.5 collective-permute-start.11
  39.9 1.1 %products.1 = (f32[4,2,2,16,128]{4,3,2,1,0:T(8,128)S(1)}, f32[2,2,128,128]{3,2,1,0:T(8,128)S(1)}) custom-call(s32[2,2]{1,0:T(2,128)S(1)} %copy-done, f32[128,256]{1,0:T(8,128)S(1)} %sum_chips.2.field_ref.refs_0_, f32[128,256]{1,0:T(8,128)S(1)} %sum_chips.3.field_ref.refs_1_, f32[128,256]{1,0:T(8,128)S(1)} %collective-permute-done.8.refs_4_.refs_2_, ...), custom_call_target="tpu_custom_call" | custom-call | flops 33554432 | bytes 1048576 | tf_op jit(solution)/shard_map/products/pallas_call | solution.py:387
  41.1 1.3 %collective-permute-done.13.got_ref = f32[4,2,2,16,128]{4,3,2,1,0:T(8,128)S(1)} collective-permute-done((f32[4,2,2,16,128]{4,3,2,1,0:T(8,128)S(1)}, f32[4,2,2,16,128]{4,3,2,1,0:T(8,128)S(1)}, u32[]{:S(2)}, u32[]{:S(2)}) %collective-permute-start.13) | collective-permute-done | bytes 131104 | tf_op jit(solution)/shard_map/ppermute | solution.py:482
  42.4 3.4 %collective-permute-start.14 = (f32[2,2,2,16,128]{4,3,2,1,0:T(8,128)S(1)}, f32[2,2,2,16,128]{4,3,2,1,0:T(8,128)S(1)}, u32[]{:S(2)}, u32[]{:S(2)}) collective-permute-start(f32[2,2,2,16,128]{4,3,2,1,0:T(8,128)S(1)} %get-tuple-element.55), channel_id=1, source_target_pairs={{0,12},{4,8},{8,4},{12,0},{1,13},{5,9},{9,5},{13,1},{2,14},{6,10},... | collective-permute-start | bytes 196616 | tf_op jit(solution)/shard_map/ppermute | solution.py:482
  45.9 0.5 collective-permute-start.15
  46.4 0.5 collective-permute-start.16
  46.9 0.8 %put_early.1.refs_0_ = f32[2,8,2,16,128]{4,3,2,1,0:T(8,128)} custom-call(f32[2,2,2,16,128]{4,3,2,1,0:T(8,128)S(1)} %get-tuple-element.48.refs_0_, f32[2,2,2,16,128]{4,3,2,1,0:T(8,128)S(1)} %collective-permute-done.10.refs_1_, f32[2,2,2,16,128]{4,3,2,1,0:T(8,128)S(1)} %collective-permute-done.11.refs_2_), custom_call_target="tpu_custom_call" | custom-call | flops 99999997952 | bytes 1 | tf_op jit(solution)/shard_map/put_early/pallas_call | solution.py:466
  47.7 0.9 %collective-permute-done.14.refs_2_ = f32[2,2,2,16,128]{4,3,2,1,0:T(8,128)S(1)} collective-permute-done((f32[2,2,2,16,128]{4,3,2,1,0:T(8,128)S(1)}, f32[2,2,2,16,128]{4,3,2,1,0:T(8,128)S(1)}, u32[]{:S(2)}, u32[]{:S(2)}) %collective-permute-start.14) | collective-permute-done | bytes 65568 | tf_op jit(solution)/shard_map/ppermute | solution.py:482
  48.6 4.1 %collective-permute-done.15.refs_3_ = f32[2,2,2,16,128]{4,3,2,1,0:T(8,128)S(1)} collective-permute-done((f32[2,2,2,16,128]{4,3,2,1,0:T(8,128)S(1)}, f32[2,2,2,16,128]{4,3,2,1,0:T(8,128)S(1)}, u32[]{:S(2)}, u32[]{:S(2)}) %collective-permute-start.15) | collective-permute-done | bytes 65568 | tf_op jit(solution)/shard_map/ppermute | solution.py:482
  52.7 0.3 collective-permute-done.16.refs_4_
  53.0 0.9 %put_late.1 = (f32[2,8,2,16,128]{4,3,2,1,0:T(8,128)}, f32[2,8,2,16,128]{4,3,2,1,0:T(8,128)}) custom-call(f32[2,8,2,16,128]{4,3,2,1,0:T(8,128)} %put_early.1.refs_0_, f32[2,2,2,16,128]{4,3,2,1,0:T(8,128)S(1)} %get-tuple-element.54.refs_1_, f32[2,2,2,16,128]{4,3,2,1,0:T(8,128)S(1)} %collective-permute-done.14.refs_2_, ...), custom_call_target="tpu_custom_call", output_to_operand_aliasing={{0}: (0, {})} | custom-call | flops 1 | bytes 1 | tf_op jit(solution)/shard_map/put_late/pallas_call | solution.py:466
  (28 shorter events, 0.3 us)
Async XLA Ops:
  0.6 4.1 %copy-start.1 = (s32[2,128]{1,0:T(2,128)S(1)}, s32[2,128]{1,0:T(2,128)}, u32[]{:S(2)}) copy-start(s32[2,128]{1,0:T(2,128)} %pattern_ref.3) | copy-start | bytes 3076
  0.6 4.1 %copy-start.3 = (s32[8]{0:T(128)S(1)}, s32[8]{0:T(128)}, u32[]{:S(2)}) copy-start(s32[8]{0:T(128)} %gamma_ref.3) | copy-start | bytes 100
  4.2 2.1 %collective-permute-start = (f32[4,128,256]{2,1,0:T(8,128)S(1)}, f32[4,128,256]{2,1,0:T(8,128)S(1)}, u32[]{:S(2)}, u32[]{:S(2)}) collective-permute-start(f32[4,128,256]{2,1,0:T(8,128)S(1)} %get-tuple-element.32), channel_id=1, source_target_pairs={{0,1},{1,0},{2,3},{3,2},{4,5},{5,4},{6,7},{7,6},{8,9},{9,8},{10,11... | collective-permute-start | bytes 1572872 | tf_op jit(solution)/shard_map/ppermute | solution.py:482
  7.1 14.6 %collective-permute-start.1 = (f32[128,256]{1,0:T(8,128)}, f32[128,256]{1,0:T(8,128)}, u32[]{:S(2)}, u32[]{:S(2)}) collective-permute-start(f32[128,256]{1,0:T(8,128)} %get-tuple-element.34), channel_id=1, source_target_pairs={{0,8},{4,12},{8,0},{12,4},{1,9},{5,13},{9,1},{13,5},{2,10},{6,14},... | collective-permute-start | bytes 393224 | tf_op jit(solution)/shard_map/ppermute | solution.py:482
  11.0 11.3 %collective-permute-start.2 = (f32[128,256]{1,0:T(8,128)}, f32[128,256]{1,0:T(8,128)}, u32[]{:S(2)}, u32[]{:S(2)}) collective-permute-start(f32[128,256]{1,0:T(8,128)} %get-tuple-element.35), channel_id=1, source_target_pairs={{0,4},{4,0},{8,12},{12,8},{1,5},{5,1},{9,13},{13,9},{2,6},{6,2},{1... | collective-permute-start | bytes 393224 | tf_op jit(solution)/shard_map/ppermute | solution.py:482
  12.6 9.8 %collective-permute-start.3 = (f32[128,256]{1,0:T(8,128)}, f32[128,256]{1,0:T(8,128)}, u32[]{:S(2)}, u32[]{:S(2)}) collective-permute-start(f32[128,256]{1,0:T(8,128)} %get-tuple-element.36), channel_id=1, source_target_pairs={{0,12},{4,8},{8,4},{12,0},{1,13},{5,9},{9,5},{13,1},{2,14},{6,10},... | collective-permute-start | bytes 393224 | tf_op jit(solution)/shard_map/ppermute | solution.py:482
  12.6 2.7 %copy-start.2 = (s32[2,128]{1,0:T(2,128)S(1)}, s32[2,128]{1,0:T(2,128)}, u32[]{:S(2)}) copy-start(s32[2,128]{1,0:T(2,128)} %pattern_ref.3) | copy-start | bytes 3076
  12.6 2.8 %copy-start.4 = (s32[8]{0:T(128)S(1)}, s32[8]{0:T(128)}, u32[]{:S(2)}) copy-start(s32[8]{0:T(128)} %gamma_ref.3) | copy-start | bytes 100
  15.3 2.0 %collective-permute-start.4 = (f32[4,128,256]{2,1,0:T(8,128)S(1)}, f32[4,128,256]{2,1,0:T(8,128)S(1)}, u32[]{:S(2)}, u32[]{:S(2)}) collective-permute-start(f32[4,128,256]{2,1,0:T(8,128)S(1)} %get-tuple-element.41), channel_id=1, source_target_pairs={{0,1},{1,0},{2,3},{3,2},{4,5},{5,4},{6,7},{7,6},{8,9},{9,8},{10,11... | collective-permute-start | bytes 1572872 | tf_op jit(solution)/shard_map/ppermute | solution.py:482
  17.3 15.1 %collective-permute-start.5 = (f32[128,256]{1,0:T(8,128)S(1)}, f32[128,256]{1,0:T(8,128)S(1)}, u32[]{:S(2)}, u32[]{:S(2)}) collective-permute-start(f32[128,256]{1,0:T(8,128)S(1)} %get-tuple-element.42), channel_id=1, source_target_pairs={{0,8},{4,12},{8,0},{12,4},{1,9},{5,13},{9,1},{13,5},{2,10},{6,14},... | collective-permute-start | bytes 393224 | tf_op jit(solution)/shard_map/ppermute | solution.py:482
  19.3 13.1 %collective-permute-start.6 = (f32[128,256]{1,0:T(8,128)S(1)}, f32[128,256]{1,0:T(8,128)S(1)}, u32[]{:S(2)}, u32[]{:S(2)}) collective-permute-start(f32[128,256]{1,0:T(8,128)S(1)} %get-tuple-element.43), channel_id=1, source_target_pairs={{0,4},{4,0},{8,12},{12,8},{1,5},{5,1},{9,13},{13,9},{2,6},{6,2},{1... | collective-permute-start | bytes 393224 | tf_op jit(solution)/shard_map/ppermute | solution.py:482
  21.8 10.6 %collective-permute-start.7 = (f32[128,256]{1,0:T(8,128)S(1)}, f32[128,256]{1,0:T(8,128)S(1)}, u32[]{:S(2)}, u32[]{:S(2)}) collective-permute-start(f32[128,256]{1,0:T(8,128)S(1)} %get-tuple-element.44), channel_id=1, source_target_pairs={{0,12},{4,8},{8,4},{12,0},{1,13},{5,9},{9,5},{13,1},{2,14},{6,10},... | collective-permute-start | bytes 393224 | tf_op jit(solution)/shard_map/ppermute | solution.py:482
  23.4 16.4 %copy-start = (s32[2,2]{1,0:T(2,128)S(1)}, s32[2,2]{1,0:T(2,128)}, u32[]{:S(2)}) copy-start(s32[2,2]{1,0:T(2,128)} %pairs_ref.1) | copy-start | bytes 52
  23.5 9.0 %collective-permute-start.8 = (f32[128,256]{1,0:T(8,128)S(1)}, f32[128,256]{1,0:T(8,128)S(1)}, u32[]{:S(2)}, u32[]{:S(2)}) collective-permute-start(f32[128,256]{1,0:T(8,128)S(1)} %sum_chips.2.field_ref.refs_0_), channel_id=1, source_target_pairs={{0,2},{2,0},{1,3},{3,1},{4,6},{6,4},{5,7},{7,5},{8,10},{10,8},{9,1... | collective-permute-start | bytes 393224 | tf_op jit(solution)/shard_map/ppermute | solution.py:482
  32.6 2.0 %collective-permute-start.9 = (f32[4,2,2,16,128]{4,3,2,1,0:T(8,128)S(1)}, f32[4,2,2,16,128]{4,3,2,1,0:T(8,128)S(1)}, u32[]{:S(2)}, u32[]{:S(2)}) collective-permute-start(f32[4,2,2,16,128]{4,3,2,1,0:T(8,128)S(1)} %get-tuple-element.47), channel_id=1, source_target_pairs={{0,1},{1,0},{2,3},{3,2},{4,5},{5,4},{6,7},{7,6},{8,9},{9,8},{10,11... | collective-permute-start | bytes 393224 | tf_op jit(solution)/shard_map/ppermute | solution.py:482
  32.7 7.1 %collective-permute-start.12 = (f32[128,256]{1,0:T(8,128)S(1)}, f32[128,256]{1,0:T(8,128)S(1)}, u32[]{:S(2)}, u32[]{:S(2)}) collective-permute-start(f32[128,256]{1,0:T(8,128)S(1)} %sum_chips.3.field_ref.refs_1_), channel_id=1, source_target_pairs={{0,2},{2,0},{1,3},{3,1},{4,6},{6,4},{5,7},{7,5},{8,10},{10,8},{9,1... | collective-permute-start | bytes 393224 | tf_op jit(solution)/shard_map/ppermute | solution.py:482
  34.7 12.2 %collective-permute-start.10 = (f32[2,2,2,16,128]{4,3,2,1,0:T(8,128)S(1)}, f32[2,2,2,16,128]{4,3,2,1,0:T(8,128)S(1)}, u32[]{:S(2)}, u32[]{:S(2)}) collective-permute-start(f32[2,2,2,16,128]{4,3,2,1,0:T(8,128)S(1)} %get-tuple-element.49), channel_id=1, source_target_pairs={{0,8},{4,12},{8,0},{12,4},{1,9},{5,13},{9,1},{13,5},{2,10},{6,14},... | collective-permute-start | bytes 196616 | tf_op jit(solution)/shard_map/ppermute | solution.py:482
  39.4 7.5 %collective-permute-start.11 = (f32[2,2,2,16,128]{4,3,2,1,0:T(8,128)S(1)}, f32[2,2,2,16,128]{4,3,2,1,0:T(8,128)S(1)}, u32[]{:S(2)}, u32[]{:S(2)}) collective-permute-start(f32[2,2,2,16,128]{4,3,2,1,0:T(8,128)S(1)} %get-tuple-element.50), channel_id=1, source_target_pairs={{0,12},{4,8},{8,4},{12,0},{1,13},{5,9},{9,5},{13,1},{2,14},{6,10},... | collective-permute-start | bytes 196616 | tf_op jit(solution)/shard_map/ppermute | solution.py:482
  41.0 1.4 %collective-permute-start.13 = (f32[4,2,2,16,128]{4,3,2,1,0:T(8,128)S(1)}, f32[4,2,2,16,128]{4,3,2,1,0:T(8,128)S(1)}, u32[]{:S(2)}, u32[]{:S(2)}) collective-permute-start(f32[4,2,2,16,128]{4,3,2,1,0:T(8,128)S(1)} %get-tuple-element.53), channel_id=1, source_target_pairs={{0,1},{1,0},{2,3},{3,2},{4,5},{5,4},{6,7},{7,6},{8,9},{9,8},{10,11... | collective-permute-start | bytes 393224 | tf_op jit(solution)/shard_map/ppermute | solution.py:482
  42.4 6.2 %collective-permute-start.14 = (f32[2,2,2,16,128]{4,3,2,1,0:T(8,128)S(1)}, f32[2,2,2,16,128]{4,3,2,1,0:T(8,128)S(1)}, u32[]{:S(2)}, u32[]{:S(2)}) collective-permute-start(f32[2,2,2,16,128]{4,3,2,1,0:T(8,128)S(1)} %get-tuple-element.55), channel_id=1, source_target_pairs={{0,12},{4,8},{8,4},{12,0},{1,13},{5,9},{9,5},{13,1},{2,14},{6,10},... | collective-permute-start | bytes 196616 | tf_op jit(solution)/shard_map/ppermute | solution.py:482
  45.9 6.8 %collective-permute-start.15 = (f32[2,2,2,16,128]{4,3,2,1,0:T(8,128)S(1)}, f32[2,2,2,16,128]{4,3,2,1,0:T(8,128)S(1)}, u32[]{:S(2)}, u32[]{:S(2)}) collective-permute-start(f32[2,2,2,16,128]{4,3,2,1,0:T(8,128)S(1)} %get-tuple-element.56), channel_id=1, source_target_pairs={{0,8},{4,12},{8,0},{12,4},{1,9},{5,13},{9,1},{13,5},{2,10},{6,14},... | collective-permute-start | bytes 196616 | tf_op jit(solution)/shard_map/ppermute | solution.py:482
  46.4 6.7 %collective-permute-start.16 = (f32[2,2,2,2,16,128]{5,4,3,2,1,0:T(8,128)S(1)}, f32[2,2,2,2,16,128]{5,4,3,2,1,0:T(8,128)S(1)}, u32[]{:S(2)}, u32[]{:S(2)}) collective-permute-start(f32[2,2,2,2,16,128]{5,4,3,2,1,0:T(8,128)S(1)} %get-tuple-element.57), channel_id=1, source_target_pairs={{0,4},{4,0},{8,12},{12,8},{1,5},{5,1},{9,13},{13,9},{2,6},{6,2},{1... | collective-permute-start | bytes 393224 | tf_op jit(solution)/shard_map/ppermute | solution.py:482

commit v4 on v3

--- a/solution.py
+++ b/solution.py
@@ -212,7 +212,7 @@
 
 def block_cost(slots, nmode, depth):
     return pl.CostEstimate(
-        flops=400 * slots * nmode * nmode * depth,
+        flops=100 * slots * nmode * nmode * depth,
         bytes_accessed=8 * nmode * depth,
         transcendentals=0,
     )
@@ -450,14 +450,13 @@
             for s, operand, index in group:
                 block = refs[operand] if index is None else refs[operand].at[index]
                 for c in range(subs):
-                    for lane in range(lanes):
-                        copy = pltpu.make_async_copy(
-                            block.at[c, lane],
-                            out.at[lane, (z ^ s) * subs + (core ^ c)],
-                            sems.at[len(copies)],
-                        )
-                        copy.start()
-                        copies.append(copy)
+                    copy = pltpu.make_async_copy(
+                        block.at[c],
+                        out.at[:, (z ^ s) * subs + (core ^ c)],
+                        sems.at[len(copies)],
+                    )
+                    copy.start()
+                    copies.append(copy)
         for copy in copies:
             copy.wait()
 
@@ -470,7 +469,7 @@
         out_specs=[pl.BlockSpec(memory_space=pltpu.HBM)] * count,
         out_shape=[out] * count,
         input_output_aliases={n: k for n, (k, _) in enumerate(given)},
-        scratch_shapes=[pltpu.SemaphoreType.DMA((sum(map(len, places)) * subs * lanes,))],
+        scratch_shapes=[pltpu.SemaphoreType.DMA((sum(map(len, places)) * subs,))],
         compiler_params=pltpu.CompilerParams(vmem_limit_bytes=SMALL_LIMIT),
         cost_estimate=pl.CostEstimate(flops=flops, bytes_accessed=1, transcendentals=0),
         name=name,
@@ -519,16 +518,15 @@
     away, whole = product_rows(time_pairs, fields, spaces, subs, tms)
     got = swap(away, "sub", 1)
     products = pair_with(meson_near, keep_rows(whole, spaces, subs), got)
-    places = [[(0, 0, None), (2, 1, None), (3, 2, None)]]
-    (meson,) = put_blocks(
-        [own, two, three], places, [None], spaces, subs, "put_early", LARGE
-    )
+    places = [[(0, 0, None), (2, 1, None), (3, 2, None)], [(0, 3, None)]]
+    meson_parts = [own, two, three]
     own, near, two, three = products
     two, three, near = (swap(v, "space", s) for v, s in ((two, 2), (three, 3), (near, 1)))
-    places = [[(1, 3, 0)], [(0, 0, None), (1, 3, 1), (2, 2, None), (3, 1, None)]]
-    return put_blocks(
-        [own, three, two, near], places, [meson, None], spaces, subs, "put_late", 1
+    arrays = put_blocks(
+        meson_parts + [own], places, [None, None], spaces, subs, "put_early", LARGE
     )
+    places = [[(1, 2, 0)], [(1, 2, 1), (2, 1, None), (3, 0, None)]]
+    return put_blocks([three, two, near], places, arrays, spaces, subs, "put_late", 1)
 
 
 def by_rows(sink, source, gamma_index, momenta, pattern, time_pairs, nmode, times, scale):

time: 54.1 us -> 53.1 us (0.982)
  Pallas kernels: 14.4 us -> 12.5 us
  waiting for transfers between devices: 14.4 us -> 15.5 us
    pallas_call x9, Pallas kernels: 2.19 us -> 0.43 us  [small_call(): pl.pallas_call(kernel, in_specs=[pl.BlockSpec(memory_space=pltpu.VMEM)] *...]
    ppermute x17, waiting for transfers between devices: 14.4 us -> 15.5 us  [swap(): return lax.ppermute(value, axis, [(i, i ^ distance) for i in range(size)])]
  transfers between devices with their start and end apart: 17 -> 17, of which waited for: 6 -> 6; matrix products, arithmetic and copies ran while one was open for 0% -> 0% of each run, Pallas kernels for 17% -> 15%
where the time goes in v4:
time: 53.1 us; the launch traced here: 52.9 us
  starting transfers between devices  24.1 us (45%)
  waiting for transfers between devices  15.5 us (29%)
  Pallas kernels  12.5 us (24%)
  between operations  0.83 us (2%)
    ppermute x17, starting transfers between devices, swap(): return lax.ppermute(value, axis, [(i, i ^ distance) for i in range(size)])  24.1 us
    ppermute x17, waiting for transfers between devices, swap(): return lax.ppermute(value, axis, [(i, i ^ distance) for i in range(size)])  15.5 us
    pallas_call x2, Pallas kernels, first_blocks(): pl.pallas_call(functools.partial(first_kernel, order, time, slots, chunks...  6.24 us
    pallas_call x2, Pallas kernels, later_blocks(): pl.pallas_call(functools.partial(later_kernel, order, time, slots), in_sp...  3.16 us
    pallas_call x2, Pallas kernels, put_blocks(): pl.pallas_call(kernel, in_specs=[pl.BlockSpec(memory_space=pltpu.HBM)] *...  1.52 us
    pallas_call x1, Pallas kernels, product_rows(): pl.pallas_call(functools.partial(product_kernel, spaces, subs, tms), in_s...  1.12 us
  transfers between devices with their start and end apart: 17, of which 6 were waited for; matrix products, arithmetic and copies ran while one was open for 0% of the time, Pallas kernels for 15%

profile of v4, /device:TPU:0, one launch (start us, length us, event | category | flops | bytes accessed | tf_op | source)
XLA Modules:
  0.0 52.9 jit_solution(12888674394643671081)
XLA Ops:
  0.7 3.6 %first_blocks.2 = (f32[4,128,256]{2,1,0:T(8,128)S(1)}, bf16[256,3072]{1,0:T(8,128)(2,1)S(1)}, bf16[2,12,2,128,128]{4,3,2,1,0:T(8,128)(2,1)S(1)}, bf16[3072,128]{1,0:T(8,128)(2,1)S(1)}, bf16[3072,128]{1,0:T(8,128)(2,1)S(1)}) custom-call(bf16[2,3072,128]{2,1,0:T(8,128)(2,1)} %bitcast.7, bf16[2,3072,128]{2,1,0:T(8,128)(2,1)} %bitcast.8, s32[8]{0:T(128)} %gamma_ref.3, ...), custom_call_target="tpu_custom_call" | custom-call | flops 20132659200 | bytes 3145728 | tf_op jit(solution)/shard_map/first_blocks/pallas_call | solution.py:238
  4.2 0.5 collective-permute-start
  4.8 1.6 %later_blocks.2.keep_ref = f32[4,128,256]{2,1,0:T(8,128)S(1)} custom-call(s32[8]{0:T(128)S(1)} %copy-done.3, s32[2,128]{1,0:T(2,128)S(1)} %copy-done.1, bf16[256,3072]{1,0:T(8,128)(2,1)S(1)} %get-tuple-element.32.sink_mat, bf16[2,12,2,128,128]{4,3,2,1,0:T(8,128)(2,1)S(1)} %get-tuple-element.33.turned), custom_call_target="tpu_custom_call" | custom-call | flops 20132659200 | bytes 3145728 | tf_op jit(solution)/shard_map/later_blocks/pallas_call | solution.py:278
  6.4 0.1 add_cores.2
  6.4 4.0 %collective-permute-start.1 = (f32[128,256]{1,0:T(8,128)S(1)}, f32[128,256]{1,0:T(8,128)S(1)}, u32[]{:S(2)}, u32[]{:S(2)}) collective-permute-start(f32[128,256]{1,0:T(8,128)S(1)} %get-tuple-element.36), channel_id=1, source_target_pairs={{0,8},{4,12},{8,0},{12,4},{1,9},{5,13},{9,1},{13,5},{2,10},{6,14},... | collective-permute-start | bytes 393224 | tf_op jit(solution)/shard_map/ppermute | solution.py:481
  10.4 1.6 %collective-permute-start.2 = (f32[128,256]{1,0:T(8,128)S(1)}, f32[128,256]{1,0:T(8,128)S(1)}, u32[]{:S(2)}, u32[]{:S(2)}) collective-permute-start(f32[128,256]{1,0:T(8,128)S(1)} %get-tuple-element.37), channel_id=1, source_target_pairs={{0,4},{4,0},{8,12},{12,8},{1,5},{5,1},{9,13},{13,9},{2,6},{6,2},{1... | collective-permute-start | bytes 393224 | tf_op jit(solution)/shard_map/ppermute | solution.py:481
  12.0 2.7 %first_blocks.3 = (f32[4,128,256]{2,1,0:T(8,128)S(1)}, bf16[256,3072]{1,0:T(8,128)(2,1)S(1)}, bf16[2,12,2,128,128]{4,3,2,1,0:T(8,128)(2,1)S(1)}) custom-call(bf16[3072,128]{1,0:T(8,128)(2,1)S(1)} %get-tuple-element.39.refs_0_, bf16[3072,128]{1,0:T(8,128)(2,1)S(1)} %get-tuple-element.40.refs_1_, s32[8]{0:T(128)} %gamma_ref.3, s32[3,8]{1,0:T(4,128)} %bitcast.10, ...), custom_call_target="tpu_custom_call" | custom-call | flops 20132659200 | bytes 3145728 | tf_op jit(solution)/shard_map/first_blocks/pallas_call | solution.py:238
  14.6 0.1 collective-permute-start.4
  14.7 1.6 %later_blocks.3.keep_ref = f32[4,128,256]{2,1,0:T(8,128)S(1)} custom-call(s32[8]{0:T(128)S(1)} %copy-done.4, s32[2,128]{1,0:T(2,128)S(1)} %copy-done.2, bf16[256,3072]{1,0:T(8,128)(2,1)S(1)} %get-tuple-element.41.sink_mat, bf16[2,12,2,128,128]{4,3,2,1,0:T(8,128)(2,1)S(1)} %get-tuple-element.42.turned), custom_call_target="tpu_custom_call" | custom-call | flops 20132659200 | bytes 3145728 | tf_op jit(solution)/shard_map/later_blocks/pallas_call | solution.py:278
  16.3 0.3 collective-permute-done.4.got_ref
  16.7 2.0 %collective-permute-start.5 = (f32[128,256]{1,0:T(8,128)S(1)}, f32[128,256]{1,0:T(8,128)S(1)}, u32[]{:S(2)}, u32[]{:S(2)}) collective-permute-start(f32[128,256]{1,0:T(8,128)S(1)} %get-tuple-element.44), channel_id=1, source_target_pairs={{0,8},{4,12},{8,0},{12,4},{1,9},{5,13},{9,1},{13,5},{2,10},{6,14},... | collective-permute-start | bytes 393224 | tf_op jit(solution)/shard_map/ppermute | solution.py:481
  18.6 2.5 %collective-permute-start.6 = (f32[128,256]{1,0:T(8,128)S(1)}, f32[128,256]{1,0:T(8,128)S(1)}, u32[]{:S(2)}, u32[]{:S(2)}) collective-permute-start(f32[128,256]{1,0:T(8,128)S(1)} %get-tuple-element.45), channel_id=1, source_target_pairs={{0,4},{4,0},{8,12},{12,8},{1,5},{5,1},{9,13},{13,9},{2,6},{6,2},{1... | collective-permute-start | bytes 393224 | tf_op jit(solution)/shard_map/ppermute | solution.py:481
  21.1 0.3 collective-permute-start.7
  21.5 1.6 %collective-permute-start.8 = (f32[128,256]{1,0:T(8,128)S(1)}, f32[128,256]{1,0:T(8,128)S(1)}, u32[]{:S(2)}, u32[]{:S(2)}) collective-permute-start(f32[128,256]{1,0:T(8,128)S(1)} %sum_chips.2.field_ref.refs_0_), channel_id=1, source_target_pairs={{0,2},{2,0},{1,3},{3,1},{4,6},{6,4},{5,7},{7,5},{8,10},{10,8},{9,1... | collective-permute-start | bytes 393224 | tf_op jit(solution)/shard_map/ppermute | solution.py:481
  23.0 8.5 %collective-permute-done.5.refs_0_.refs_1_ = f32[128,256]{1,0:T(8,128)S(1)} collective-permute-done((f32[128,256]{1,0:T(8,128)S(1)}, f32[128,256]{1,0:T(8,128)S(1)}, u32[]{:S(2)}, u32[]{:S(2)}) %collective-permute-start.5) | collective-permute-done | bytes 131104 | tf_op jit(solution)/shard_map/ppermute | solution.py:481
  31.5 0.1 turn_field.1.refs_5_.whole_ref
  31.7 0.1 split_rows.1
  31.8 0.1 collective-permute-start.9
  31.9 1.9 %collective-permute-start.12 = (f32[128,256]{1,0:T(8,128)S(1)}, f32[128,256]{1,0:T(8,128)S(1)}, u32[]{:S(2)}, u32[]{:S(2)}) collective-permute-start(f32[128,256]{1,0:T(8,128)S(1)} %sum_chips.3.field_ref.refs_1_), channel_id=1, source_target_pairs={{0,2},{2,0},{1,3},{3,1},{4,6},{6,4},{5,7},{7,5},{8,10},{10,8},{9,1... | collective-permute-start | bytes 393224 | tf_op jit(solution)/shard_map/ppermute | solution.py:481
  33.8 4.7 %collective-permute-start.10 = (f32[2,2,2,16,128]{4,3,2,1,0:T(8,128)S(1)}, f32[2,2,2,16,128]{4,3,2,1,0:T(8,128)S(1)}, u32[]{:S(2)}, u32[]{:S(2)}) collective-permute-start(f32[2,2,2,16,128]{4,3,2,1,0:T(8,128)S(1)} %get-tuple-element.51), channel_id=1, source_target_pairs={{0,8},{4,12},{8,0},{12,4},{1,9},{5,13},{9,1},{13,5},{2,10},{6,14},... | collective-permute-start | bytes 196616 | tf_op jit(solution)/shard_map/ppermute | solution.py:481
  38.5 0.5 collective-permute-start.11
  39.0 1.1 %products.1 = (f32[4,2,2,16,128]{4,3,2,1,0:T(8,128)S(1)}, f32[2,2,128,128]{3,2,1,0:T(8,128)S(1)}) custom-call(s32[2,2]{1,0:T(2,128)S(1)} %copy-done, f32[128,256]{1,0:T(8,128)S(1)} %sum_chips.2.field_ref.refs_0_, f32[128,256]{1,0:T(8,128)S(1)} %sum_chips.3.field_ref.refs_1_, f32[128,256]{1,0:T(8,128)S(1)} %collective-permute-done.8.refs_4_.refs_2_, ...), custom_call_target="tpu_custom_call" | custom-call | flops 33554432 | bytes 1048576 | tf_op jit(solution)/shard_map/products/pallas_call | solution.py:387
  40.1 0.1 collective-permute-start.13
  40.2 1.3 %collective-permute-done.13.got_ref = f32[4,2,2,16,128]{4,3,2,1,0:T(8,128)S(1)} collective-permute-done((f32[4,2,2,16,128]{4,3,2,1,0:T(8,128)S(1)}, f32[4,2,2,16,128]{4,3,2,1,0:T(8,128)S(1)}, u32[]{:S(2)}, u32[]{:S(2)}) %collective-permute-start.13) | collective-permute-done | bytes 131104 | tf_op jit(solution)/shard_map/ppermute | solution.py:481
  41.6 3.4 %collective-permute-start.14 = (f32[2,2,2,16,128]{4,3,2,1,0:T(8,128)S(1)}, f32[2,2,2,16,128]{4,3,2,1,0:T(8,128)S(1)}, u32[]{:S(2)}, u32[]{:S(2)}) collective-permute-start(f32[2,2,2,16,128]{4,3,2,1,0:T(8,128)S(1)} %get-tuple-element.59), channel_id=1, source_target_pairs={{0,12},{4,8},{8,4},{12,0},{1,13},{5,9},{9,5},{13,1},{2,14},{6,10},... | collective-permute-start | bytes 196616 | tf_op jit(solution)/shard_map/ppermute | solution.py:481
  45.0 0.5 collective-permute-start.15
  45.5 0.5 collective-permute-start.16
  46.0 0.8 %put_early.1 = (f32[2,8,2,16,128]{4,3,2,1,0:T(8,128)}, f32[2,8,2,16,128]{4,3,2,1,0:T(8,128)}) custom-call(f32[2,2,2,16,128]{4,3,2,1,0:T(8,128)S(1)} %get-tuple-element.50.refs_0_, f32[2,2,2,16,128]{4,3,2,1,0:T(8,128)S(1)} %collective-permute-done.10.refs_1_, f32[2,2,2,16,128]{4,3,2,1,0:T(8,128)S(1)} %collective-permute-done.11.refs_2_, ...), custom_call_target="tpu_custom_call" | custom-call | flops 99999997952 | bytes 1 | tf_op jit(solution)/shard_map/put_early/pallas_call | solution.py:465
  46.8 1.0 %collective-permute-done.14.refs_2_ = f32[2,2,2,16,128]{4,3,2,1,0:T(8,128)S(1)} collective-permute-done((f32[2,2,2,16,128]{4,3,2,1,0:T(8,128)S(1)}, f32[2,2,2,16,128]{4,3,2,1,0:T(8,128)S(1)}, u32[]{:S(2)}, u32[]{:S(2)}) %collective-permute-start.14) | collective-permute-done | bytes 65568 | tf_op jit(solution)/shard_map/ppermute | solution.py:481
  47.7 4.1 %collective-permute-done.15.refs_3_ = f32[2,2,2,16,128]{4,3,2,1,0:T(8,128)S(1)} collective-permute-done((f32[2,2,2,16,128]{4,3,2,1,0:T(8,128)S(1)}, f32[2,2,2,16,128]{4,3,2,1,0:T(8,128)S(1)}, u32[]{:S(2)}, u32[]{:S(2)}) %collective-permute-start.15) | collective-permute-done | bytes 65568 | tf_op jit(solution)/shard_map/ppermute | solution.py:481
  51.8 0.3 collective-permute-done.16.refs_4_
  52.2 0.8 %put_late.1 = (f32[2,8,2,16,128]{4,3,2,1,0:T(8,128)}, f32[2,8,2,16,128]{4,3,2,1,0:T(8,128)}) custom-call(f32[2,8,2,16,128]{4,3,2,1,0:T(8,128)} %get-tuple-element.57.refs_0_, f32[2,8,2,16,128]{4,3,2,1,0:T(8,128)} %get-tuple-element.58.refs_1_, ...), custom_call_target="tpu_custom_call", output_to_operand_aliasing={{0}: (0, {}), {1}: (1, {})} | custom-call | flops 1 | bytes 1 | tf_op jit(solution)/shard_map/put_late/pallas_call | solution.py:465
  (28 shorter events, 0.2 us)
Async XLA Ops:
  0.6 4.1 %copy-start.1 = (s32[2,128]{1,0:T(2,128)S(1)}, s32[2,128]{1,0:T(2,128)}, u32[]{:S(2)}) copy-start(s32[2,128]{1,0:T(2,128)} %pattern_ref.3) | copy-start | bytes 3076
  0.6 4.1 %copy-start.3 = (s32[8]{0:T(128)S(1)}, s32[8]{0:T(128)}, u32[]{:S(2)}) copy-start(s32[8]{0:T(128)} %gamma_ref.3) | copy-start | bytes 100
  4.2 2.1 %collective-permute-start = (f32[4,128,256]{2,1,0:T(8,128)S(1)}, f32[4,128,256]{2,1,0:T(8,128)S(1)}, u32[]{:S(2)}, u32[]{:S(2)}) collective-permute-start(f32[4,128,256]{2,1,0:T(8,128)S(1)} %get-tuple-element.34), channel_id=1, source_target_pairs={{0,1},{1,0},{2,3},{3,2},{4,5},{5,4},{6,7},{7,6},{8,9},{9,8},{10,11... | collective-permute-start | bytes 1572872 | tf_op jit(solution)/shard_map/ppermute | solution.py:481
  6.4 14.7 %collective-permute-start.1 = (f32[128,256]{1,0:T(8,128)S(1)}, f32[128,256]{1,0:T(8,128)S(1)}, u32[]{:S(2)}, u32[]{:S(2)}) collective-permute-start(f32[128,256]{1,0:T(8,128)S(1)} %get-tuple-element.36), channel_id=1, source_target_pairs={{0,8},{4,12},{8,0},{12,4},{1,9},{5,13},{9,1},{13,5},{2,10},{6,14},... | collective-permute-start | bytes 393224 | tf_op jit(solution)/shard_map/ppermute | solution.py:481
  10.4 11.0 %collective-permute-start.2 = (f32[128,256]{1,0:T(8,128)S(1)}, f32[128,256]{1,0:T(8,128)S(1)}, u32[]{:S(2)}, u32[]{:S(2)}) collective-permute-start(f32[128,256]{1,0:T(8,128)S(1)} %get-tuple-element.37), channel_id=1, source_target_pairs={{0,4},{4,0},{8,12},{12,8},{1,5},{5,1},{9,13},{13,9},{2,6},{6,2},{1... | collective-permute-start | bytes 393224 | tf_op jit(solution)/shard_map/ppermute | solution.py:481
  12.0 9.5 %collective-permute-start.3 = (f32[128,256]{1,0:T(8,128)S(1)}, f32[128,256]{1,0:T(8,128)S(1)}, u32[]{:S(2)}, u32[]{:S(2)}) collective-permute-start(f32[128,256]{1,0:T(8,128)S(1)} %get-tuple-element.38), channel_id=1, source_target_pairs={{0,12},{4,8},{8,4},{12,0},{1,13},{5,9},{9,5},{13,1},{2,14},{6,10},... | collective-permute-start | bytes 393224 | tf_op jit(solution)/shard_map/ppermute | solution.py:481
  12.0 2.8 %copy-start.2 = (s32[2,128]{1,0:T(2,128)S(1)}, s32[2,128]{1,0:T(2,128)}, u32[]{:S(2)}) copy-start(s32[2,128]{1,0:T(2,128)} %pattern_ref.3) | copy-start | bytes 3076
  12.0 2.8 %copy-start.4 = (s32[8]{0:T(128)S(1)}, s32[8]{0:T(128)}, u32[]{:S(2)}) copy-start(s32[8]{0:T(128)} %gamma_ref.3) | copy-start | bytes 100
  14.6 2.0 %collective-permute-start.4 = (f32[4,128,256]{2,1,0:T(8,128)S(1)}, f32[4,128,256]{2,1,0:T(8,128)S(1)}, u32[]{:S(2)}, u32[]{:S(2)}) collective-permute-start(f32[4,128,256]{2,1,0:T(8,128)S(1)} %get-tuple-element.43), channel_id=1, source_target_pairs={{0,1},{1,0},{2,3},{3,2},{4,5},{5,4},{6,7},{7,6},{8,9},{9,8},{10,11... | collective-permute-start | bytes 1572872 | tf_op jit(solution)/shard_map/ppermute | solution.py:481
  16.7 14.8 %collective-permute-start.5 = (f32[128,256]{1,0:T(8,128)S(1)}, f32[128,256]{1,0:T(8,128)S(1)}, u32[]{:S(2)}, u32[]{:S(2)}) collective-permute-start(f32[128,256]{1,0:T(8,128)S(1)} %get-tuple-element.44), channel_id=1, source_target_pairs={{0,8},{4,12},{8,0},{12,4},{1,9},{5,13},{9,1},{13,5},{2,10},{6,14},... | collective-permute-start | bytes 393224 | tf_op jit(solution)/shard_map/ppermute | solution.py:481
  18.6 12.9 %collective-permute-start.6 = (f32[128,256]{1,0:T(8,128)S(1)}, f32[128,256]{1,0:T(8,128)S(1)}, u32[]{:S(2)}, u32[]{:S(2)}) collective-permute-start(f32[128,256]{1,0:T(8,128)S(1)} %get-tuple-element.45), channel_id=1, source_target_pairs={{0,4},{4,0},{8,12},{12,8},{1,5},{5,1},{9,13},{13,9},{2,6},{6,2},{1... | collective-permute-start | bytes 393224 | tf_op jit(solution)/shard_map/ppermute | solution.py:481
  21.1 10.4 %collective-permute-start.7 = (f32[128,256]{1,0:T(8,128)S(1)}, f32[128,256]{1,0:T(8,128)S(1)}, u32[]{:S(2)}, u32[]{:S(2)}) collective-permute-start(f32[128,256]{1,0:T(8,128)S(1)} %get-tuple-element.46), channel_id=1, source_target_pairs={{0,12},{4,8},{8,4},{12,0},{1,13},{5,9},{9,5},{13,1},{2,14},{6,10},... | collective-permute-start | bytes 393224 | tf_op jit(solution)/shard_map/ppermute | solution.py:481
  21.4 17.5 %copy-start = (s32[2,2]{1,0:T(2,128)S(1)}, s32[2,2]{1,0:T(2,128)}, u32[]{:S(2)}) copy-start(s32[2,2]{1,0:T(2,128)} %pairs_ref.1) | copy-start | bytes 52
  21.5 10.2 %collective-permute-start.8 = (f32[128,256]{1,0:T(8,128)S(1)}, f32[128,256]{1,0:T(8,128)S(1)}, u32[]{:S(2)}, u32[]{:S(2)}) collective-permute-start(f32[128,256]{1,0:T(8,128)S(1)} %sum_chips.2.field_ref.refs_0_), channel_id=1, source_target_pairs={{0,2},{2,0},{1,3},{3,1},{4,6},{6,4},{5,7},{7,5},{8,10},{10,8},{9,1... | collective-permute-start | bytes 393224 | tf_op jit(solution)/shard_map/ppermute | solution.py:481
  31.8 2.0 %collective-permute-start.9 = (f32[4,2,2,16,128]{4,3,2,1,0:T(8,128)S(1)}, f32[4,2,2,16,128]{4,3,2,1,0:T(8,128)S(1)}, u32[]{:S(2)}, u32[]{:S(2)}) collective-permute-start(f32[4,2,2,16,128]{4,3,2,1,0:T(8,128)S(1)} %get-tuple-element.49), channel_id=1, source_target_pairs={{0,1},{1,0},{2,3},{3,2},{4,5},{5,4},{6,7},{7,6},{8,9},{9,8},{10,11... | collective-permute-start | bytes 393224 | tf_op jit(solution)/shard_map/ppermute | solution.py:481
  31.9 7.1 %collective-permute-start.12 = (f32[128,256]{1,0:T(8,128)S(1)}, f32[128,256]{1,0:T(8,128)S(1)}, u32[]{:S(2)}, u32[]{:S(2)}) collective-permute-start(f32[128,256]{1,0:T(8,128)S(1)} %sum_chips.3.field_ref.refs_1_), channel_id=1, source_target_pairs={{0,2},{2,0},{1,3},{3,1},{4,6},{6,4},{5,7},{7,5},{8,10},{10,8},{9,1... | collective-permute-start | bytes 393224 | tf_op jit(solution)/shard_map/ppermute | solution.py:481
  33.8 12.2 %collective-permute-start.10 = (f32[2,2,2,16,128]{4,3,2,1,0:T(8,128)S(1)}, f32[2,2,2,16,128]{4,3,2,1,0:T(8,128)S(1)}, u32[]{:S(2)}, u32[]{:S(2)}) collective-permute-start(f32[2,2,2,16,128]{4,3,2,1,0:T(8,128)S(1)} %get-tuple-element.51), channel_id=1, source_target_pairs={{0,8},{4,12},{8,0},{12,4},{1,9},{5,13},{9,1},{13,5},{2,10},{6,14},... | collective-permute-start | bytes 196616 | tf_op jit(solution)/shard_map/ppermute | solution.py:481
  38.5 7.5 %collective-permute-start.11 = (f32[2,2,2,16,128]{4,3,2,1,0:T(8,128)S(1)}, f32[2,2,2,16,128]{4,3,2,1,0:T(8,128)S(1)}, u32[]{:S(2)}, u32[]{:S(2)}) collective-permute-start(f32[2,2,2,16,128]{4,3,2,1,0:T(8,128)S(1)} %get-tuple-element.52), channel_id=1, source_target_pairs={{0,12},{4,8},{8,4},{12,0},{1,13},{5,9},{9,5},{13,1},{2,14},{6,10},... | collective-permute-start | bytes 196616 | tf_op jit(solution)/shard_map/ppermute | solution.py:481
  40.1 1.4 %collective-permute-start.13 = (f32[4,2,2,16,128]{4,3,2,1,0:T(8,128)S(1)}, f32[4,2,2,16,128]{4,3,2,1,0:T(8,128)S(1)}, u32[]{:S(2)}, u32[]{:S(2)}) collective-permute-start(f32[4,2,2,16,128]{4,3,2,1,0:T(8,128)S(1)} %get-tuple-element.55), channel_id=1, source_target_pairs={{0,1},{1,0},{2,3},{3,2},{4,5},{5,4},{6,7},{7,6},{8,9},{9,8},{10,11... | collective-permute-start | bytes 393224 | tf_op jit(solution)/shard_map/ppermute | solution.py:481
  41.6 6.2 %collective-permute-start.14 = (f32[2,2,2,16,128]{4,3,2,1,0:T(8,128)S(1)}, f32[2,2,2,16,128]{4,3,2,1,0:T(8,128)S(1)}, u32[]{:S(2)}, u32[]{:S(2)}) collective-permute-start(f32[2,2,2,16,128]{4,3,2,1,0:T(8,128)S(1)} %get-tuple-element.59), channel_id=1, source_target_pairs={{0,12},{4,8},{8,4},{12,0},{1,13},{5,9},{9,5},{13,1},{2,14},{6,10},... | collective-permute-start | bytes 196616 | tf_op jit(solution)/shard_map/ppermute | solution.py:481
  45.0 6.8 %collective-permute-start.15 = (f32[2,2,2,16,128]{4,3,2,1,0:T(8,128)S(1)}, f32[2,2,2,16,128]{4,3,2,1,0:T(8,128)S(1)}, u32[]{:S(2)}, u32[]{:S(2)}) collective-permute-start(f32[2,2,2,16,128]{4,3,2,1,0:T(8,128)S(1)} %get-tuple-element.60), channel_id=1, source_target_pairs={{0,8},{4,12},{8,0},{12,4},{1,9},{5,13},{9,1},{13,5},{2,10},{6,14},... | collective-permute-start | bytes 196616 | tf_op jit(solution)/shard_map/ppermute | solution.py:481
  45.5 6.7 %collective-permute-start.16 = (f32[2,2,2,2,16,128]{5,4,3,2,1,0:T(8,128)S(1)}, f32[2,2,2,2,16,128]{5,4,3,2,1,0:T(8,128)S(1)}, u32[]{:S(2)}, u32[]{:S(2)}) collective-permute-start(f32[2,2,2,2,16,128]{5,4,3,2,1,0:T(8,128)S(1)} %get-tuple-element.61), channel_id=1, source_target_pairs={{0,4},{4,0},{8,12},{12,8},{1,5},{5,1},{9,13},{13,9},{2,6},{6,2},{1... | collective-permute-start | bytes 393224 | tf_op jit(solution)/shard_map/ppermute | solution.py:481

commit v5 on v4

--- a/solution.py
+++ b/solution.py
@@ -356,7 +356,7 @@
 
     outs = [pltpu.VMEM((spaces, 2, 2, nmode // (spaces * subs), nmode), F32)] * 2
     scratch = [pltpu.VMEM((2, nmode, nmode), F32)]
-    return small_call(kernel, outs, "split_rows", whole, field, scratch=scratch)
+    return small_call(kernel, outs, "split_rows", whole, field, scratch=scratch, flops=LARGE)
 
 
 def product_kernel(spaces, subs, tms, pairs_ref, *refs):
@@ -512,21 +512,25 @@
 
     away, keep = split_rows(whole, second, spaces, subs)
     meson = pair_cores(keep, swap(away, "sub", 1))
-    own, meson_near, two, three = meson
-    two, three = swap(two, "space", 2), swap(three, "space", 3)
+    own, near, two, three = meson
+    two, three, near = (swap(v, "space", s) for v, s in ((two, 2), (three, 3), (near, 1)))
     fields = [first, second, first_other, second_other]
     away, whole = product_rows(time_pairs, fields, spaces, subs, tms)
     got = swap(away, "sub", 1)
-    products = pair_with(meson_near, keep_rows(whole, spaces, subs), got)
-    places = [[(0, 0, None), (2, 1, None), (3, 2, None)], [(0, 3, None)]]
-    meson_parts = [own, two, three]
+    products = pair_cores(keep_rows(whole, spaces, subs), got)
+    places = [
+        [(0, 0, None), (1, 3, None), (2, 2, None), (3, 1, None)],
+        [(0, 4, None)],
+    ]
+    meson_parts = [own, three, two, near]
     own, near, two, three = products
     two, three, near = (swap(v, "space", s) for v, s in ((two, 2), (three, 3), (near, 1)))
-    arrays = put_blocks(
+    meson, products = put_blocks(
         meson_parts + [own], places, [None, None], spaces, subs, "put_early", LARGE
     )
-    places = [[(1, 2, 0)], [(1, 2, 1), (2, 1, None), (3, 0, None)]]
-    return put_blocks([three, two, near], places, arrays, spaces, subs, "put_late", 1)
+    places = [[(1, 1, None), (2, 0, None), (3, 2, None)]]
+    (products,) = put_blocks([two, near, three], places, [products], spaces, subs, "put_late", 1)
+    return meson, products
 
 
 def by_rows(sink, source, gamma_index, momenta, pattern, time_pairs, nmode, times, scale):

time: 53.1 us -> 52.6 us (level)
  waiting for transfers between devices: 15.5 us -> 14 us
  starting transfers between devices: 24.1 us -> 25.1 us
    ppermute x17 -> x18, waiting for transfers between devices: 15.5 us -> 14 us  [swap(): return lax.ppermute(value, axis, [(i, i ^ distance) for i in range(size)])]
    ppermute x17 -> x18, starting transfers between devices: 24.1 us -> 25.1 us  [swap(): return lax.ppermute(value, axis, [(i, i ^ distance) for i in range(size)])]
  transfers between devices with their start and end apart: 17 -> 18, of which waited for: 6 -> 5; matrix products, arithmetic and copies ran while one was open for 0% -> 0% of each run, Pallas kernels for 15% -> 15%
where the time goes in v5:
time: 52.6 us; the launch traced here: 52.4 us
  starting transfers between devices  25.1 us (48%)
  waiting for transfers between devices  14 us (27%)
  Pallas kernels  12.5 us (24%)
  between operations  0.83 us (2%)
    ppermute x18, starting transfers between devices, swap(): return lax.ppermute(value, axis, [(i, i ^ distance) for i in range(size)])  25.1 us
    ppermute x18, waiting for transfers between devices, swap(): return lax.ppermute(value, axis, [(i, i ^ distance) for i in range(size)])  14 us
    pallas_call x2, Pallas kernels, first_blocks(): pl.pallas_call(functools.partial(first_kernel, order, time, slots, chunks...  6.24 us
    pallas_call x2, Pallas kernels, later_blocks(): pl.pallas_call(functools.partial(later_kernel, order, time, slots), in_sp...  3.16 us
    pallas_call x2, Pallas kernels, put_blocks(): pl.pallas_call(kernel, in_specs=[pl.BlockSpec(memory_space=pltpu.HBM)] *...  1.52 us
    pallas_call x1, Pallas kernels, product_rows(): pl.pallas_call(functools.partial(product_kernel, spaces, subs, tms), in_s...  1.12 us
  transfers between devices with their start and end apart: 18, of which 5 were waited for; matrix products, arithmetic and copies ran while one was open for 0% of the time, Pallas kernels for 15%

profile of v5, /device:TPU:0, one launch (start us, length us, event | category | flops | bytes accessed | tf_op | source)
XLA Modules:
  0.0 52.4 jit_solution(535327493128723031)
XLA Ops:
  0.7 3.6 %first_blocks.2 = (f32[4,128,256]{2,1,0:T(8,128)S(1)}, bf16[256,3072]{1,0:T(8,128)(2,1)S(1)}, bf16[2,12,2,128,128]{4,3,2,1,0:T(8,128)(2,1)S(1)}, bf16[3072,128]{1,0:T(8,128)(2,1)S(1)}, bf16[3072,128]{1,0:T(8,128)(2,1)S(1)}) custom-call(bf16[2,3072,128]{2,1,0:T(8,128)(2,1)} %bitcast.7, bf16[2,3072,128]{2,1,0:T(8,128)(2,1)} %bitcast.8, s32[8]{0:T(128)} %gamma_ref.3, ...), custom_call_target="tpu_custom_call" | custom-call | flops 20132659200 | bytes 3145728 | tf_op jit(solution)/shard_map/first_blocks/pallas_call | solution.py:238
  4.2 0.5 collective-permute-start
  4.8 1.6 %later_blocks.2.keep_ref = f32[4,128,256]{2,1,0:T(8,128)S(1)} custom-call(s32[8]{0:T(128)S(1)} %copy-done.3, s32[2,128]{1,0:T(2,128)S(1)} %copy-done.1, bf16[256,3072]{1,0:T(8,128)(2,1)S(1)} %get-tuple-element.32.sink_mat, bf16[2,12,2,128,128]{4,3,2,1,0:T(8,128)(2,1)S(1)} %get-tuple-element.33.turned), custom_call_target="tpu_custom_call" | custom-call | flops 20132659200 | bytes 3145728 | tf_op jit(solution)/shard_map/later_blocks/pallas_call | solution.py:278
  6.4 0.1 add_cores.2
  6.4 4.0 %collective-permute-start.1 = (f32[128,256]{1,0:T(8,128)S(1)}, f32[128,256]{1,0:T(8,128)S(1)}, u32[]{:S(2)}, u32[]{:S(2)}) collective-permute-start(f32[128,256]{1,0:T(8,128)S(1)} %get-tuple-element.36), channel_id=1, source_target_pairs={{0,8},{4,12},{8,0},{12,4},{1,9},{5,13},{9,1},{13,5},{2,10},{6,14},... | collective-permute-start | bytes 393224 | tf_op jit(solution)/shard_map/ppermute | solution.py:481
  10.4 1.6 %collective-permute-start.2 = (f32[128,256]{1,0:T(8,128)S(1)}, f32[128,256]{1,0:T(8,128)S(1)}, u32[]{:S(2)}, u32[]{:S(2)}) collective-permute-start(f32[128,256]{1,0:T(8,128)S(1)} %get-tuple-element.37), channel_id=1, source_target_pairs={{0,4},{4,0},{8,12},{12,8},{1,5},{5,1},{9,13},{13,9},{2,6},{6,2},{1... | collective-permute-start | bytes 393224 | tf_op jit(solution)/shard_map/ppermute | solution.py:481
  12.0 2.7 %first_blocks.3 = (f32[4,128,256]{2,1,0:T(8,128)S(1)}, bf16[256,3072]{1,0:T(8,128)(2,1)S(1)}, bf16[2,12,2,128,128]{4,3,2,1,0:T(8,128)(2,1)S(1)}) custom-call(bf16[3072,128]{1,0:T(8,128)(2,1)S(1)} %get-tuple-element.39.refs_0_, bf16[3072,128]{1,0:T(8,128)(2,1)S(1)} %get-tuple-element.40.refs_1_, s32[8]{0:T(128)} %gamma_ref.3, s32[3,8]{1,0:T(4,128)} %bitcast.10, ...), custom_call_target="tpu_custom_call" | custom-call | flops 20132659200 | bytes 3145728 | tf_op jit(solution)/shard_map/first_blocks/pallas_call | solution.py:238
  14.6 0.1 collective-permute-start.4
  14.7 1.6 %later_blocks.3.keep_ref = f32[4,128,256]{2,1,0:T(8,128)S(1)} custom-call(s32[8]{0:T(128)S(1)} %copy-done.4, s32[2,128]{1,0:T(2,128)S(1)} %copy-done.2, bf16[256,3072]{1,0:T(8,128)(2,1)S(1)} %get-tuple-element.41.sink_mat, bf16[2,12,2,128,128]{4,3,2,1,0:T(8,128)(2,1)S(1)} %get-tuple-element.42.turned), custom_call_target="tpu_custom_call" | custom-call | flops 20132659200 | bytes 3145728 | tf_op jit(solution)/shard_map/later_blocks/pallas_call | solution.py:278
  16.3 0.3 collective-permute-done.4.got_ref
  16.6 0.1 add_cores.3
  16.7 2.0 %collective-permute-start.5 = (f32[128,256]{1,0:T(8,128)S(1)}, f32[128,256]{1,0:T(8,128)S(1)}, u32[]{:S(2)}, u32[]{:S(2)}) collective-permute-start(f32[128,256]{1,0:T(8,128)S(1)} %get-tuple-element.44), channel_id=1, source_target_pairs={{0,8},{4,12},{8,0},{12,4},{1,9},{5,13},{9,1},{13,5},{2,10},{6,14},... | collective-permute-start | bytes 393224 | tf_op jit(solution)/shard_map/ppermute | solution.py:481
  18.6 2.5 %collective-permute-start.6 = (f32[128,256]{1,0:T(8,128)S(1)}, f32[128,256]{1,0:T(8,128)S(1)}, u32[]{:S(2)}, u32[]{:S(2)}) collective-permute-start(f32[128,256]{1,0:T(8,128)S(1)} %get-tuple-element.45), channel_id=1, source_target_pairs={{0,4},{4,0},{8,12},{12,8},{1,5},{5,1},{9,13},{13,9},{2,6},{6,2},{1... | collective-permute-start | bytes 393224 | tf_op jit(solution)/shard_map/ppermute | solution.py:481
  21.1 0.3 collective-permute-start.7
  21.4 1.6 %collective-permute-start.8 = (f32[128,256]{1,0:T(8,128)S(1)}, f32[128,256]{1,0:T(8,128)S(1)}, u32[]{:S(2)}, u32[]{:S(2)}) collective-permute-start(f32[128,256]{1,0:T(8,128)S(1)} %sum_chips.2.field_ref.refs_0_), channel_id=1, source_target_pairs={{0,2},{2,0},{1,3},{3,1},{4,6},{6,4},{5,7},{7,5},{8,10},{10,8},{9,1... | collective-permute-start | bytes 393224 | tf_op jit(solution)/shard_map/ppermute | solution.py:481
  23.0 8.5 %collective-permute-done.5.refs_0_.refs_1_ = f32[128,256]{1,0:T(8,128)S(1)} collective-permute-done((f32[128,256]{1,0:T(8,128)S(1)}, f32[128,256]{1,0:T(8,128)S(1)}, u32[]{:S(2)}, u32[]{:S(2)}) %collective-permute-start.5) | collective-permute-done | bytes 131104 | tf_op jit(solution)/shard_map/ppermute | solution.py:481
  31.5 0.1 turn_field.1.refs_5_.whole_ref
  31.7 0.1 split_rows.1
  31.8 0.1 collective-permute-start.9
  31.9 1.9 %collective-permute-start.13 = (f32[128,256]{1,0:T(8,128)S(1)}, f32[128,256]{1,0:T(8,128)S(1)}, u32[]{:S(2)}, u32[]{:S(2)}) collective-permute-start(f32[128,256]{1,0:T(8,128)S(1)} %sum_chips.3.field_ref.refs_1_), channel_id=1, source_target_pairs={{0,2},{2,0},{1,3},{3,1},{4,6},{6,4},{5,7},{7,5},{8,10},{10,8},{9,1... | collective-permute-start | bytes 393224 | tf_op jit(solution)/shard_map/ppermute | solution.py:481
  33.8 2.9 %collective-permute-start.10 = (f32[2,2,2,16,128]{4,3,2,1,0:T(8,128)S(1)}, f32[2,2,2,16,128]{4,3,2,1,0:T(8,128)S(1)}, u32[]{:S(2)}, u32[]{:S(2)}) collective-permute-start(f32[2,2,2,16,128]{4,3,2,1,0:T(8,128)S(1)} %get-tuple-element.51), channel_id=1, source_target_pairs={{0,12},{4,8},{8,4},{12,0},{1,13},{5,9},{9,5},{13,1},{2,14},{6,10},... | collective-permute-start | bytes 196616 | tf_op jit(solution)/shard_map/ppermute | solution.py:481
  36.7 1.9 %collective-permute-start.11 = (f32[2,2,2,16,128]{4,3,2,1,0:T(8,128)S(1)}, f32[2,2,2,16,128]{4,3,2,1,0:T(8,128)S(1)}, u32[]{:S(2)}, u32[]{:S(2)}) collective-permute-start(f32[2,2,2,16,128]{4,3,2,1,0:T(8,128)S(1)} %get-tuple-element.52), channel_id=1, source_target_pairs={{0,8},{4,12},{8,0},{12,4},{1,9},{5,13},{9,1},{13,5},{2,10},{6,14},... | collective-permute-start | bytes 196616 | tf_op jit(solution)/shard_map/ppermute | solution.py:481
  38.6 0.5 collective-permute-start.12
  39.1 1.1 %products.1 = (f32[4,2,2,16,128]{4,3,2,1,0:T(8,128)S(1)}, f32[2,2,128,128]{3,2,1,0:T(8,128)S(1)}) custom-call(s32[2,2]{1,0:T(2,128)S(1)} %copy-done, f32[128,256]{1,0:T(8,128)S(1)} %sum_chips.2.field_ref.refs_0_, f32[128,256]{1,0:T(8,128)S(1)} %sum_chips.3.field_ref.refs_1_, f32[128,256]{1,0:T(8,128)S(1)} %collective-permute-done.8.refs_4_.refs_2_, ...), custom_call_target="tpu_custom_call" | custom-call | flops 33554432 | bytes 1048576 | tf_op jit(solution)/shard_map/products/pallas_call | solution.py:387
  40.2 0.1 collective-permute-start.14
  40.3 1.3 %collective-permute-done.14.got_ref = f32[4,2,2,16,128]{4,3,2,1,0:T(8,128)S(1)} collective-permute-done((f32[4,2,2,16,128]{4,3,2,1,0:T(8,128)S(1)}, f32[4,2,2,16,128]{4,3,2,1,0:T(8,128)S(1)}, u32[]{:S(2)}, u32[]{:S(2)}) %collective-permute-start.14) | collective-permute-done | bytes 131104 | tf_op jit(solution)/shard_map/ppermute | solution.py:481
  41.7 3.8 %collective-permute-start.15 = (f32[2,2,2,16,128]{4,3,2,1,0:T(8,128)S(1)}, f32[2,2,2,16,128]{4,3,2,1,0:T(8,128)S(1)}, u32[]{:S(2)}, u32[]{:S(2)}) collective-permute-start(f32[2,2,2,16,128]{4,3,2,1,0:T(8,128)S(1)} %get-tuple-element.59), channel_id=1, source_target_pairs={{0,8},{4,12},{8,0},{12,4},{1,9},{5,13},{9,1},{13,5},{2,10},{6,14},... | collective-permute-start | bytes 196616 | tf_op jit(solution)/shard_map/ppermute | solution.py:481
  45.4 1.5 %collective-permute-start.17 = (f32[2,2,2,16,128]{4,3,2,1,0:T(8,128)S(1)}, f32[2,2,2,16,128]{4,3,2,1,0:T(8,128)S(1)}, u32[]{:S(2)}, u32[]{:S(2)}) collective-permute-start(f32[2,2,2,16,128]{4,3,2,1,0:T(8,128)S(1)} %get-tuple-element.61), channel_id=1, source_target_pairs={{0,12},{4,8},{8,4},{12,0},{1,13},{5,9},{9,5},{13,1},{2,14},{6,10},... | collective-permute-start | bytes 196616 | tf_op jit(solution)/shard_map/ppermute | solution.py:481
  47.0 0.8 %put_early.1 = (f32[2,8,2,16,128]{4,3,2,1,0:T(8,128)}, f32[2,8,2,16,128]{4,3,2,1,0:T(8,128)}) custom-call(f32[2,2,2,16,128]{4,3,2,1,0:T(8,128)S(1)} %get-tuple-element.50.refs_0_, f32[2,2,2,16,128]{4,3,2,1,0:T(8,128)S(1)} %collective-permute-done.10.refs_1_, f32[2,2,2,16,128]{4,3,2,1,0:T(8,128)S(1)} %collective-permute-done.11.refs_2_, ...), custom_call_target="tpu_custom_call" | custom-call | flops 99999997952 | bytes 1 | tf_op jit(solution)/shard_map/put_early/pallas_call | solution.py:465
  47.8 1.6 %collective-permute-done.15.refs_1_ = f32[2,2,2,16,128]{4,3,2,1,0:T(8,128)S(1)} collective-permute-done((f32[2,2,2,16,128]{4,3,2,1,0:T(8,128)S(1)}, f32[2,2,2,16,128]{4,3,2,1,0:T(8,128)S(1)}, u32[]{:S(2)}, u32[]{:S(2)}) %collective-permute-start.15) | collective-permute-done | bytes 65568 | tf_op jit(solution)/shard_map/ppermute | solution.py:481
  49.4 2.4 %collective-permute-done.16.refs_2_ = f32[2,2,2,16,128]{4,3,2,1,0:T(8,128)S(1)} collective-permute-done((f32[2,2,2,16,128]{4,3,2,1,0:T(8,128)S(1)}, f32[2,2,2,16,128]{4,3,2,1,0:T(8,128)S(1)}, u32[]{:S(2)}, u32[]{:S(2)}) %collective-permute-start.16) | collective-permute-done | bytes 65568 | tf_op jit(solution)/shard_map/ppermute | solution.py:481
  51.7 0.7 %put_late.1 = f32[2,8,2,16,128]{4,3,2,1,0:T(8,128)} custom-call(f32[2,8,2,16,128]{4,3,2,1,0:T(8,128)} %get-tuple-element.58.refs_0_, f32[2,2,2,16,128]{4,3,2,1,0:T(8,128)S(1)} %collective-permute-done.15.refs_1_, f32[2,2,2,16,128]{4,3,2,1,0:T(8,128)S(1)} %collective-permute-done.16.refs_2_, ...), custom_call_target="tpu_custom_call", output_to_operand_aliasing={{}: (0, {})} | custom-call | flops 1 | bytes 1 | tf_op jit(solution)/shard_map/put_late/pallas_call | solution.py:465
  (30 shorter events, 0.2 us)
Async XLA Ops:
  0.6 4.1 %copy-start.1 = (s32[2,128]{1,0:T(2,128)S(1)}, s32[2,128]{1,0:T(2,128)}, u32[]{:S(2)}) copy-start(s32[2,128]{1,0:T(2,128)} %pattern_ref.3) | copy-start | bytes 3076
  0.6 4.1 %copy-start.3 = (s32[8]{0:T(128)S(1)}, s32[8]{0:T(128)}, u32[]{:S(2)}) copy-start(s32[8]{0:T(128)} %gamma_ref.3) | copy-start | bytes 100
  4.2 2.1 %collective-permute-start = (f32[4,128,256]{2,1,0:T(8,128)S(1)}, f32[4,128,256]{2,1,0:T(8,128)S(1)}, u32[]{:S(2)}, u32[]{:S(2)}) collective-permute-start(f32[4,128,256]{2,1,0:T(8,128)S(1)} %get-tuple-element.34), channel_id=1, source_target_pairs={{0,1},{1,0},{2,3},{3,2},{4,5},{5,4},{6,7},{7,6},{8,9},{9,8},{10,11... | collective-permute-start | bytes 1572872 | tf_op jit(solution)/shard_map/ppermute | solution.py:481
  6.4 14.7 %collective-permute-start.1 = (f32[128,256]{1,0:T(8,128)S(1)}, f32[128,256]{1,0:T(8,128)S(1)}, u32[]{:S(2)}, u32[]{:S(2)}) collective-permute-start(f32[128,256]{1,0:T(8,128)S(1)} %get-tuple-element.36), channel_id=1, source_target_pairs={{0,8},{4,12},{8,0},{12,4},{1,9},{5,13},{9,1},{13,5},{2,10},{6,14},... | collective-permute-start | bytes 393224 | tf_op jit(solution)/shard_map/ppermute | solution.py:481
  10.4 11.0 %collective-permute-start.2 = (f32[128,256]{1,0:T(8,128)S(1)}, f32[128,256]{1,0:T(8,128)S(1)}, u32[]{:S(2)}, u32[]{:S(2)}) collective-permute-start(f32[128,256]{1,0:T(8,128)S(1)} %get-tuple-element.37), channel_id=1, source_target_pairs={{0,4},{4,0},{8,12},{12,8},{1,5},{5,1},{9,13},{13,9},{2,6},{6,2},{1... | collective-permute-start | bytes 393224 | tf_op jit(solution)/shard_map/ppermute | solution.py:481
  12.0 9.5 %collective-permute-start.3 = (f32[128,256]{1,0:T(8,128)S(1)}, f32[128,256]{1,0:T(8,128)S(1)}, u32[]{:S(2)}, u32[]{:S(2)}) collective-permute-start(f32[128,256]{1,0:T(8,128)S(1)} %get-tuple-element.38), channel_id=1, source_target_pairs={{0,12},{4,8},{8,4},{12,0},{1,13},{5,9},{9,5},{13,1},{2,14},{6,10},... | collective-permute-start | bytes 393224 | tf_op jit(solution)/shard_map/ppermute | solution.py:481
  12.0 2.8 %copy-start.2 = (s32[2,128]{1,0:T(2,128)S(1)}, s32[2,128]{1,0:T(2,128)}, u32[]{:S(2)}) copy-start(s32[2,128]{1,0:T(2,128)} %pattern_ref.3) | copy-start | bytes 3076
  12.0 2.8 %copy-start.4 = (s32[8]{0:T(128)S(1)}, s32[8]{0:T(128)}, u32[]{:S(2)}) copy-start(s32[8]{0:T(128)} %gamma_ref.3) | copy-start | bytes 100
  14.6 2.0 %collective-permute-start.4 = (f32[4,128,256]{2,1,0:T(8,128)S(1)}, f32[4,128,256]{2,1,0:T(8,128)S(1)}, u32[]{:S(2)}, u32[]{:S(2)}) collective-permute-start(f32[4,128,256]{2,1,0:T(8,128)S(1)} %get-tuple-element.43), channel_id=1, source_target_pairs={{0,1},{1,0},{2,3},{3,2},{4,5},{5,4},{6,7},{7,6},{8,9},{9,8},{10,11... | collective-permute-start | bytes 1572872 | tf_op jit(solution)/shard_map/ppermute | solution.py:481
  16.7 14.8 %collective-permute-start.5 = (f32[128,256]{1,0:T(8,128)S(1)}, f32[128,256]{1,0:T(8,128)S(1)}, u32[]{:S(2)}, u32[]{:S(2)}) collective-permute-start(f32[128,256]{1,0:T(8,128)S(1)} %get-tuple-element.44), channel_id=1, source_target_pairs={{0,8},{4,12},{8,0},{12,4},{1,9},{5,13},{9,1},{13,5},{2,10},{6,14},... | collective-permute-start | bytes 393224 | tf_op jit(solution)/shard_map/ppermute | solution.py:481
  18.6 12.9 %collective-permute-start.6 = (f32[128,256]{1,0:T(8,128)S(1)}, f32[128,256]{1,0:T(8,128)S(1)}, u32[]{:S(2)}, u32[]{:S(2)}) collective-permute-start(f32[128,256]{1,0:T(8,128)S(1)} %get-tuple-element.45), channel_id=1, source_target_pairs={{0,4},{4,0},{8,12},{12,8},{1,5},{5,1},{9,13},{13,9},{2,6},{6,2},{1... | collective-permute-start | bytes 393224 | tf_op jit(solution)/shard_map/ppermute | solution.py:481
  21.1 10.4 %collective-permute-start.7 = (f32[128,256]{1,0:T(8,128)S(1)}, f32[128,256]{1,0:T(8,128)S(1)}, u32[]{:S(2)}, u32[]{:S(2)}) collective-permute-start(f32[128,256]{1,0:T(8,128)S(1)} %get-tuple-element.46), channel_id=1, source_target_pairs={{0,12},{4,8},{8,4},{12,0},{1,13},{5,9},{9,5},{13,1},{2,14},{6,10},... | collective-permute-start | bytes 393224 | tf_op jit(solution)/shard_map/ppermute | solution.py:481
  21.4 10.2 %collective-permute-start.8 = (f32[128,256]{1,0:T(8,128)S(1)}, f32[128,256]{1,0:T(8,128)S(1)}, u32[]{:S(2)}, u32[]{:S(2)}) collective-permute-start(f32[128,256]{1,0:T(8,128)S(1)} %sum_chips.2.field_ref.refs_0_), channel_id=1, source_target_pairs={{0,2},{2,0},{1,3},{3,1},{4,6},{6,4},{5,7},{7,5},{8,10},{10,8},{9,1... | collective-permute-start | bytes 393224 | tf_op jit(solution)/shard_map/ppermute | solution.py:481
  31.7 7.5 %copy-start = (s32[2,2]{1,0:T(2,128)S(1)}, s32[2,2]{1,0:T(2,128)}, u32[]{:S(2)}) copy-start(s32[2,2]{1,0:T(2,128)} %pairs_ref.1) | copy-start | bytes 52
  31.8 2.0 %collective-permute-start.9 = (f32[4,2,2,16,128]{4,3,2,1,0:T(8,128)S(1)}, f32[4,2,2,16,128]{4,3,2,1,0:T(8,128)S(1)}, u32[]{:S(2)}, u32[]{:S(2)}) collective-permute-start(f32[4,2,2,16,128]{4,3,2,1,0:T(8,128)S(1)} %get-tuple-element.49), channel_id=1, source_target_pairs={{0,1},{1,0},{2,3},{3,2},{4,5},{5,4},{6,7},{7,6},{8,9},{9,8},{10,11... | collective-permute-start | bytes 393224 | tf_op jit(solution)/shard_map/ppermute | solution.py:481
  31.9 7.2 %collective-permute-start.13 = (f32[128,256]{1,0:T(8,128)S(1)}, f32[128,256]{1,0:T(8,128)S(1)}, u32[]{:S(2)}, u32[]{:S(2)}) collective-permute-start(f32[128,256]{1,0:T(8,128)S(1)} %sum_chips.3.field_ref.refs_1_), channel_id=1, source_target_pairs={{0,2},{2,0},{1,3},{3,1},{4,6},{6,4},{5,7},{7,5},{8,10},{10,8},{9,1... | collective-permute-start | bytes 393224 | tf_op jit(solution)/shard_map/ppermute | solution.py:481
  33.8 11.6 %collective-permute-start.10 = (f32[2,2,2,16,128]{4,3,2,1,0:T(8,128)S(1)}, f32[2,2,2,16,128]{4,3,2,1,0:T(8,128)S(1)}, u32[]{:S(2)}, u32[]{:S(2)}) collective-permute-start(f32[2,2,2,16,128]{4,3,2,1,0:T(8,128)S(1)} %get-tuple-element.51), channel_id=1, source_target_pairs={{0,12},{4,8},{8,4},{12,0},{1,13},{5,9},{9,5},{13,1},{2,14},{6,10},... | collective-permute-start | bytes 196616 | tf_op jit(solution)/shard_map/ppermute | solution.py:481
  36.7 10.3 %collective-permute-start.11 = (f32[2,2,2,16,128]{4,3,2,1,0:T(8,128)S(1)}, f32[2,2,2,16,128]{4,3,2,1,0:T(8,128)S(1)}, u32[]{:S(2)}, u32[]{:S(2)}) collective-permute-start(f32[2,2,2,16,128]{4,3,2,1,0:T(8,128)S(1)} %get-tuple-element.52), channel_id=1, source_target_pairs={{0,8},{4,12},{8,0},{12,4},{1,9},{5,13},{9,1},{13,5},{2,10},{6,14},... | collective-permute-start | bytes 196616 | tf_op jit(solution)/shard_map/ppermute | solution.py:481
  38.6 8.4 %collective-permute-start.12 = (f32[2,2,2,16,128]{4,3,2,1,0:T(8,128)S(1)}, f32[2,2,2,16,128]{4,3,2,1,0:T(8,128)S(1)}, u32[]{:S(2)}, u32[]{:S(2)}) collective-permute-start(f32[2,2,2,16,128]{4,3,2,1,0:T(8,128)S(1)} %get-tuple-element.53), channel_id=1, source_target_pairs={{0,4},{4,0},{8,12},{12,8},{1,5},{5,1},{9,13},{13,9},{2,6},{6,2},{1... | collective-permute-start | bytes 196616 | tf_op jit(solution)/shard_map/ppermute | solution.py:481
  40.2 1.4 %collective-permute-start.14 = (f32[4,2,2,16,128]{4,3,2,1,0:T(8,128)S(1)}, f32[4,2,2,16,128]{4,3,2,1,0:T(8,128)S(1)}, u32[]{:S(2)}, u32[]{:S(2)}) collective-permute-start(f32[4,2,2,16,128]{4,3,2,1,0:T(8,128)S(1)} %get-tuple-element.55), channel_id=1, source_target_pairs={{0,1},{1,0},{2,3},{3,2},{4,5},{5,4},{6,7},{7,6},{8,9},{9,8},{10,11... | collective-permute-start | bytes 393224 | tf_op jit(solution)/shard_map/ppermute | solution.py:481
  41.7 7.7 %collective-permute-start.15 = (f32[2,2,2,16,128]{4,3,2,1,0:T(8,128)S(1)}, f32[2,2,2,16,128]{4,3,2,1,0:T(8,128)S(1)}, u32[]{:S(2)}, u32[]{:S(2)}) collective-permute-start(f32[2,2,2,16,128]{4,3,2,1,0:T(8,128)S(1)} %get-tuple-element.59), channel_id=1, source_target_pairs={{0,8},{4,12},{8,0},{12,4},{1,9},{5,13},{9,1},{13,5},{2,10},{6,14},... | collective-permute-start | bytes 196616 | tf_op jit(solution)/shard_map/ppermute | solution.py:481
  45.4 6.3 %collective-permute-start.16 = (f32[2,2,2,16,128]{4,3,2,1,0:T(8,128)S(1)}, f32[2,2,2,16,128]{4,3,2,1,0:T(8,128)S(1)}, u32[]{:S(2)}, u32[]{:S(2)}) collective-permute-start(f32[2,2,2,16,128]{4,3,2,1,0:T(8,128)S(1)} %get-tuple-element.60), channel_id=1, source_target_pairs={{0,4},{4,0},{8,12},{12,8},{1,5},{5,1},{9,13},{13,9},{2,6},{6,2},{1... | collective-permute-start | bytes 196616 | tf_op jit(solution)/shard_map/ppermute | solution.py:481
  45.4 6.3 %collective-permute-start.17 = (f32[2,2,2,16,128]{4,3,2,1,0:T(8,128)S(1)}, f32[2,2,2,16,128]{4,3,2,1,0:T(8,128)S(1)}, u32[]{:S(2)}, u32[]{:S(2)}) collective-permute-start(f32[2,2,2,16,128]{4,3,2,1,0:T(8,128)S(1)} %get-tuple-element.61), channel_id=1, source_target_pairs={{0,12},{4,8},{8,4},{12,0},{1,13},{5,9},{9,5},{13,1},{2,14},{6,10},... | collective-permute-start | bytes 196616 | tf_op jit(solution)/shard_map/ppermute | solution.py:481

commit v6 on v5

--- a/solution.py
+++ b/solution.py
@@ -15,7 +15,7 @@
 BF16 = jnp.bfloat16
 VMEM_LIMIT = 16 * 2**20
 SMALL_LIMIT = 4 * 2**20
-ROUND = ((2, 1, 3), (2, 1, 3))
+ROUND = ((3, 1, 2), (2, 1, 3))
 LARGE = 10**11
 
 
@@ -421,22 +421,6 @@
     return small_call(kernel, outs, "pair_cores", keep, got)
 
 
-def pair_with(near, keep, got):
-    shape = keep.shape
-
-    def kernel(near_ref, keep_ref, got_ref, *outs):
-        outs[1][0] = near_ref[...]
-        for s, out in enumerate(outs):
-            out = out.at[1] if s == 1 else out
-            out[0] = keep_ref[s]
-            out[1] = got_ref[s]
-
-    outs = [
-        pltpu.VMEM(((2,) if s == 1 else ()) + (2,) + shape[1:], F32) for s in range(shape[0])
-    ]
-    return small_call(kernel, outs, "pair_cores", near, keep, got)
-
-
 def put_blocks(args, places, arrays, spaces, subs, name, flops):
     lanes, _, row_count, nmode = args[0].shape[-4:]
     count = len(arrays)

time: 52.6 us -> 51.8 us (0.985)
  starting transfers between devices: 25.1 us -> 23.4 us
  waiting for transfers between devices: 14 us -> 14.9 us
    ppermute x18, starting transfers between devices: 25.1 us -> 23.4 us  [swap(): return lax.ppermute(value, axis, [(i, i ^ distance) for i in range(size)])]
    ppermute x18, waiting for transfers between devices: 14 us -> 14.9 us  [swap(): return lax.ppermute(value, axis, [(i, i ^ distance) for i in range(size)])]
  transfers between devices with their start and end apart: 18 -> 18, of which waited for: 5 -> 7; matrix products, arithmetic and copies ran while one was open for 0% -> 0% of each run, Pallas kernels for 15% -> 15%
where the time goes in v6:
time: 51.8 us; the launch traced here: 51.6 us
  starting transfers between devices  23.4 us (45%)
  waiting for transfers between devices  14.9 us (29%)
  Pallas kernels  12.5 us (24%)
  between operations  0.83 us (2%)
    ppermute x18, starting transfers between devices, swap(): return lax.ppermute(value, axis, [(i, i ^ distance) for i in range(size)])  23.4 us
    ppermute x18, waiting for transfers between devices, swap(): return lax.ppermute(value, axis, [(i, i ^ distance) for i in range(size)])  14.9 us
    pallas_call x2, Pallas kernels, first_blocks(): pl.pallas_call(functools.partial(first_kernel, order, time, slots, chunks...  6.24 us
    pallas_call x2, Pallas kernels, later_blocks(): pl.pallas_call(functools.partial(later_kernel, order, time, slots), in_sp...  3.16 us
    pallas_call x2, Pallas kernels, put_blocks(): pl.pallas_call(kernel, in_specs=[pl.BlockSpec(memory_space=pltpu.HBM)] *...  1.52 us
    pallas_call x1, Pallas kernels, product_rows(): pl.pallas_call(functools.partial(product_kernel, spaces, subs, tms), in_s...  1.12 us
  transfers between devices with their start and end apart: 18, of which 7 were waited for; matrix products, arithmetic and copies ran while one was open for 0% of the time, Pallas kernels for 15%

profile of v6, /device:TPU:0, one launch (start us, length us, event | category | flops | bytes accessed | tf_op | source)
XLA Modules:
  0.0 51.6 jit_solution(6022024227299343485)
XLA Ops:
  0.7 3.6 %first_blocks.2 = (f32[4,128,256]{2,1,0:T(8,128)S(1)}, bf16[256,3072]{1,0:T(8,128)(2,1)S(1)}, bf16[2,12,2,128,128]{4,3,2,1,0:T(8,128)(2,1)S(1)}, bf16[3072,128]{1,0:T(8,128)(2,1)S(1)}, bf16[3072,128]{1,0:T(8,128)(2,1)S(1)}) custom-call(bf16[2,3072,128]{2,1,0:T(8,128)(2,1)} %bitcast.7, bf16[2,3072,128]{2,1,0:T(8,128)(2,1)} %bitcast.8, s32[8]{0:T(128)} %gamma_ref.3, ...), custom_call_target="tpu_custom_call" | custom-call | flops 20132659200 | bytes 3145728 | tf_op jit(solution)/shard_map/first_blocks/pallas_call | solution.py:238
  4.2 0.5 %collective-permute-start = (f32[4,128,256]{2,1,0:T(8,128)S(1)}, f32[4,128,256]{2,1,0:T(8,128)S(1)}, u32[]{:S(2)}, u32[]{:S(2)}) collective-permute-start(f32[4,128,256]{2,1,0:T(8,128)S(1)} %get-tuple-element.34), channel_id=1, source_target_pairs={{0,1},{1,0},{2,3},{3,2},{4,5},{5,4},{6,7},{7,6},{8,9},{9,8},{10,11... | collective-permute-start | bytes 1572872 | tf_op jit(solution)/shard_map/ppermute | solution.py:465
  4.8 1.6 %later_blocks.2.keep_ref = f32[4,128,256]{2,1,0:T(8,128)S(1)} custom-call(s32[8]{0:T(128)S(1)} %copy-done.3, s32[2,128]{1,0:T(2,128)S(1)} %copy-done.1, bf16[256,3072]{1,0:T(8,128)(2,1)S(1)} %get-tuple-element.32.sink_mat, bf16[2,12,2,128,128]{4,3,2,1,0:T(8,128)(2,1)S(1)} %get-tuple-element.33.turned), custom_call_target="tpu_custom_call" | custom-call | flops 20132659200 | bytes 3145728 | tf_op jit(solution)/shard_map/later_blocks/pallas_call | solution.py:278
  6.4 5.0 %collective-permute-start.1 = (f32[128,256]{1,0:T(8,128)S(1)}, f32[128,256]{1,0:T(8,128)S(1)}, u32[]{:S(2)}, u32[]{:S(2)}) collective-permute-start(f32[128,256]{1,0:T(8,128)S(1)} %get-tuple-element.36), channel_id=1, source_target_pairs={{0,12},{4,8},{8,4},{12,0},{1,13},{5,9},{9,5},{13,1},{2,14},{6,10},... | collective-permute-start | bytes 393224 | tf_op jit(solution)/shard_map/ppermute | solution.py:465
  11.4 0.6 %collective-permute-start.3 = (f32[128,256]{1,0:T(8,128)S(1)}, f32[128,256]{1,0:T(8,128)S(1)}, u32[]{:S(2)}, u32[]{:S(2)}) collective-permute-start(f32[128,256]{1,0:T(8,128)S(1)} %get-tuple-element.38), channel_id=1, source_target_pairs={{0,8},{4,12},{8,0},{12,4},{1,9},{5,13},{9,1},{13,5},{2,10},{6,14},... | collective-permute-start | bytes 393224 | tf_op jit(solution)/shard_map/ppermute | solution.py:465
  12.0 2.7 %first_blocks.3 = (f32[4,128,256]{2,1,0:T(8,128)S(1)}, bf16[256,3072]{1,0:T(8,128)(2,1)S(1)}, bf16[2,12,2,128,128]{4,3,2,1,0:T(8,128)(2,1)S(1)}) custom-call(bf16[3072,128]{1,0:T(8,128)(2,1)S(1)} %get-tuple-element.39.refs_0_, bf16[3072,128]{1,0:T(8,128)(2,1)S(1)} %get-tuple-element.40.refs_1_, s32[8]{0:T(128)} %gamma_ref.3, s32[3,8]{1,0:T(4,128)} %bitcast.10, ...), custom_call_target="tpu_custom_call" | custom-call | flops 20132659200 | bytes 3145728 | tf_op jit(solution)/shard_map/first_blocks/pallas_call | solution.py:238
  14.7 0.1 collective-permute-start.4
  14.8 1.6 %later_blocks.3.keep_ref = f32[4,128,256]{2,1,0:T(8,128)S(1)} custom-call(s32[8]{0:T(128)S(1)} %copy-done.4, s32[2,128]{1,0:T(2,128)S(1)} %copy-done.2, bf16[256,3072]{1,0:T(8,128)(2,1)S(1)} %get-tuple-element.41.sink_mat, bf16[2,12,2,128,128]{4,3,2,1,0:T(8,128)(2,1)S(1)} %get-tuple-element.42.turned), custom_call_target="tpu_custom_call" | custom-call | flops 20132659200 | bytes 3145728 | tf_op jit(solution)/shard_map/later_blocks/pallas_call | solution.py:278
  16.4 0.3 collective-permute-done.4.got_ref
  16.7 2.3 %collective-permute-start.5 = (f32[128,256]{1,0:T(8,128)S(1)}, f32[128,256]{1,0:T(8,128)S(1)}, u32[]{:S(2)}, u32[]{:S(2)}) collective-permute-start(f32[128,256]{1,0:T(8,128)S(1)} %get-tuple-element.44), channel_id=1, source_target_pairs={{0,8},{4,12},{8,0},{12,4},{1,9},{5,13},{9,1},{13,5},{2,10},{6,14},... | collective-permute-start | bytes 393224 | tf_op jit(solution)/shard_map/ppermute | solution.py:465
  19.1 2.0 %collective-permute-start.6 = (f32[128,256]{1,0:T(8,128)S(1)}, f32[128,256]{1,0:T(8,128)S(1)}, u32[]{:S(2)}, u32[]{:S(2)}) collective-permute-start(f32[128,256]{1,0:T(8,128)S(1)} %get-tuple-element.45), channel_id=1, source_target_pairs={{0,4},{4,0},{8,12},{12,8},{1,5},{5,1},{9,13},{13,9},{2,6},{6,2},{1... | collective-permute-start | bytes 393224 | tf_op jit(solution)/shard_map/ppermute | solution.py:465
  21.1 0.1 collective-permute-start.7
  21.2 5.3 %collective-permute-done.3.refs_3_ = f32[128,256]{1,0:T(8,128)S(1)} collective-permute-done((f32[128,256]{1,0:T(8,128)S(1)}, f32[128,256]{1,0:T(8,128)S(1)}, u32[]{:S(2)}, u32[]{:S(2)}) %collective-permute-start.3) | collective-permute-done | bytes 131104 | tf_op jit(solution)/shard_map/ppermute | solution.py:465
  26.5 1.6 %collective-permute-start.8 = (f32[128,256]{1,0:T(8,128)S(1)}, f32[128,256]{1,0:T(8,128)S(1)}, u32[]{:S(2)}, u32[]{:S(2)}) collective-permute-start(f32[128,256]{1,0:T(8,128)S(1)} %sum_chips.2.field_ref.refs_0_), channel_id=1, source_target_pairs={{0,2},{2,0},{1,3},{3,1},{4,6},{6,4},{5,7},{7,5},{8,10},{10,8},{9,1... | collective-permute-start | bytes 393224 | tf_op jit(solution)/shard_map/ppermute | solution.py:465
  28.1 4.0 %collective-permute-done.5.refs_0_.refs_1_ = f32[128,256]{1,0:T(8,128)S(1)} collective-permute-done((f32[128,256]{1,0:T(8,128)S(1)}, f32[128,256]{1,0:T(8,128)S(1)}, u32[]{:S(2)}, u32[]{:S(2)}) %collective-permute-start.5) | collective-permute-done | bytes 131104 | tf_op jit(solution)/shard_map/ppermute | solution.py:465
  32.0 0.1 turn_field.1.refs_5_.whole_ref
  32.2 0.1 split_rows.1
  32.3 0.1 collective-permute-start.9
  32.4 1.6 %collective-permute-start.13 = (f32[128,256]{1,0:T(8,128)S(1)}, f32[128,256]{1,0:T(8,128)S(1)}, u32[]{:S(2)}, u32[]{:S(2)}) collective-permute-start(f32[128,256]{1,0:T(8,128)S(1)} %sum_chips.3.field_ref.refs_1_), channel_id=1, source_target_pairs={{0,2},{2,0},{1,3},{3,1},{4,6},{6,4},{5,7},{7,5},{8,10},{10,8},{9,1... | collective-permute-start | bytes 393224 | tf_op jit(solution)/shard_map/ppermute | solution.py:465
  34.0 2.5 %collective-permute-start.10 = (f32[2,2,2,16,128]{4,3,2,1,0:T(8,128)S(1)}, f32[2,2,2,16,128]{4,3,2,1,0:T(8,128)S(1)}, u32[]{:S(2)}, u32[]{:S(2)}) collective-permute-start(f32[2,2,2,16,128]{4,3,2,1,0:T(8,128)S(1)} %get-tuple-element.51), channel_id=1, source_target_pairs={{0,12},{4,8},{8,4},{12,0},{1,13},{5,9},{9,5},{13,1},{2,14},{6,10},... | collective-permute-start | bytes 196616 | tf_op jit(solution)/shard_map/ppermute | solution.py:465
  36.5 1.7 %collective-permute-start.11 = (f32[2,2,2,16,128]{4,3,2,1,0:T(8,128)S(1)}, f32[2,2,2,16,128]{4,3,2,1,0:T(8,128)S(1)}, u32[]{:S(2)}, u32[]{:S(2)}) collective-permute-start(f32[2,2,2,16,128]{4,3,2,1,0:T(8,128)S(1)} %get-tuple-element.52), channel_id=1, source_target_pairs={{0,8},{4,12},{8,0},{12,4},{1,9},{5,13},{9,1},{13,5},{2,10},{6,14},... | collective-permute-start | bytes 196616 | tf_op jit(solution)/shard_map/ppermute | solution.py:465
  38.1 0.3 collective-permute-start.12
  38.4 1.1 %products.1 = (f32[4,2,2,16,128]{4,3,2,1,0:T(8,128)S(1)}, f32[2,2,128,128]{3,2,1,0:T(8,128)S(1)}) custom-call(s32[2,2]{1,0:T(2,128)S(1)} %copy-done, f32[128,256]{1,0:T(8,128)S(1)} %sum_chips.2.field_ref.refs_0_, f32[128,256]{1,0:T(8,128)S(1)} %sum_chips.3.field_ref.refs_1_, f32[128,256]{1,0:T(8,128)S(1)} %collective-permute-done.8.refs_4_.refs_2_, ...), custom_call_target="tpu_custom_call" | custom-call | flops 33554432 | bytes 1048576 | tf_op jit(solution)/shard_map/products/pallas_call | solution.py:387
  39.6 0.1 collective-permute-start.14
  39.7 1.3 %collective-permute-done.14.got_ref = f32[4,2,2,16,128]{4,3,2,1,0:T(8,128)S(1)} collective-permute-done((f32[4,2,2,16,128]{4,3,2,1,0:T(8,128)S(1)}, f32[4,2,2,16,128]{4,3,2,1,0:T(8,128)S(1)}, u32[]{:S(2)}, u32[]{:S(2)}) %collective-permute-start.14) | collective-permute-done | bytes 131104 | tf_op jit(solution)/shard_map/ppermute | solution.py:465
  41.0 3.5 %collective-permute-start.15 = (f32[2,2,2,16,128]{4,3,2,1,0:T(8,128)S(1)}, f32[2,2,2,16,128]{4,3,2,1,0:T(8,128)S(1)}, u32[]{:S(2)}, u32[]{:S(2)}) collective-permute-start(f32[2,2,2,16,128]{4,3,2,1,0:T(8,128)S(1)} %get-tuple-element.59), channel_id=1, source_target_pairs={{0,8},{4,12},{8,0},{12,4},{1,9},{5,13},{9,1},{13,5},{2,10},{6,14},... | collective-permute-start | bytes 196616 | tf_op jit(solution)/shard_map/ppermute | solution.py:465
  44.5 1.5 %collective-permute-start.17 = (f32[2,2,2,16,128]{4,3,2,1,0:T(8,128)S(1)}, f32[2,2,2,16,128]{4,3,2,1,0:T(8,128)S(1)}, u32[]{:S(2)}, u32[]{:S(2)}) collective-permute-start(f32[2,2,2,16,128]{4,3,2,1,0:T(8,128)S(1)} %get-tuple-element.61), channel_id=1, source_target_pairs={{0,12},{4,8},{8,4},{12,0},{1,13},{5,9},{9,5},{13,1},{2,14},{6,10},... | collective-permute-start | bytes 196616 | tf_op jit(solution)/shard_map/ppermute | solution.py:465
  46.1 0.8 %put_early.1 = (f32[2,8,2,16,128]{4,3,2,1,0:T(8,128)}, f32[2,8,2,16,128]{4,3,2,1,0:T(8,128)}) custom-call(f32[2,2,2,16,128]{4,3,2,1,0:T(8,128)S(1)} %get-tuple-element.50.refs_0_, f32[2,2,2,16,128]{4,3,2,1,0:T(8,128)S(1)} %collective-permute-done.10.refs_1_, f32[2,2,2,16,128]{4,3,2,1,0:T(8,128)S(1)} %collective-permute-done.11.refs_2_, ...), custom_call_target="tpu_custom_call" | custom-call | flops 99999997952 | bytes 1 | tf_op jit(solution)/shard_map/put_early/pallas_call | solution.py:449
  46.9 0.9 %collective-permute-done.15.refs_1_ = f32[2,2,2,16,128]{4,3,2,1,0:T(8,128)S(1)} collective-permute-done((f32[2,2,2,16,128]{4,3,2,1,0:T(8,128)S(1)}, f32[2,2,2,16,128]{4,3,2,1,0:T(8,128)S(1)}, u32[]{:S(2)}, u32[]{:S(2)}) %collective-permute-start.15) | collective-permute-done | bytes 65568 | tf_op jit(solution)/shard_map/ppermute | solution.py:465
  47.8 1.0 %collective-permute-done.16.refs_2_ = f32[2,2,2,16,128]{4,3,2,1,0:T(8,128)S(1)} collective-permute-done((f32[2,2,2,16,128]{4,3,2,1,0:T(8,128)S(1)}, f32[2,2,2,16,128]{4,3,2,1,0:T(8,128)S(1)}, u32[]{:S(2)}, u32[]{:S(2)}) %collective-permute-start.16) | collective-permute-done | bytes 65568 | tf_op jit(solution)/shard_map/ppermute | solution.py:465
  48.8 2.1 %collective-permute-done.17.refs_3_ = f32[2,2,2,16,128]{4,3,2,1,0:T(8,128)S(1)} collective-permute-done((f32[2,2,2,16,128]{4,3,2,1,0:T(8,128)S(1)}, f32[2,2,2,16,128]{4,3,2,1,0:T(8,128)S(1)}, u32[]{:S(2)}, u32[]{:S(2)}) %collective-permute-start.17) | collective-permute-done | bytes 65568 | tf_op jit(solution)/shard_map/ppermute | solution.py:465
  50.9 0.7 %put_late.1 = f32[2,8,2,16,128]{4,3,2,1,0:T(8,128)} custom-call(f32[2,8,2,16,128]{4,3,2,1,0:T(8,128)} %get-tuple-element.58.refs_0_, f32[2,2,2,16,128]{4,3,2,1,0:T(8,128)S(1)} %collective-permute-done.15.refs_1_, f32[2,2,2,16,128]{4,3,2,1,0:T(8,128)S(1)} %collective-permute-done.16.refs_2_, ...), custom_call_target="tpu_custom_call", output_to_operand_aliasing={{}: (0, {})} | custom-call | flops 1 | bytes 1 | tf_op jit(solution)/shard_map/put_late/pallas_call | solution.py:449
  (30 shorter events, 0.3 us)
Async XLA Ops:
  0.6 4.1 %copy-start.1 = (s32[2,128]{1,0:T(2,128)S(1)}, s32[2,128]{1,0:T(2,128)}, u32[]{:S(2)}) copy-start(s32[2,128]{1,0:T(2,128)} %pattern_ref.3) | copy-start | bytes 3076
  0.6 4.1 %copy-start.3 = (s32[8]{0:T(128)S(1)}, s32[8]{0:T(128)}, u32[]{:S(2)}) copy-start(s32[8]{0:T(128)} %gamma_ref.3) | copy-start | bytes 100
  4.2 2.1 %collective-permute-start = (f32[4,128,256]{2,1,0:T(8,128)S(1)}, f32[4,128,256]{2,1,0:T(8,128)S(1)}, u32[]{:S(2)}, u32[]{:S(2)}) collective-permute-start(f32[4,128,256]{2,1,0:T(8,128)S(1)} %get-tuple-element.34), channel_id=1, source_target_pairs={{0,1},{1,0},{2,3},{3,2},{4,5},{5,4},{6,7},{7,6},{8,9},{9,8},{10,11... | collective-permute-start | bytes 1572872 | tf_op jit(solution)/shard_map/ppermute | solution.py:465
  6.4 14.7 %collective-permute-start.1 = (f32[128,256]{1,0:T(8,128)S(1)}, f32[128,256]{1,0:T(8,128)S(1)}, u32[]{:S(2)}, u32[]{:S(2)}) collective-permute-start(f32[128,256]{1,0:T(8,128)S(1)} %get-tuple-element.36), channel_id=1, source_target_pairs={{0,12},{4,8},{8,4},{12,0},{1,13},{5,9},{9,5},{13,1},{2,14},{6,10},... | collective-permute-start | bytes 393224 | tf_op jit(solution)/shard_map/ppermute | solution.py:465
  11.4 9.8 %collective-permute-start.2 = (f32[128,256]{1,0:T(8,128)S(1)}, f32[128,256]{1,0:T(8,128)S(1)}, u32[]{:S(2)}, u32[]{:S(2)}) collective-permute-start(f32[128,256]{1,0:T(8,128)S(1)} %get-tuple-element.37), channel_id=1, source_target_pairs={{0,4},{4,0},{8,12},{12,8},{1,5},{5,1},{9,13},{13,9},{2,6},{6,2},{1... | collective-permute-start | bytes 393224 | tf_op jit(solution)/shard_map/ppermute | solution.py:465
  11.4 15.1 %collective-permute-start.3 = (f32[128,256]{1,0:T(8,128)S(1)}, f32[128,256]{1,0:T(8,128)S(1)}, u32[]{:S(2)}, u32[]{:S(2)}) collective-permute-start(f32[128,256]{1,0:T(8,128)S(1)} %get-tuple-element.38), channel_id=1, source_target_pairs={{0,8},{4,12},{8,0},{12,4},{1,9},{5,13},{9,1},{13,5},{2,10},{6,14},... | collective-permute-start | bytes 393224 | tf_op jit(solution)/shard_map/ppermute | solution.py:465
  12.0 2.8 %copy-start.2 = (s32[2,128]{1,0:T(2,128)S(1)}, s32[2,128]{1,0:T(2,128)}, u32[]{:S(2)}) copy-start(s32[2,128]{1,0:T(2,128)} %pattern_ref.3) | copy-start | bytes 3076
  12.0 2.8 %copy-start.4 = (s32[8]{0:T(128)S(1)}, s32[8]{0:T(128)}, u32[]{:S(2)}) copy-start(s32[8]{0:T(128)} %gamma_ref.3) | copy-start | bytes 100
  14.7 2.0 %collective-permute-start.4 = (f32[4,128,256]{2,1,0:T(8,128)S(1)}, f32[4,128,256]{2,1,0:T(8,128)S(1)}, u32[]{:S(2)}, u32[]{:S(2)}) collective-permute-start(f32[4,128,256]{2,1,0:T(8,128)S(1)} %get-tuple-element.43), channel_id=1, source_target_pairs={{0,1},{1,0},{2,3},{3,2},{4,5},{5,4},{6,7},{7,6},{8,9},{9,8},{10,11... | collective-permute-start | bytes 1572872 | tf_op jit(solution)/shard_map/ppermute | solution.py:465
  16.7 15.3 %collective-permute-start.5 = (f32[128,256]{1,0:T(8,128)S(1)}, f32[128,256]{1,0:T(8,128)S(1)}, u32[]{:S(2)}, u32[]{:S(2)}) collective-permute-start(f32[128,256]{1,0:T(8,128)S(1)} %get-tuple-element.44), channel_id=1, source_target_pairs={{0,8},{4,12},{8,0},{12,4},{1,9},{5,13},{9,1},{13,5},{2,10},{6,14},... | collective-permute-start | bytes 393224 | tf_op jit(solution)/shard_map/ppermute | solution.py:465
  19.1 13.0 %collective-permute-start.6 = (f32[128,256]{1,0:T(8,128)S(1)}, f32[128,256]{1,0:T(8,128)S(1)}, u32[]{:S(2)}, u32[]{:S(2)}) collective-permute-start(f32[128,256]{1,0:T(8,128)S(1)} %get-tuple-element.45), channel_id=1, source_target_pairs={{0,4},{4,0},{8,12},{12,8},{1,5},{5,1},{9,13},{13,9},{2,6},{6,2},{1... | collective-permute-start | bytes 393224 | tf_op jit(solution)/shard_map/ppermute | solution.py:465
  21.1 10.9 %collective-permute-start.7 = (f32[128,256]{1,0:T(8,128)S(1)}, f32[128,256]{1,0:T(8,128)S(1)}, u32[]{:S(2)}, u32[]{:S(2)}) collective-permute-start(f32[128,256]{1,0:T(8,128)S(1)} %get-tuple-element.46), channel_id=1, source_target_pairs={{0,12},{4,8},{8,4},{12,0},{1,13},{5,9},{9,5},{13,1},{2,14},{6,10},... | collective-permute-start | bytes 393224 | tf_op jit(solution)/shard_map/ppermute | solution.py:465
  26.5 5.6 %collective-permute-start.8 = (f32[128,256]{1,0:T(8,128)S(1)}, f32[128,256]{1,0:T(8,128)S(1)}, u32[]{:S(2)}, u32[]{:S(2)}) collective-permute-start(f32[128,256]{1,0:T(8,128)S(1)} %sum_chips.2.field_ref.refs_0_), channel_id=1, source_target_pairs={{0,2},{2,0},{1,3},{3,1},{4,6},{6,4},{5,7},{7,5},{8,10},{10,8},{9,1... | collective-permute-start | bytes 393224 | tf_op jit(solution)/shard_map/ppermute | solution.py:465
  32.2 6.2 %copy-start = (s32[2,2]{1,0:T(2,128)S(1)}, s32[2,2]{1,0:T(2,128)}, u32[]{:S(2)}) copy-start(s32[2,2]{1,0:T(2,128)} %pairs_ref.1) | copy-start | bytes 52
  32.3 1.6 %collective-permute-start.9 = (f32[4,2,2,16,128]{4,3,2,1,0:T(8,128)S(1)}, f32[4,2,2,16,128]{4,3,2,1,0:T(8,128)S(1)}, u32[]{:S(2)}, u32[]{:S(2)}) collective-permute-start(f32[4,2,2,16,128]{4,3,2,1,0:T(8,128)S(1)} %get-tuple-element.49), channel_id=1, source_target_pairs={{0,1},{1,0},{2,3},{3,2},{4,5},{5,4},{6,7},{7,6},{8,9},{9,8},{10,11... | collective-permute-start | bytes 393224 | tf_op jit(solution)/shard_map/ppermute | solution.py:465
  32.4 6.0 %collective-permute-start.13 = (f32[128,256]{1,0:T(8,128)S(1)}, f32[128,256]{1,0:T(8,128)S(1)}, u32[]{:S(2)}, u32[]{:S(2)}) collective-permute-start(f32[128,256]{1,0:T(8,128)S(1)} %sum_chips.3.field_ref.refs_1_), channel_id=1, source_target_pairs={{0,2},{2,0},{1,3},{3,1},{4,6},{6,4},{5,7},{7,5},{8,10},{10,8},{9,1... | collective-permute-start | bytes 393224 | tf_op jit(solution)/shard_map/ppermute | solution.py:465
  34.0 10.6 %collective-permute-start.10 = (f32[2,2,2,16,128]{4,3,2,1,0:T(8,128)S(1)}, f32[2,2,2,16,128]{4,3,2,1,0:T(8,128)S(1)}, u32[]{:S(2)}, u32[]{:S(2)}) collective-permute-start(f32[2,2,2,16,128]{4,3,2,1,0:T(8,128)S(1)} %get-tuple-element.51), channel_id=1, source_target_pairs={{0,12},{4,8},{8,4},{12,0},{1,13},{5,9},{9,5},{13,1},{2,14},{6,10},... | collective-permute-start | bytes 196616 | tf_op jit(solution)/shard_map/ppermute | solution.py:465
  36.5 9.6 %collective-permute-start.11 = (f32[2,2,2,16,128]{4,3,2,1,0:T(8,128)S(1)}, f32[2,2,2,16,128]{4,3,2,1,0:T(8,128)S(1)}, u32[]{:S(2)}, u32[]{:S(2)}) collective-permute-start(f32[2,2,2,16,128]{4,3,2,1,0:T(8,128)S(1)} %get-tuple-element.52), channel_id=1, source_target_pairs={{0,8},{4,12},{8,0},{12,4},{1,9},{5,13},{9,1},{13,5},{2,10},{6,14},... | collective-permute-start | bytes 196616 | tf_op jit(solution)/shard_map/ppermute | solution.py:465
  38.1 8.0 %collective-permute-start.12 = (f32[2,2,2,16,128]{4,3,2,1,0:T(8,128)S(1)}, f32[2,2,2,16,128]{4,3,2,1,0:T(8,128)S(1)}, u32[]{:S(2)}, u32[]{:S(2)}) collective-permute-start(f32[2,2,2,16,128]{4,3,2,1,0:T(8,128)S(1)} %get-tuple-element.53), channel_id=1, source_target_pairs={{0,4},{4,0},{8,12},{12,8},{1,5},{5,1},{9,13},{13,9},{2,6},{6,2},{1... | collective-permute-start | bytes 196616 | tf_op jit(solution)/shard_map/ppermute | solution.py:465
  39.6 1.4 %collective-permute-start.14 = (f32[4,2,2,16,128]{4,3,2,1,0:T(8,128)S(1)}, f32[4,2,2,16,128]{4,3,2,1,0:T(8,128)S(1)}, u32[]{:S(2)}, u32[]{:S(2)}) collective-permute-start(f32[4,2,2,16,128]{4,3,2,1,0:T(8,128)S(1)} %get-tuple-element.55), channel_id=1, source_target_pairs={{0,1},{1,0},{2,3},{3,2},{4,5},{5,4},{6,7},{7,6},{8,9},{9,8},{10,11... | collective-permute-start | bytes 393224 | tf_op jit(solution)/shard_map/ppermute | solution.py:465
  41.0 6.8 %collective-permute-start.15 = (f32[2,2,2,16,128]{4,3,2,1,0:T(8,128)S(1)}, f32[2,2,2,16,128]{4,3,2,1,0:T(8,128)S(1)}, u32[]{:S(2)}, u32[]{:S(2)}) collective-permute-start(f32[2,2,2,16,128]{4,3,2,1,0:T(8,128)S(1)} %get-tuple-element.59), channel_id=1, source_target_pairs={{0,8},{4,12},{8,0},{12,4},{1,9},{5,13},{9,1},{13,5},{2,10},{6,14},... | collective-permute-start | bytes 196616 | tf_op jit(solution)/shard_map/ppermute | solution.py:465
  44.5 4.3 %collective-permute-start.16 = (f32[2,2,2,16,128]{4,3,2,1,0:T(8,128)S(1)}, f32[2,2,2,16,128]{4,3,2,1,0:T(8,128)S(1)}, u32[]{:S(2)}, u32[]{:S(2)}) collective-permute-start(f32[2,2,2,16,128]{4,3,2,1,0:T(8,128)S(1)} %get-tuple-element.60), channel_id=1, source_target_pairs={{0,4},{4,0},{8,12},{12,8},{1,5},{5,1},{9,13},{13,9},{2,6},{6,2},{1... | collective-permute-start | bytes 196616 | tf_op jit(solution)/shard_map/ppermute | solution.py:465
  44.5 6.4 %collective-permute-start.17 = (f32[2,2,2,16,128]{4,3,2,1,0:T(8,128)S(1)}, f32[2,2,2,16,128]{4,3,2,1,0:T(8,128)S(1)}, u32[]{:S(2)}, u32[]{:S(2)}) collective-permute-start(f32[2,2,2,16,128]{4,3,2,1,0:T(8,128)S(1)} %get-tuple-element.61), channel_id=1, source_target_pairs={{0,12},{4,8},{8,4},{12,0},{1,13},{5,9},{9,5},{13,1},{2,14},{6,10},... | collective-permute-start | bytes 196616 | tf_op jit(solution)/shard_map/ppermute | solution.py:465

commit v7 on v6

--- a/solution.py
+++ b/solution.py
@@ -359,6 +359,18 @@
     return small_call(kernel, outs, "split_rows", whole, field, scratch=scratch, flops=LARGE)
 
 
+def split_dot(a, b):
+    a_high, b_high = a.astype(BF16), b.astype(BF16)
+    a_low = (a - a_high.astype(F32)).astype(BF16)
+    b_low = (b - b_high.astype(F32)).astype(BF16)
+
+    def dot(x, y):
+        return lax.dot_general(x, y, (((1,), (0,)), ((), ())), preferred_element_type=F32)
+
+    small = dot(a_low, b_low) + dot(a_low, b_high) + dot(a_high, b_low)
+    return small + dot(a_high, b_high)
+
+
 def product_kernel(spaces, subs, tms, pairs_ref, *refs):
     fields, (away, whole, held) = refs[:-3], refs[-3:]
     nmode = fields[0].shape[0]
@@ -370,13 +382,9 @@
     for pair in range(pairs_ref.shape[0]):
         left, right = held[pairs_ref[pair, 0]], held[pairs_ref[pair, 1]]
         swapped = jnp.concatenate([-left[:, nmode:], left[:, :nmode]], axis=1)
-        result = lax.dot_general(
-            right,
-            jnp.concatenate([left, swapped], axis=0),
-            (((1,), (0,)), ((), ())),
-            preferred_element_type=F32,
-            precision=lax.Precision.HIGHEST,
-        ) * (1.0 / math.sqrt(nmode))
+        result = split_dot(right, jnp.concatenate([left, swapped], axis=0)) * (
+            1.0 / math.sqrt(nmode)
+        )
         turn(result, whole.at[pair])
         write_rows(whole.at[pair], pair, spaces, subs, [1], [away])
 

time: 51.8 us -> 51.7 us (level)
  no operation moved by 1% of the time
where the time goes in v7:
time: 51.7 us; the launch traced here: 51.5 us
  starting transfers between devices  23.4 us (45%)
  waiting for transfers between devices  14.9 us (29%)
  Pallas kernels  12.4 us (24%)
  between operations  0.83 us (2%)
    ppermute x18, starting transfers between devices, swap(): return lax.ppermute(value, axis, [(i, i ^ distance) for i in range(size)])  23.4 us
    ppermute x18, waiting for transfers between devices, swap(): return lax.ppermute(value, axis, [(i, i ^ distance) for i in range(size)])  14.9 us
    pallas_call x2, Pallas kernels, first_blocks(): pl.pallas_call(functools.partial(first_kernel, order, time, slots, chunks...  6.24 us
    pallas_call x2, Pallas kernels, later_blocks(): pl.pallas_call(functools.partial(later_kernel, order, time, slots), in_sp...  3.16 us
    pallas_call x2, Pallas kernels, put_blocks(): pl.pallas_call(kernel, in_specs=[pl.BlockSpec(memory_space=pltpu.HBM)] *...  1.52 us
  transfers between devices with their start and end apart: 18, of which 7 were waited for; matrix products, arithmetic and copies ran while one was open for 0% of the time, Pallas kernels for 15%

profile of v7, /device:TPU:0, one launch (start us, length us, event | category | flops | bytes accessed | tf_op | source)
XLA Modules:
  0.0 51.5 jit_solution(7675455219556424386)
XLA Ops:
  0.7 3.6 %first_blocks.2 = (f32[4,128,256]{2,1,0:T(8,128)S(1)}, bf16[256,3072]{1,0:T(8,128)(2,1)S(1)}, bf16[2,12,2,128,128]{4,3,2,1,0:T(8,128)(2,1)S(1)}, bf16[3072,128]{1,0:T(8,128)(2,1)S(1)}, bf16[3072,128]{1,0:T(8,128)(2,1)S(1)}) custom-call(bf16[2,3072,128]{2,1,0:T(8,128)(2,1)} %bitcast.7, bf16[2,3072,128]{2,1,0:T(8,128)(2,1)} %bitcast.8, s32[8]{0:T(128)} %gamma_ref.3, ...), custom_call_target="tpu_custom_call" | custom-call | flops 20132659200 | bytes 3145728 | tf_op jit(solution)/shard_map/first_blocks/pallas_call | solution.py:238
  4.2 0.5 %collective-permute-start = (f32[4,128,256]{2,1,0:T(8,128)S(1)}, f32[4,128,256]{2,1,0:T(8,128)S(1)}, u32[]{:S(2)}, u32[]{:S(2)}) collective-permute-start(f32[4,128,256]{2,1,0:T(8,128)S(1)} %get-tuple-element.34), channel_id=1, source_target_pairs={{0,1},{1,0},{2,3},{3,2},{4,5},{5,4},{6,7},{7,6},{8,9},{9,8},{10,11... | collective-permute-start | bytes 1572872 | tf_op jit(solution)/shard_map/ppermute | solution.py:473
  4.8 1.6 %later_blocks.2.keep_ref = f32[4,128,256]{2,1,0:T(8,128)S(1)} custom-call(s32[8]{0:T(128)S(1)} %copy-done.3, s32[2,128]{1,0:T(2,128)S(1)} %copy-done.1, bf16[256,3072]{1,0:T(8,128)(2,1)S(1)} %get-tuple-element.32.sink_mat, bf16[2,12,2,128,128]{4,3,2,1,0:T(8,128)(2,1)S(1)} %get-tuple-element.33.turned), custom_call_target="tpu_custom_call" | custom-call | flops 20132659200 | bytes 3145728 | tf_op jit(solution)/shard_map/later_blocks/pallas_call | solution.py:278
  6.4 5.0 %collective-permute-start.1 = (f32[128,256]{1,0:T(8,128)S(1)}, f32[128,256]{1,0:T(8,128)S(1)}, u32[]{:S(2)}, u32[]{:S(2)}) collective-permute-start(f32[128,256]{1,0:T(8,128)S(1)} %get-tuple-element.36), channel_id=1, source_target_pairs={{0,12},{4,8},{8,4},{12,0},{1,13},{5,9},{9,5},{13,1},{2,14},{6,10},... | collective-permute-start | bytes 393224 | tf_op jit(solution)/shard_map/ppermute | solution.py:473
  11.4 0.6 %collective-permute-start.3 = (f32[128,256]{1,0:T(8,128)S(1)}, f32[128,256]{1,0:T(8,128)S(1)}, u32[]{:S(2)}, u32[]{:S(2)}) collective-permute-start(f32[128,256]{1,0:T(8,128)S(1)} %get-tuple-element.38), channel_id=1, source_target_pairs={{0,8},{4,12},{8,0},{12,4},{1,9},{5,13},{9,1},{13,5},{2,10},{6,14},... | collective-permute-start | bytes 393224 | tf_op jit(solution)/shard_map/ppermute | solution.py:473
  12.0 2.7 %first_blocks.3 = (f32[4,128,256]{2,1,0:T(8,128)S(1)}, bf16[256,3072]{1,0:T(8,128)(2,1)S(1)}, bf16[2,12,2,128,128]{4,3,2,1,0:T(8,128)(2,1)S(1)}) custom-call(bf16[3072,128]{1,0:T(8,128)(2,1)S(1)} %get-tuple-element.39.refs_0_, bf16[3072,128]{1,0:T(8,128)(2,1)S(1)} %get-tuple-element.40.refs_1_, s32[8]{0:T(128)} %gamma_ref.3, s32[3,8]{1,0:T(4,128)} %bitcast.10, ...), custom_call_target="tpu_custom_call" | custom-call | flops 20132659200 | bytes 3145728 | tf_op jit(solution)/shard_map/first_blocks/pallas_call | solution.py:238
  14.7 0.1 collective-permute-start.4
  14.8 1.6 %later_blocks.3.keep_ref = f32[4,128,256]{2,1,0:T(8,128)S(1)} custom-call(s32[8]{0:T(128)S(1)} %copy-done.4, s32[2,128]{1,0:T(2,128)S(1)} %copy-done.2, bf16[256,3072]{1,0:T(8,128)(2,1)S(1)} %get-tuple-element.41.sink_mat, bf16[2,12,2,128,128]{4,3,2,1,0:T(8,128)(2,1)S(1)} %get-tuple-element.42.turned), custom_call_target="tpu_custom_call" | custom-call | flops 20132659200 | bytes 3145728 | tf_op jit(solution)/shard_map/later_blocks/pallas_call | solution.py:278
  16.4 0.3 collective-permute-done.4.got_ref
  16.7 2.3 %collective-permute-start.5 = (f32[128,256]{1,0:T(8,128)S(1)}, f32[128,256]{1,0:T(8,128)S(1)}, u32[]{:S(2)}, u32[]{:S(2)}) collective-permute-start(f32[128,256]{1,0:T(8,128)S(1)} %get-tuple-element.44), channel_id=1, source_target_pairs={{0,8},{4,12},{8,0},{12,4},{1,9},{5,13},{9,1},{13,5},{2,10},{6,14},... | collective-permute-start | bytes 393224 | tf_op jit(solution)/shard_map/ppermute | solution.py:473
  19.1 2.0 %collective-permute-start.6 = (f32[128,256]{1,0:T(8,128)S(1)}, f32[128,256]{1,0:T(8,128)S(1)}, u32[]{:S(2)}, u32[]{:S(2)}) collective-permute-start(f32[128,256]{1,0:T(8,128)S(1)} %get-tuple-element.45), channel_id=1, source_target_pairs={{0,4},{4,0},{8,12},{12,8},{1,5},{5,1},{9,13},{13,9},{2,6},{6,2},{1... | collective-permute-start | bytes 393224 | tf_op jit(solution)/shard_map/ppermute | solution.py:473
  21.1 0.1 collective-permute-start.7
  21.2 5.3 %collective-permute-done.3.refs_3_ = f32[128,256]{1,0:T(8,128)S(1)} collective-permute-done((f32[128,256]{1,0:T(8,128)S(1)}, f32[128,256]{1,0:T(8,128)S(1)}, u32[]{:S(2)}, u32[]{:S(2)}) %collective-permute-start.3) | collective-permute-done | bytes 131104 | tf_op jit(solution)/shard_map/ppermute | solution.py:473
  26.5 1.6 %collective-permute-start.8 = (f32[128,256]{1,0:T(8,128)S(1)}, f32[128,256]{1,0:T(8,128)S(1)}, u32[]{:S(2)}, u32[]{:S(2)}) collective-permute-start(f32[128,256]{1,0:T(8,128)S(1)} %sum_chips.2.field_ref.refs_0_), channel_id=1, source_target_pairs={{0,2},{2,0},{1,3},{3,1},{4,6},{6,4},{5,7},{7,5},{8,10},{10,8},{9,1... | collective-permute-start | bytes 393224 | tf_op jit(solution)/shard_map/ppermute | solution.py:473
  28.1 4.0 %collective-permute-done.5.refs_0_.refs_1_ = f32[128,256]{1,0:T(8,128)S(1)} collective-permute-done((f32[128,256]{1,0:T(8,128)S(1)}, f32[128,256]{1,0:T(8,128)S(1)}, u32[]{:S(2)}, u32[]{:S(2)}) %collective-permute-start.5) | collective-permute-done | bytes 131104 | tf_op jit(solution)/shard_map/ppermute | solution.py:473
  32.0 0.1 turn_field.1.refs_5_.whole_ref
  32.2 0.1 split_rows.1
  32.3 0.1 collective-permute-start.9
  32.4 1.6 %collective-permute-start.13 = (f32[128,256]{1,0:T(8,128)S(1)}, f32[128,256]{1,0:T(8,128)S(1)}, u32[]{:S(2)}, u32[]{:S(2)}) collective-permute-start(f32[128,256]{1,0:T(8,128)S(1)} %sum_chips.3.field_ref.refs_1_), channel_id=1, source_target_pairs={{0,2},{2,0},{1,3},{3,1},{4,6},{6,4},{5,7},{7,5},{8,10},{10,8},{9,1... | collective-permute-start | bytes 393224 | tf_op jit(solution)/shard_map/ppermute | solution.py:473
  34.0 2.5 %collective-permute-start.10 = (f32[2,2,2,16,128]{4,3,2,1,0:T(8,128)S(1)}, f32[2,2,2,16,128]{4,3,2,1,0:T(8,128)S(1)}, u32[]{:S(2)}, u32[]{:S(2)}) collective-permute-start(f32[2,2,2,16,128]{4,3,2,1,0:T(8,128)S(1)} %get-tuple-element.51), channel_id=1, source_target_pairs={{0,12},{4,8},{8,4},{12,0},{1,13},{5,9},{9,5},{13,1},{2,14},{6,10},... | collective-permute-start | bytes 196616 | tf_op jit(solution)/shard_map/ppermute | solution.py:473
  36.5 1.7 %collective-permute-start.11 = (f32[2,2,2,16,128]{4,3,2,1,0:T(8,128)S(1)}, f32[2,2,2,16,128]{4,3,2,1,0:T(8,128)S(1)}, u32[]{:S(2)}, u32[]{:S(2)}) collective-permute-start(f32[2,2,2,16,128]{4,3,2,1,0:T(8,128)S(1)} %get-tuple-element.52), channel_id=1, source_target_pairs={{0,8},{4,12},{8,0},{12,4},{1,9},{5,13},{9,1},{13,5},{2,10},{6,14},... | collective-permute-start | bytes 196616 | tf_op jit(solution)/shard_map/ppermute | solution.py:473
  38.1 0.3 collective-permute-start.12
  38.4 1.0 %products.1 = (f32[4,2,2,16,128]{4,3,2,1,0:T(8,128)S(1)}, f32[2,2,128,128]{3,2,1,0:T(8,128)S(1)}) custom-call(s32[2,2]{1,0:T(2,128)S(1)} %copy-done, f32[128,256]{1,0:T(8,128)S(1)} %sum_chips.2.field_ref.refs_0_, f32[128,256]{1,0:T(8,128)S(1)} %sum_chips.3.field_ref.refs_1_, f32[128,256]{1,0:T(8,128)S(1)} %collective-permute-done.8.refs_4_.refs_2_, ...), custom_call_target="tpu_custom_call" | custom-call | flops 33554432 | bytes 1048576 | tf_op jit(solution)/shard_map/products/pallas_call | solution.py:395
  39.5 0.1 collective-permute-start.14
  39.6 1.3 %collective-permute-done.14.got_ref = f32[4,2,2,16,128]{4,3,2,1,0:T(8,128)S(1)} collective-permute-done((f32[4,2,2,16,128]{4,3,2,1,0:T(8,128)S(1)}, f32[4,2,2,16,128]{4,3,2,1,0:T(8,128)S(1)}, u32[]{:S(2)}, u32[]{:S(2)}) %collective-permute-start.14) | collective-permute-done | bytes 131104 | tf_op jit(solution)/shard_map/ppermute | solution.py:473
  40.9 3.5 %collective-permute-start.15 = (f32[2,2,2,16,128]{4,3,2,1,0:T(8,128)S(1)}, f32[2,2,2,16,128]{4,3,2,1,0:T(8,128)S(1)}, u32[]{:S(2)}, u32[]{:S(2)}) collective-permute-start(f32[2,2,2,16,128]{4,3,2,1,0:T(8,128)S(1)} %get-tuple-element.59), channel_id=1, source_target_pairs={{0,8},{4,12},{8,0},{12,4},{1,9},{5,13},{9,1},{13,5},{2,10},{6,14},... | collective-permute-start | bytes 196616 | tf_op jit(solution)/shard_map/ppermute | solution.py:473
  44.4 1.5 %collective-permute-start.17 = (f32[2,2,2,16,128]{4,3,2,1,0:T(8,128)S(1)}, f32[2,2,2,16,128]{4,3,2,1,0:T(8,128)S(1)}, u32[]{:S(2)}, u32[]{:S(2)}) collective-permute-start(f32[2,2,2,16,128]{4,3,2,1,0:T(8,128)S(1)} %get-tuple-element.61), channel_id=1, source_target_pairs={{0,12},{4,8},{8,4},{12,0},{1,13},{5,9},{9,5},{13,1},{2,14},{6,10},... | collective-permute-start | bytes 196616 | tf_op jit(solution)/shard_map/ppermute | solution.py:473
  46.0 0.8 %put_early.1 = (f32[2,8,2,16,128]{4,3,2,1,0:T(8,128)}, f32[2,8,2,16,128]{4,3,2,1,0:T(8,128)}) custom-call(f32[2,2,2,16,128]{4,3,2,1,0:T(8,128)S(1)} %get-tuple-element.50.refs_0_, f32[2,2,2,16,128]{4,3,2,1,0:T(8,128)S(1)} %collective-permute-done.10.refs_1_, f32[2,2,2,16,128]{4,3,2,1,0:T(8,128)S(1)} %collective-permute-done.11.refs_2_, ...), custom_call_target="tpu_custom_call" | custom-call | flops 99999997952 | bytes 1 | tf_op jit(solution)/shard_map/put_early/pallas_call | solution.py:457
  46.8 0.9 %collective-permute-done.15.refs_1_ = f32[2,2,2,16,128]{4,3,2,1,0:T(8,128)S(1)} collective-permute-done((f32[2,2,2,16,128]{4,3,2,1,0:T(8,128)S(1)}, f32[2,2,2,16,128]{4,3,2,1,0:T(8,128)S(1)}, u32[]{:S(2)}, u32[]{:S(2)}) %collective-permute-start.15) | collective-permute-done | bytes 65568 | tf_op jit(solution)/shard_map/ppermute | solution.py:473
  47.7 1.0 %collective-permute-done.16.refs_2_ = f32[2,2,2,16,128]{4,3,2,1,0:T(8,128)S(1)} collective-permute-done((f32[2,2,2,16,128]{4,3,2,1,0:T(8,128)S(1)}, f32[2,2,2,16,128]{4,3,2,1,0:T(8,128)S(1)}, u32[]{:S(2)}, u32[]{:S(2)}) %collective-permute-start.16) | collective-permute-done | bytes 65568 | tf_op jit(solution)/shard_map/ppermute | solution.py:473
  48.7 2.1 %collective-permute-done.17.refs_3_ = f32[2,2,2,16,128]{4,3,2,1,0:T(8,128)S(1)} collective-permute-done((f32[2,2,2,16,128]{4,3,2,1,0:T(8,128)S(1)}, f32[2,2,2,16,128]{4,3,2,1,0:T(8,128)S(1)}, u32[]{:S(2)}, u32[]{:S(2)}) %collective-permute-start.17) | collective-permute-done | bytes 65568 | tf_op jit(solution)/shard_map/ppermute | solution.py:473
  50.8 0.7 %put_late.1 = f32[2,8,2,16,128]{4,3,2,1,0:T(8,128)} custom-call(f32[2,8,2,16,128]{4,3,2,1,0:T(8,128)} %get-tuple-element.58.refs_0_, f32[2,2,2,16,128]{4,3,2,1,0:T(8,128)S(1)} %collective-permute-done.15.refs_1_, f32[2,2,2,16,128]{4,3,2,1,0:T(8,128)S(1)} %collective-permute-done.16.refs_2_, ...), custom_call_target="tpu_custom_call", output_to_operand_aliasing={{}: (0, {})} | custom-call | flops 1 | bytes 1 | tf_op jit(solution)/shard_map/put_late/pallas_call | solution.py:457
  (30 shorter events, 0.3 us)
Async XLA Ops:
  0.6 4.1 %copy-start.1 = (s32[2,128]{1,0:T(2,128)S(1)}, s32[2,128]{1,0:T(2,128)}, u32[]{:S(2)}) copy-start(s32[2,128]{1,0:T(2,128)} %pattern_ref.3) | copy-start | bytes 3076
  0.6 4.1 %copy-start.3 = (s32[8]{0:T(128)S(1)}, s32[8]{0:T(128)}, u32[]{:S(2)}) copy-start(s32[8]{0:T(128)} %gamma_ref.3) | copy-start | bytes 100
  4.2 2.1 %collective-permute-start = (f32[4,128,256]{2,1,0:T(8,128)S(1)}, f32[4,128,256]{2,1,0:T(8,128)S(1)}, u32[]{:S(2)}, u32[]{:S(2)}) collective-permute-start(f32[4,128,256]{2,1,0:T(8,128)S(1)} %get-tuple-element.34), channel_id=1, source_target_pairs={{0,1},{1,0},{2,3},{3,2},{4,5},{5,4},{6,7},{7,6},{8,9},{9,8},{10,11... | collective-permute-start | bytes 1572872 | tf_op jit(solution)/shard_map/ppermute | solution.py:473
  6.4 14.7 %collective-permute-start.1 = (f32[128,256]{1,0:T(8,128)S(1)}, f32[128,256]{1,0:T(8,128)S(1)}, u32[]{:S(2)}, u32[]{:S(2)}) collective-permute-start(f32[128,256]{1,0:T(8,128)S(1)} %get-tuple-element.36), channel_id=1, source_target_pairs={{0,12},{4,8},{8,4},{12,0},{1,13},{5,9},{9,5},{13,1},{2,14},{6,10},... | collective-permute-start | bytes 393224 | tf_op jit(solution)/shard_map/ppermute | solution.py:473
  11.4 9.8 %collective-permute-start.2 = (f32[128,256]{1,0:T(8,128)S(1)}, f32[128,256]{1,0:T(8,128)S(1)}, u32[]{:S(2)}, u32[]{:S(2)}) collective-permute-start(f32[128,256]{1,0:T(8,128)S(1)} %get-tuple-element.37), channel_id=1, source_target_pairs={{0,4},{4,0},{8,12},{12,8},{1,5},{5,1},{9,13},{13,9},{2,6},{6,2},{1... | collective-permute-start | bytes 393224 | tf_op jit(solution)/shard_map/ppermute | solution.py:473
  11.4 15.1 %collective-permute-start.3 = (f32[128,256]{1,0:T(8,128)S(1)}, f32[128,256]{1,0:T(8,128)S(1)}, u32[]{:S(2)}, u32[]{:S(2)}) collective-permute-start(f32[128,256]{1,0:T(8,128)S(1)} %get-tuple-element.38), channel_id=1, source_target_pairs={{0,8},{4,12},{8,0},{12,4},{1,9},{5,13},{9,1},{13,5},{2,10},{6,14},... | collective-permute-start | bytes 393224 | tf_op jit(solution)/shard_map/ppermute | solution.py:473
  12.0 2.8 %copy-start.2 = (s32[2,128]{1,0:T(2,128)S(1)}, s32[2,128]{1,0:T(2,128)}, u32[]{:S(2)}) copy-start(s32[2,128]{1,0:T(2,128)} %pattern_ref.3) | copy-start | bytes 3076
  12.0 2.8 %copy-start.4 = (s32[8]{0:T(128)S(1)}, s32[8]{0:T(128)}, u32[]{:S(2)}) copy-start(s32[8]{0:T(128)} %gamma_ref.3) | copy-start | bytes 100
  14.7 2.0 %collective-permute-start.4 = (f32[4,128,256]{2,1,0:T(8,128)S(1)}, f32[4,128,256]{2,1,0:T(8,128)S(1)}, u32[]{:S(2)}, u32[]{:S(2)}) collective-permute-start(f32[4,128,256]{2,1,0:T(8,128)S(1)} %get-tuple-element.43), channel_id=1, source_target_pairs={{0,1},{1,0},{2,3},{3,2},{4,5},{5,4},{6,7},{7,6},{8,9},{9,8},{10,11... | collective-permute-start | bytes 1572872 | tf_op jit(solution)/shard_map/ppermute | solution.py:473
  16.7 15.3 %collective-permute-start.5 = (f32[128,256]{1,0:T(8,128)S(1)}, f32[128,256]{1,0:T(8,128)S(1)}, u32[]{:S(2)}, u32[]{:S(2)}) collective-permute-start(f32[128,256]{1,0:T(8,128)S(1)} %get-tuple-element.44), channel_id=1, source_target_pairs={{0,8},{4,12},{8,0},{12,4},{1,9},{5,13},{9,1},{13,5},{2,10},{6,14},... | collective-permute-start | bytes 393224 | tf_op jit(solution)/shard_map/ppermute | solution.py:473
  19.1 13.0 %collective-permute-start.6 = (f32[128,256]{1,0:T(8,128)S(1)}, f32[128,256]{1,0:T(8,128)S(1)}, u32[]{:S(2)}, u32[]{:S(2)}) collective-permute-start(f32[128,256]{1,0:T(8,128)S(1)} %get-tuple-element.45), channel_id=1, source_target_pairs={{0,4},{4,0},{8,12},{12,8},{1,5},{5,1},{9,13},{13,9},{2,6},{6,2},{1... | collective-permute-start | bytes 393224 | tf_op jit(solution)/shard_map/ppermute | solution.py:473
  21.1 10.9 %collective-permute-start.7 = (f32[128,256]{1,0:T(8,128)S(1)}, f32[128,256]{1,0:T(8,128)S(1)}, u32[]{:S(2)}, u32[]{:S(2)}) collective-permute-start(f32[128,256]{1,0:T(8,128)S(1)} %get-tuple-element.46), channel_id=1, source_target_pairs={{0,12},{4,8},{8,4},{12,0},{1,13},{5,9},{9,5},{13,1},{2,14},{6,10},... | collective-permute-start | bytes 393224 | tf_op jit(solution)/shard_map/ppermute | solution.py:473
  26.5 5.6 %collective-permute-start.8 = (f32[128,256]{1,0:T(8,128)S(1)}, f32[128,256]{1,0:T(8,128)S(1)}, u32[]{:S(2)}, u32[]{:S(2)}) collective-permute-start(f32[128,256]{1,0:T(8,128)S(1)} %sum_chips.2.field_ref.refs_0_), channel_id=1, source_target_pairs={{0,2},{2,0},{1,3},{3,1},{4,6},{6,4},{5,7},{7,5},{8,10},{10,8},{9,1... | collective-permute-start | bytes 393224 | tf_op jit(solution)/shard_map/ppermute | solution.py:473
  32.2 6.2 %copy-start = (s32[2,2]{1,0:T(2,128)S(1)}, s32[2,2]{1,0:T(2,128)}, u32[]{:S(2)}) copy-start(s32[2,2]{1,0:T(2,128)} %pairs_ref.1) | copy-start | bytes 52
  32.3 1.6 %collective-permute-start.9 = (f32[4,2,2,16,128]{4,3,2,1,0:T(8,128)S(1)}, f32[4,2,2,16,128]{4,3,2,1,0:T(8,128)S(1)}, u32[]{:S(2)}, u32[]{:S(2)}) collective-permute-start(f32[4,2,2,16,128]{4,3,2,1,0:T(8,128)S(1)} %get-tuple-element.49), channel_id=1, source_target_pairs={{0,1},{1,0},{2,3},{3,2},{4,5},{5,4},{6,7},{7,6},{8,9},{9,8},{10,11... | collective-permute-start | bytes 393224 | tf_op jit(solution)/shard_map/ppermute | solution.py:473
  32.4 6.0 %collective-permute-start.13 = (f32[128,256]{1,0:T(8,128)S(1)}, f32[128,256]{1,0:T(8,128)S(1)}, u32[]{:S(2)}, u32[]{:S(2)}) collective-permute-start(f32[128,256]{1,0:T(8,128)S(1)} %sum_chips.3.field_ref.refs_1_), channel_id=1, source_target_pairs={{0,2},{2,0},{1,3},{3,1},{4,6},{6,4},{5,7},{7,5},{8,10},{10,8},{9,1... | collective-permute-start | bytes 393224 | tf_op jit(solution)/shard_map/ppermute | solution.py:473
  34.0 10.5 %collective-permute-start.10 = (f32[2,2,2,16,128]{4,3,2,1,0:T(8,128)S(1)}, f32[2,2,2,16,128]{4,3,2,1,0:T(8,128)S(1)}, u32[]{:S(2)}, u32[]{:S(2)}) collective-permute-start(f32[2,2,2,16,128]{4,3,2,1,0:T(8,128)S(1)} %get-tuple-element.51), channel_id=1, source_target_pairs={{0,12},{4,8},{8,4},{12,0},{1,13},{5,9},{9,5},{13,1},{2,14},{6,10},... | collective-permute-start | bytes 196616 | tf_op jit(solution)/shard_map/ppermute | solution.py:473
  36.5 9.5 %collective-permute-start.11 = (f32[2,2,2,16,128]{4,3,2,1,0:T(8,128)S(1)}, f32[2,2,2,16,128]{4,3,2,1,0:T(8,128)S(1)}, u32[]{:S(2)}, u32[]{:S(2)}) collective-permute-start(f32[2,2,2,16,128]{4,3,2,1,0:T(8,128)S(1)} %get-tuple-element.52), channel_id=1, source_target_pairs={{0,8},{4,12},{8,0},{12,4},{1,9},{5,13},{9,1},{13,5},{2,10},{6,14},... | collective-permute-start | bytes 196616 | tf_op jit(solution)/shard_map/ppermute | solution.py:473
  38.1 7.9 %collective-permute-start.12 = (f32[2,2,2,16,128]{4,3,2,1,0:T(8,128)S(1)}, f32[2,2,2,16,128]{4,3,2,1,0:T(8,128)S(1)}, u32[]{:S(2)}, u32[]{:S(2)}) collective-permute-start(f32[2,2,2,16,128]{4,3,2,1,0:T(8,128)S(1)} %get-tuple-element.53), channel_id=1, source_target_pairs={{0,4},{4,0},{8,12},{12,8},{1,5},{5,1},{9,13},{13,9},{2,6},{6,2},{1... | collective-permute-start | bytes 196616 | tf_op jit(solution)/shard_map/ppermute | solution.py:473
  39.5 1.4 %collective-permute-start.14 = (f32[4,2,2,16,128]{4,3,2,1,0:T(8,128)S(1)}, f32[4,2,2,16,128]{4,3,2,1,0:T(8,128)S(1)}, u32[]{:S(2)}, u32[]{:S(2)}) collective-permute-start(f32[4,2,2,16,128]{4,3,2,1,0:T(8,128)S(1)} %get-tuple-element.55), channel_id=1, source_target_pairs={{0,1},{1,0},{2,3},{3,2},{4,5},{5,4},{6,7},{7,6},{8,9},{9,8},{10,11... | collective-permute-start | bytes 393224 | tf_op jit(solution)/shard_map/ppermute | solution.py:473
  40.9 6.8 %collective-permute-start.15 = (f32[2,2,2,16,128]{4,3,2,1,0:T(8,128)S(1)}, f32[2,2,2,16,128]{4,3,2,1,0:T(8,128)S(1)}, u32[]{:S(2)}, u32[]{:S(2)}) collective-permute-start(f32[2,2,2,16,128]{4,3,2,1,0:T(8,128)S(1)} %get-tuple-element.59), channel_id=1, source_target_pairs={{0,8},{4,12},{8,0},{12,4},{1,9},{5,13},{9,1},{13,5},{2,10},{6,14},... | collective-permute-start | bytes 196616 | tf_op jit(solution)/shard_map/ppermute | solution.py:473
  44.4 4.3 %collective-permute-start.16 = (f32[2,2,2,16,128]{4,3,2,1,0:T(8,128)S(1)}, f32[2,2,2,16,128]{4,3,2,1,0:T(8,128)S(1)}, u32[]{:S(2)}, u32[]{:S(2)}) collective-permute-start(f32[2,2,2,16,128]{4,3,2,1,0:T(8,128)S(1)} %get-tuple-element.60), channel_id=1, source_target_pairs={{0,4},{4,0},{8,12},{12,8},{1,5},{5,1},{9,13},{13,9},{2,6},{6,2},{1... | collective-permute-start | bytes 196616 | tf_op jit(solution)/shard_map/ppermute | solution.py:473
  44.4 6.4 %collective-permute-start.17 = (f32[2,2,2,16,128]{4,3,2,1,0:T(8,128)S(1)}, f32[2,2,2,16,128]{4,3,2,1,0:T(8,128)S(1)}, u32[]{:S(2)}, u32[]{:S(2)}) collective-permute-start(f32[2,2,2,16,128]{4,3,2,1,0:T(8,128)S(1)} %get-tuple-element.61), channel_id=1, source_target_pairs={{0,12},{4,8},{8,4},{12,0},{1,13},{5,9},{9,5},{13,1},{2,14},{6,10},... | collective-permute-start | bytes 196616 | tf_op jit(solution)/shard_map/ppermute | solution.py:473

commit v8 on v7

--- a/solution.py
+++ b/solution.py
@@ -15,7 +15,7 @@
 BF16 = jnp.bfloat16
 VMEM_LIMIT = 16 * 2**20
 SMALL_LIMIT = 4 * 2**20
-ROUND = ((3, 1, 2), (2, 1, 3))
+ROUND = ((3, 1, 2), (1, 2, 3))
 LARGE = 10**11
 
 

time: 51.7 us -> 51.7 us (level)
  transfers between devices with their start and end apart: 18 -> 18, of which waited for: 7 -> 8; matrix products, arithmetic and copies ran while one was open for 0% -> 0% of each run, Pallas kernels for 15% -> 15%
where the time goes in v8:
time: 51.7 us; the launch traced here: 51.5 us
  starting transfers between devices  23.5 us (45%)
  waiting for transfers between devices  14.8 us (29%)
  Pallas kernels  12.4 us (24%)
  between operations  0.83 us (2%)
    ppermute x18, starting transfers between devices, swap(): return lax.ppermute(value, axis, [(i, i ^ distance) for i in range(size)])  23.5 us
    ppermute x18, waiting for transfers between devices, swap(): return lax.ppermute(value, axis, [(i, i ^ distance) for i in range(size)])  14.8 us
    pallas_call x2, Pallas kernels, first_blocks(): pl.pallas_call(functools.partial(first_kernel, order, time, slots, chunks...  6.24 us
    pallas_call x2, Pallas kernels, later_blocks(): pl.pallas_call(functools.partial(later_kernel, order, time, slots), in_sp...  3.16 us
    pallas_call x2, Pallas kernels, put_blocks(): pl.pallas_call(kernel, in_specs=[pl.BlockSpec(memory_space=pltpu.HBM)] *...  1.52 us
  transfers between devices with their start and end apart: 18, of which 8 were waited for; matrix products, arithmetic and copies ran while one was open for 0% of the time, Pallas kernels for 15%

profile of v8, /device:TPU:0, one launch (start us, length us, event | category | flops | bytes accessed | tf_op | source)
XLA Modules:
  0.0 51.5 jit_solution(16576103063722523369)
XLA Ops:
  0.7 3.6 %first_blocks.2 = (f32[4,128,256]{2,1,0:T(8,128)S(1)}, bf16[256,3072]{1,0:T(8,128)(2,1)S(1)}, bf16[2,12,2,128,128]{4,3,2,1,0:T(8,128)(2,1)S(1)}, bf16[3072,128]{1,0:T(8,128)(2,1)S(1)}, bf16[3072,128]{1,0:T(8,128)(2,1)S(1)}) custom-call(bf16[2,3072,128]{2,1,0:T(8,128)(2,1)} %bitcast.7, bf16[2,3072,128]{2,1,0:T(8,128)(2,1)} %bitcast.8, s32[8]{0:T(128)} %gamma_ref.3, ...), custom_call_target="tpu_custom_call" | custom-call | flops 20132659200 | bytes 3145728 | tf_op jit(solution)/shard_map/first_blocks/pallas_call | solution.py:238
  4.2 0.5 %collective-permute-start = (f32[4,128,256]{2,1,0:T(8,128)S(1)}, f32[4,128,256]{2,1,0:T(8,128)S(1)}, u32[]{:S(2)}, u32[]{:S(2)}) collective-permute-start(f32[4,128,256]{2,1,0:T(8,128)S(1)} %get-tuple-element.34), channel_id=1, source_target_pairs={{0,1},{1,0},{2,3},{3,2},{4,5},{5,4},{6,7},{7,6},{8,9},{9,8},{10,11... | collective-permute-start | bytes 1572872 | tf_op jit(solution)/shard_map/ppermute | solution.py:473
  4.8 1.6 %later_blocks.2.keep_ref = f32[4,128,256]{2,1,0:T(8,128)S(1)} custom-call(s32[8]{0:T(128)S(1)} %copy-done.3, s32[2,128]{1,0:T(2,128)S(1)} %copy-done.1, bf16[256,3072]{1,0:T(8,128)(2,1)S(1)} %get-tuple-element.32.sink_mat, bf16[2,12,2,128,128]{4,3,2,1,0:T(8,128)(2,1)S(1)} %get-tuple-element.33.turned), custom_call_target="tpu_custom_call" | custom-call | flops 20132659200 | bytes 3145728 | tf_op jit(solution)/shard_map/later_blocks/pallas_call | solution.py:278
  6.4 5.0 %collective-permute-start.1 = (f32[128,256]{1,0:T(8,128)S(1)}, f32[128,256]{1,0:T(8,128)S(1)}, u32[]{:S(2)}, u32[]{:S(2)}) collective-permute-start(f32[128,256]{1,0:T(8,128)S(1)} %get-tuple-element.36), channel_id=1, source_target_pairs={{0,12},{4,8},{8,4},{12,0},{1,13},{5,9},{9,5},{13,1},{2,14},{6,10},... | collective-permute-start | bytes 393224 | tf_op jit(solution)/shard_map/ppermute | solution.py:473
  11.4 0.6 %collective-permute-start.3 = (f32[128,256]{1,0:T(8,128)S(1)}, f32[128,256]{1,0:T(8,128)S(1)}, u32[]{:S(2)}, u32[]{:S(2)}) collective-permute-start(f32[128,256]{1,0:T(8,128)S(1)} %get-tuple-element.38), channel_id=1, source_target_pairs={{0,8},{4,12},{8,0},{12,4},{1,9},{5,13},{9,1},{13,5},{2,10},{6,14},... | collective-permute-start | bytes 393224 | tf_op jit(solution)/shard_map/ppermute | solution.py:473
  12.0 2.7 %first_blocks.3 = (f32[4,128,256]{2,1,0:T(8,128)S(1)}, bf16[256,3072]{1,0:T(8,128)(2,1)S(1)}, bf16[2,12,2,128,128]{4,3,2,1,0:T(8,128)(2,1)S(1)}) custom-call(bf16[3072,128]{1,0:T(8,128)(2,1)S(1)} %get-tuple-element.39.refs_0_, bf16[3072,128]{1,0:T(8,128)(2,1)S(1)} %get-tuple-element.40.refs_1_, s32[8]{0:T(128)} %gamma_ref.3, s32[3,8]{1,0:T(4,128)} %bitcast.10, ...), custom_call_target="tpu_custom_call" | custom-call | flops 20132659200 | bytes 3145728 | tf_op jit(solution)/shard_map/first_blocks/pallas_call | solution.py:238
  14.8 1.6 %later_blocks.3.keep_ref = f32[4,128,256]{2,1,0:T(8,128)S(1)} custom-call(s32[8]{0:T(128)S(1)} %copy-done.4, s32[2,128]{1,0:T(2,128)S(1)} %copy-done.2, bf16[256,3072]{1,0:T(8,128)(2,1)S(1)} %get-tuple-element.41.sink_mat, bf16[2,12,2,128,128]{4,3,2,1,0:T(8,128)(2,1)S(1)} %get-tuple-element.42.turned), custom_call_target="tpu_custom_call" | custom-call | flops 20132659200 | bytes 3145728 | tf_op jit(solution)/shard_map/later_blocks/pallas_call | solution.py:278
  16.4 0.3 collective-permute-done.4.got_ref
  16.7 1.4 %collective-permute-start.5 = (f32[128,256]{1,0:T(8,128)S(1)}, f32[128,256]{1,0:T(8,128)S(1)}, u32[]{:S(2)}, u32[]{:S(2)}) collective-permute-start(f32[128,256]{1,0:T(8,128)S(1)} %get-tuple-element.44), channel_id=1, source_target_pairs={{0,4},{4,0},{8,12},{12,8},{1,5},{5,1},{9,13},{13,9},{2,6},{6,2},{1... | collective-permute-start | bytes 393224 | tf_op jit(solution)/shard_map/ppermute | solution.py:473
  18.2 2.9 %collective-permute-start.6 = (f32[128,256]{1,0:T(8,128)S(1)}, f32[128,256]{1,0:T(8,128)S(1)}, u32[]{:S(2)}, u32[]{:S(2)}) collective-permute-start(f32[128,256]{1,0:T(8,128)S(1)} %get-tuple-element.45), channel_id=1, source_target_pairs={{0,8},{4,12},{8,0},{12,4},{1,9},{5,13},{9,1},{13,5},{2,10},{6,14},... | collective-permute-start | bytes 393224 | tf_op jit(solution)/shard_map/ppermute | solution.py:473
  21.1 0.1 collective-permute-start.7
  21.2 2.5 %collective-permute-done.3.refs_3_ = f32[128,256]{1,0:T(8,128)S(1)} collective-permute-done((f32[128,256]{1,0:T(8,128)S(1)}, f32[128,256]{1,0:T(8,128)S(1)}, u32[]{:S(2)}, u32[]{:S(2)}) %collective-permute-start.3) | collective-permute-done | bytes 131104 | tf_op jit(solution)/shard_map/ppermute | solution.py:473
  23.7 1.6 %collective-permute-start.8 = (f32[128,256]{1,0:T(8,128)S(1)}, f32[128,256]{1,0:T(8,128)S(1)}, u32[]{:S(2)}, u32[]{:S(2)}) collective-permute-start(f32[128,256]{1,0:T(8,128)S(1)} %sum_chips.2.field_ref.refs_0_), channel_id=1, source_target_pairs={{0,2},{2,0},{1,3},{3,1},{4,6},{6,4},{5,7},{7,5},{8,10},{10,8},{9,1... | collective-permute-start | bytes 393224 | tf_op jit(solution)/shard_map/ppermute | solution.py:473
  25.3 0.6 %collective-permute-done.5.refs_0_.refs_1_ = f32[128,256]{1,0:T(8,128)S(1)} collective-permute-done((f32[128,256]{1,0:T(8,128)S(1)}, f32[128,256]{1,0:T(8,128)S(1)}, u32[]{:S(2)}, u32[]{:S(2)}) %collective-permute-start.5) | collective-permute-done | bytes 131104 | tf_op jit(solution)/shard_map/ppermute | solution.py:473
  25.9 6.1 %collective-permute-done.6.refs_1_.refs_2_ = f32[128,256]{1,0:T(8,128)S(1)} collective-permute-done((f32[128,256]{1,0:T(8,128)S(1)}, f32[128,256]{1,0:T(8,128)S(1)}, u32[]{:S(2)}, u32[]{:S(2)}) %collective-permute-start.6) | collective-permute-done | bytes 131104 | tf_op jit(solution)/shard_map/ppermute | solution.py:473
  32.0 0.1 turn_field.1.refs_5_.whole_ref
  32.2 0.1 split_rows.1
  32.3 0.1 collective-permute-start.9
  32.4 1.6 %collective-permute-start.13 = (f32[128,256]{1,0:T(8,128)S(1)}, f32[128,256]{1,0:T(8,128)S(1)}, u32[]{:S(2)}, u32[]{:S(2)}) collective-permute-start(f32[128,256]{1,0:T(8,128)S(1)} %sum_chips.3.field_ref.refs_1_), channel_id=1, source_target_pairs={{0,2},{2,0},{1,3},{3,1},{4,6},{6,4},{5,7},{7,5},{8,10},{10,8},{9,1... | collective-permute-start | bytes 393224 | tf_op jit(solution)/shard_map/ppermute | solution.py:473
  34.0 2.3 %collective-permute-start.10 = (f32[2,2,2,16,128]{4,3,2,1,0:T(8,128)S(1)}, f32[2,2,2,16,128]{4,3,2,1,0:T(8,128)S(1)}, u32[]{:S(2)}, u32[]{:S(2)}) collective-permute-start(f32[2,2,2,16,128]{4,3,2,1,0:T(8,128)S(1)} %get-tuple-element.51), channel_id=1, source_target_pairs={{0,12},{4,8},{8,4},{12,0},{1,13},{5,9},{9,5},{13,1},{2,14},{6,10},... | collective-permute-start | bytes 196616 | tf_op jit(solution)/shard_map/ppermute | solution.py:473
  36.2 1.9 %collective-permute-start.11 = (f32[2,2,2,16,128]{4,3,2,1,0:T(8,128)S(1)}, f32[2,2,2,16,128]{4,3,2,1,0:T(8,128)S(1)}, u32[]{:S(2)}, u32[]{:S(2)}) collective-permute-start(f32[2,2,2,16,128]{4,3,2,1,0:T(8,128)S(1)} %get-tuple-element.52), channel_id=1, source_target_pairs={{0,8},{4,12},{8,0},{12,4},{1,9},{5,13},{9,1},{13,5},{2,10},{6,14},... | collective-permute-start | bytes 196616 | tf_op jit(solution)/shard_map/ppermute | solution.py:473
  38.1 0.3 collective-permute-start.12
  38.4 1.0 %products.1 = (f32[4,2,2,16,128]{4,3,2,1,0:T(8,128)S(1)}, f32[2,2,128,128]{3,2,1,0:T(8,128)S(1)}) custom-call(s32[2,2]{1,0:T(2,128)S(1)} %copy-done, f32[128,256]{1,0:T(8,128)S(1)} %sum_chips.2.field_ref.refs_0_, f32[128,256]{1,0:T(8,128)S(1)} %sum_chips.3.field_ref.refs_1_, f32[128,256]{1,0:T(8,128)S(1)} %collective-permute-done.8.refs_4_.refs_2_, ...), custom_call_target="tpu_custom_call" | custom-call | flops 33554432 | bytes 1048576 | tf_op jit(solution)/shard_map/products/pallas_call | solution.py:395
  39.5 0.1 collective-permute-start.14
  39.6 1.3 %collective-permute-done.14.got_ref = f32[4,2,2,16,128]{4,3,2,1,0:T(8,128)S(1)} collective-permute-done((f32[4,2,2,16,128]{4,3,2,1,0:T(8,128)S(1)}, f32[4,2,2,16,128]{4,3,2,1,0:T(8,128)S(1)}, u32[]{:S(2)}, u32[]{:S(2)}) %collective-permute-start.14) | collective-permute-done | bytes 131104 | tf_op jit(solution)/shard_map/ppermute | solution.py:473
  40.9 3.6 %collective-permute-start.15 = (f32[2,2,2,16,128]{4,3,2,1,0:T(8,128)S(1)}, f32[2,2,2,16,128]{4,3,2,1,0:T(8,128)S(1)}, u32[]{:S(2)}, u32[]{:S(2)}) collective-permute-start(f32[2,2,2,16,128]{4,3,2,1,0:T(8,128)S(1)} %get-tuple-element.59), channel_id=1, source_target_pairs={{0,8},{4,12},{8,0},{12,4},{1,9},{5,13},{9,1},{13,5},{2,10},{6,14},... | collective-permute-start | bytes 196616 | tf_op jit(solution)/shard_map/ppermute | solution.py:473
  44.5 1.5 %collective-permute-start.17 = (f32[2,2,2,16,128]{4,3,2,1,0:T(8,128)S(1)}, f32[2,2,2,16,128]{4,3,2,1,0:T(8,128)S(1)}, u32[]{:S(2)}, u32[]{:S(2)}) collective-permute-start(f32[2,2,2,16,128]{4,3,2,1,0:T(8,128)S(1)} %get-tuple-element.61), channel_id=1, source_target_pairs={{0,12},{4,8},{8,4},{12,0},{1,13},{5,9},{9,5},{13,1},{2,14},{6,10},... | collective-permute-start | bytes 196616 | tf_op jit(solution)/shard_map/ppermute | solution.py:473
  46.0 0.8 %put_early.1 = (f32[2,8,2,16,128]{4,3,2,1,0:T(8,128)}, f32[2,8,2,16,128]{4,3,2,1,0:T(8,128)}) custom-call(f32[2,2,2,16,128]{4,3,2,1,0:T(8,128)S(1)} %get-tuple-element.50.refs_0_, f32[2,2,2,16,128]{4,3,2,1,0:T(8,128)S(1)} %collective-permute-done.10.refs_1_, f32[2,2,2,16,128]{4,3,2,1,0:T(8,128)S(1)} %collective-permute-done.11.refs_2_, ...), custom_call_target="tpu_custom_call" | custom-call | flops 99999997952 | bytes 1 | tf_op jit(solution)/shard_map/put_early/pallas_call | solution.py:457
  46.8 1.0 %collective-permute-done.15.refs_1_ = f32[2,2,2,16,128]{4,3,2,1,0:T(8,128)S(1)} collective-permute-done((f32[2,2,2,16,128]{4,3,2,1,0:T(8,128)S(1)}, f32[2,2,2,16,128]{4,3,2,1,0:T(8,128)S(1)}, u32[]{:S(2)}, u32[]{:S(2)}) %collective-permute-start.15) | collective-permute-done | bytes 65568 | tf_op jit(solution)/shard_map/ppermute | solution.py:473
  47.8 0.9 %collective-permute-done.16.refs_2_ = f32[2,2,2,16,128]{4,3,2,1,0:T(8,128)S(1)} collective-permute-done((f32[2,2,2,16,128]{4,3,2,1,0:T(8,128)S(1)}, f32[2,2,2,16,128]{4,3,2,1,0:T(8,128)S(1)}, u32[]{:S(2)}, u32[]{:S(2)}) %collective-permute-start.16) | collective-permute-done | bytes 65568 | tf_op jit(solution)/shard_map/ppermute | solution.py:473
  48.8 2.1 %collective-permute-done.17.refs_3_ = f32[2,2,2,16,128]{4,3,2,1,0:T(8,128)S(1)} collective-permute-done((f32[2,2,2,16,128]{4,3,2,1,0:T(8,128)S(1)}, f32[2,2,2,16,128]{4,3,2,1,0:T(8,128)S(1)}, u32[]{:S(2)}, u32[]{:S(2)}) %collective-permute-start.17) | collective-permute-done | bytes 65568 | tf_op jit(solution)/shard_map/ppermute | solution.py:473
  50.8 0.7 %put_late.1 = f32[2,8,2,16,128]{4,3,2,1,0:T(8,128)} custom-call(f32[2,8,2,16,128]{4,3,2,1,0:T(8,128)} %get-tuple-element.58.refs_0_, f32[2,2,2,16,128]{4,3,2,1,0:T(8,128)S(1)} %collective-permute-done.15.refs_1_, f32[2,2,2,16,128]{4,3,2,1,0:T(8,128)S(1)} %collective-permute-done.16.refs_2_, ...), custom_call_target="tpu_custom_call", output_to_operand_aliasing={{}: (0, {})} | custom-call | flops 1 | bytes 1 | tf_op jit(solution)/shard_map/put_late/pallas_call | solution.py:457
  (30 shorter events, 0.4 us)
Async XLA Ops:
  0.6 4.1 %copy-start.1 = (s32[2,128]{1,0:T(2,128)S(1)}, s32[2,128]{1,0:T(2,128)}, u32[]{:S(2)}) copy-start(s32[2,128]{1,0:T(2,128)} %pattern_ref.3) | copy-start | bytes 3076
  0.6 4.1 %copy-start.3 = (s32[8]{0:T(128)S(1)}, s32[8]{0:T(128)}, u32[]{:S(2)}) copy-start(s32[8]{0:T(128)} %gamma_ref.3) | copy-start | bytes 100
  4.2 2.1 %collective-permute-start = (f32[4,128,256]{2,1,0:T(8,128)S(1)}, f32[4,128,256]{2,1,0:T(8,128)S(1)}, u32[]{:S(2)}, u32[]{:S(2)}) collective-permute-start(f32[4,128,256]{2,1,0:T(8,128)S(1)} %get-tuple-element.34), channel_id=1, source_target_pairs={{0,1},{1,0},{2,3},{3,2},{4,5},{5,4},{6,7},{7,6},{8,9},{9,8},{10,11... | collective-permute-start | bytes 1572872 | tf_op jit(solution)/shard_map/ppermute | solution.py:473
  6.4 14.7 %collective-permute-start.1 = (f32[128,256]{1,0:T(8,128)S(1)}, f32[128,256]{1,0:T(8,128)S(1)}, u32[]{:S(2)}, u32[]{:S(2)}) collective-permute-start(f32[128,256]{1,0:T(8,128)S(1)} %get-tuple-element.36), channel_id=1, source_target_pairs={{0,12},{4,8},{8,4},{12,0},{1,13},{5,9},{9,5},{13,1},{2,14},{6,10},... | collective-permute-start | bytes 393224 | tf_op jit(solution)/shard_map/ppermute | solution.py:473
  11.4 9.8 %collective-permute-start.2 = (f32[128,256]{1,0:T(8,128)S(1)}, f32[128,256]{1,0:T(8,128)S(1)}, u32[]{:S(2)}, u32[]{:S(2)}) collective-permute-start(f32[128,256]{1,0:T(8,128)S(1)} %get-tuple-element.37), channel_id=1, source_target_pairs={{0,4},{4,0},{8,12},{12,8},{1,5},{5,1},{9,13},{13,9},{2,6},{6,2},{1... | collective-permute-start | bytes 393224 | tf_op jit(solution)/shard_map/ppermute | solution.py:473
  11.4 12.3 %collective-permute-start.3 = (f32[128,256]{1,0:T(8,128)S(1)}, f32[128,256]{1,0:T(8,128)S(1)}, u32[]{:S(2)}, u32[]{:S(2)}) collective-permute-start(f32[128,256]{1,0:T(8,128)S(1)} %get-tuple-element.38), channel_id=1, source_target_pairs={{0,8},{4,12},{8,0},{12,4},{1,9},{5,13},{9,1},{13,5},{2,10},{6,14},... | collective-permute-start | bytes 393224 | tf_op jit(solution)/shard_map/ppermute | solution.py:473
  12.0 2.8 %copy-start.2 = (s32[2,128]{1,0:T(2,128)S(1)}, s32[2,128]{1,0:T(2,128)}, u32[]{:S(2)}) copy-start(s32[2,128]{1,0:T(2,128)} %pattern_ref.3) | copy-start | bytes 3076
  12.0 2.8 %copy-start.4 = (s32[8]{0:T(128)S(1)}, s32[8]{0:T(128)}, u32[]{:S(2)}) copy-start(s32[8]{0:T(128)} %gamma_ref.3) | copy-start | bytes 100
  14.7 2.0 %collective-permute-start.4 = (f32[4,128,256]{2,1,0:T(8,128)S(1)}, f32[4,128,256]{2,1,0:T(8,128)S(1)}, u32[]{:S(2)}, u32[]{:S(2)}) collective-permute-start(f32[4,128,256]{2,1,0:T(8,128)S(1)} %get-tuple-element.43), channel_id=1, source_target_pairs={{0,1},{1,0},{2,3},{3,2},{4,5},{5,4},{6,7},{7,6},{8,9},{9,8},{10,11... | collective-permute-start | bytes 1572872 | tf_op jit(solution)/shard_map/ppermute | solution.py:473
  16.7 9.2 %collective-permute-start.5 = (f32[128,256]{1,0:T(8,128)S(1)}, f32[128,256]{1,0:T(8,128)S(1)}, u32[]{:S(2)}, u32[]{:S(2)}) collective-permute-start(f32[128,256]{1,0:T(8,128)S(1)} %get-tuple-element.44), channel_id=1, source_target_pairs={{0,4},{4,0},{8,12},{12,8},{1,5},{5,1},{9,13},{13,9},{2,6},{6,2},{1... | collective-permute-start | bytes 393224 | tf_op jit(solution)/shard_map/ppermute | solution.py:473
  18.2 13.8 %collective-permute-start.6 = (f32[128,256]{1,0:T(8,128)S(1)}, f32[128,256]{1,0:T(8,128)S(1)}, u32[]{:S(2)}, u32[]{:S(2)}) collective-permute-start(f32[128,256]{1,0:T(8,128)S(1)} %get-tuple-element.45), channel_id=1, source_target_pairs={{0,8},{4,12},{8,0},{12,4},{1,9},{5,13},{9,1},{13,5},{2,10},{6,14},... | collective-permute-start | bytes 393224 | tf_op jit(solution)/shard_map/ppermute | solution.py:473
  21.1 10.9 %collective-permute-start.7 = (f32[128,256]{1,0:T(8,128)S(1)}, f32[128,256]{1,0:T(8,128)S(1)}, u32[]{:S(2)}, u32[]{:S(2)}) collective-permute-start(f32[128,256]{1,0:T(8,128)S(1)} %get-tuple-element.46), channel_id=1, source_target_pairs={{0,12},{4,8},{8,4},{12,0},{1,13},{5,9},{9,5},{13,1},{2,14},{6,10},... | collective-permute-start | bytes 393224 | tf_op jit(solution)/shard_map/ppermute | solution.py:473
  23.7 8.4 %collective-permute-start.8 = (f32[128,256]{1,0:T(8,128)S(1)}, f32[128,256]{1,0:T(8,128)S(1)}, u32[]{:S(2)}, u32[]{:S(2)}) collective-permute-start(f32[128,256]{1,0:T(8,128)S(1)} %sum_chips.2.field_ref.refs_0_), channel_id=1, source_target_pairs={{0,2},{2,0},{1,3},{3,1},{4,6},{6,4},{5,7},{7,5},{8,10},{10,8},{9,1... | collective-permute-start | bytes 393224 | tf_op jit(solution)/shard_map/ppermute | solution.py:473
  32.2 6.3 %copy-start = (s32[2,2]{1,0:T(2,128)S(1)}, s32[2,2]{1,0:T(2,128)}, u32[]{:S(2)}) copy-start(s32[2,2]{1,0:T(2,128)} %pairs_ref.1) | copy-start | bytes 52
  32.3 1.6 %collective-permute-start.9 = (f32[4,2,2,16,128]{4,3,2,1,0:T(8,128)S(1)}, f32[4,2,2,16,128]{4,3,2,1,0:T(8,128)S(1)}, u32[]{:S(2)}, u32[]{:S(2)}) collective-permute-start(f32[4,2,2,16,128]{4,3,2,1,0:T(8,128)S(1)} %get-tuple-element.49), channel_id=1, source_target_pairs={{0,1},{1,0},{2,3},{3,2},{4,5},{5,4},{6,7},{7,6},{8,9},{9,8},{10,11... | collective-permute-start | bytes 393224 | tf_op jit(solution)/shard_map/ppermute | solution.py:473
  32.4 6.0 %collective-permute-start.13 = (f32[128,256]{1,0:T(8,128)S(1)}, f32[128,256]{1,0:T(8,128)S(1)}, u32[]{:S(2)}, u32[]{:S(2)}) collective-permute-start(f32[128,256]{1,0:T(8,128)S(1)} %sum_chips.3.field_ref.refs_1_), channel_id=1, source_target_pairs={{0,2},{2,0},{1,3},{3,1},{4,6},{6,4},{5,7},{7,5},{8,10},{10,8},{9,1... | collective-permute-start | bytes 393224 | tf_op jit(solution)/shard_map/ppermute | solution.py:473
  34.0 10.5 %collective-permute-start.10 = (f32[2,2,2,16,128]{4,3,2,1,0:T(8,128)S(1)}, f32[2,2,2,16,128]{4,3,2,1,0:T(8,128)S(1)}, u32[]{:S(2)}, u32[]{:S(2)}) collective-permute-start(f32[2,2,2,16,128]{4,3,2,1,0:T(8,128)S(1)} %get-tuple-element.51), channel_id=1, source_target_pairs={{0,12},{4,8},{8,4},{12,0},{1,13},{5,9},{9,5},{13,1},{2,14},{6,10},... | collective-permute-start | bytes 196616 | tf_op jit(solution)/shard_map/ppermute | solution.py:473
  36.2 9.8 %collective-permute-start.11 = (f32[2,2,2,16,128]{4,3,2,1,0:T(8,128)S(1)}, f32[2,2,2,16,128]{4,3,2,1,0:T(8,128)S(1)}, u32[]{:S(2)}, u32[]{:S(2)}) collective-permute-start(f32[2,2,2,16,128]{4,3,2,1,0:T(8,128)S(1)} %get-tuple-element.52), channel_id=1, source_target_pairs={{0,8},{4,12},{8,0},{12,4},{1,9},{5,13},{9,1},{13,5},{2,10},{6,14},... | collective-permute-start | bytes 196616 | tf_op jit(solution)/shard_map/ppermute | solution.py:473
  38.1 7.9 %collective-permute-start.12 = (f32[2,2,2,16,128]{4,3,2,1,0:T(8,128)S(1)}, f32[2,2,2,16,128]{4,3,2,1,0:T(8,128)S(1)}, u32[]{:S(2)}, u32[]{:S(2)}) collective-permute-start(f32[2,2,2,16,128]{4,3,2,1,0:T(8,128)S(1)} %get-tuple-element.53), channel_id=1, source_target_pairs={{0,4},{4,0},{8,12},{12,8},{1,5},{5,1},{9,13},{13,9},{2,6},{6,2},{1... | collective-permute-start | bytes 196616 | tf_op jit(solution)/shard_map/ppermute | solution.py:473
  39.5 1.4 %collective-permute-start.14 = (f32[4,2,2,16,128]{4,3,2,1,0:T(8,128)S(1)}, f32[4,2,2,16,128]{4,3,2,1,0:T(8,128)S(1)}, u32[]{:S(2)}, u32[]{:S(2)}) collective-permute-start(f32[4,2,2,16,128]{4,3,2,1,0:T(8,128)S(1)} %get-tuple-element.55), channel_id=1, source_target_pairs={{0,1},{1,0},{2,3},{3,2},{4,5},{5,4},{6,7},{7,6},{8,9},{9,8},{10,11... | collective-permute-start | bytes 393224 | tf_op jit(solution)/shard_map/ppermute | solution.py:473
  40.9 6.9 %collective-permute-start.15 = (f32[2,2,2,16,128]{4,3,2,1,0:T(8,128)S(1)}, f32[2,2,2,16,128]{4,3,2,1,0:T(8,128)S(1)}, u32[]{:S(2)}, u32[]{:S(2)}) collective-permute-start(f32[2,2,2,16,128]{4,3,2,1,0:T(8,128)S(1)} %get-tuple-element.59), channel_id=1, source_target_pairs={{0,8},{4,12},{8,0},{12,4},{1,9},{5,13},{9,1},{13,5},{2,10},{6,14},... | collective-permute-start | bytes 196616 | tf_op jit(solution)/shard_map/ppermute | solution.py:473
  44.5 4.3 %collective-permute-start.16 = (f32[2,2,2,16,128]{4,3,2,1,0:T(8,128)S(1)}, f32[2,2,2,16,128]{4,3,2,1,0:T(8,128)S(1)}, u32[]{:S(2)}, u32[]{:S(2)}) collective-permute-start(f32[2,2,2,16,128]{4,3,2,1,0:T(8,128)S(1)} %get-tuple-element.60), channel_id=1, source_target_pairs={{0,4},{4,0},{8,12},{12,8},{1,5},{5,1},{9,13},{13,9},{2,6},{6,2},{1... | collective-permute-start | bytes 196616 | tf_op jit(solution)/shard_map/ppermute | solution.py:473
  44.5 6.3 %collective-permute-start.17 = (f32[2,2,2,16,128]{4,3,2,1,0:T(8,128)S(1)}, f32[2,2,2,16,128]{4,3,2,1,0:T(8,128)S(1)}, u32[]{:S(2)}, u32[]{:S(2)}) collective-permute-start(f32[2,2,2,16,128]{4,3,2,1,0:T(8,128)S(1)} %get-tuple-element.61), channel_id=1, source_target_pairs={{0,12},{4,8},{8,4},{12,0},{1,13},{5,9},{9,5},{13,1},{2,14},{6,10},... | collective-permute-start | bytes 196616 | tf_op jit(solution)/shard_map/ppermute | solution.py:473
